TPU v7x, 32 devices: a whole 2x2x4 slice. The times are simulated.
32 devices in a mesh: src: 16 (over z, y, core), tgt: 2 (over x).
Axes of the slice: x: 2, y: 2, z: 4, core: 2. Of those that a mesh axis runs over, the one named last changes fastest.
Arguments:
- edge_states: bfloat16 [16, 2, 512, 1024], P('src', 'tgt'), may hold values from -6 to 6
- triplet_coeff: bfloat16 [16, 2, 16, 128, 128], P('src', 'tgt'), may hold values from -0.3984375 to 0.3984375
- block_target: int32 [16, 2, 16], P('src', 'tgt'), may hold values from 0 to 3
- block_source: int32 [16, 2, 16], P('src', 'tgt'), may hold values from 0 to 63
- block_count: int32 [16, 2], P('src', 'tgt'), may hold values from 2 to 16, as said below
- reverse_slot: int32 [16, 2, 512], P('src', 'tgt'), may hold values from 0 to 511, as said below
- w_proj: bfloat16 [2, 1024, 64], replicated, may hold values from -0.1875 to 0.1875
- w_up: bfloat16 [2, 64, 1024], replicated, may hold values from -0.75 to 0.75
- w_in: bfloat16 [2, 1024, 1024], replicated, may hold values from -0.1875 to 0.1875
- w_out: bfloat16 [2, 1024, 1024], replicated, may hold values from -0.1875 to 0.1875
- norm_gain: float32 [2, 1024], replicated, may hold values from 0.5 to 2
Outputs:
- edge_final: bfloat16 [16, 2, 512, 1024], P('src', 'tgt')
Inputs may be any that keep to these rules, and one draw needn't show every extreme that they name: `block_count`: each tile uses between 2 and 16 blocks; some tile uses all 16 in every draw. Reverse edges pair up: with C = 8, for tile (p, q) with p = a * C + r and its mirror tile (q * C + r, a), the two reverse_slot rows are inverse permutations of 0 to 511; on a tile with a = q the row is a permutation that is its own inverse without fixed points.
All inputs are finite; a program needn't handle non-finite values.
Results may differ from a plain program's by a relative error of at most 0.014.
Values may be sent and summed in bfloat16 or wider, within the bound.
No kernel may reach another device: no remote copies, remote signals or barrier semaphores. Data moves between devices by JAX's collectives and lax.ppermute only.
A program may use at most 64 MiB of HBM per device.

v0:
```python
import jax
import jax.numpy as jnp
from jax import lax
from jax.sharding import PartitionSpec as P

BLK = 128
LAYERS = 2


def partner(value, axis, bit):
    return lax.ppermute(value, axis, [(i, i ^ 1 << bit) for i in range(lax.axis_size(axis))])


def bit_pairings():
    groups = lax.axis_size("tgt")
    width = groups.bit_length() - 1
    src_bits = lax.axis_size("src").bit_length() - 1
    position = lax.axis_index("src") * groups + lax.axis_index("tgt")
    pairings = []
    for bit_index in range(width):
        upper = bit_index + src_bits
        differ = position // 2**bit_index % 2 != position // 2**upper % 2
        pairings.append(((bit_index, upper), differ))
    return pairings


def mirror_inputs(values, pairings):
    carried = values
    for bit_pair, differ in pairings:
        hopped = carried
        for bit_index in bit_pair:
            hopped = partner(hopped, ("src", "tgt"), bit_index)
        carried = jnp.where(differ, hopped, carried)
    return carried


def mirror_mixed(values, pairings):
    carried = values
    for bit_pair, differ in pairings:
        hopped = carried
        for bit_index in bit_pair:
            hopped = partner(hopped, ("src", "tgt"), bit_index)
        carried = jnp.where(differ, hopped, carried)
    return carried


def triplet_sums(pooled, coeffs, targets, sources, live_count, edge_count):
    width = pooled.shape[0]
    slots = coeffs.shape[0]
    out_blocks = edge_count // BLK
    blocks = pooled.reshape(width, pooled.shape[1] // BLK, BLK)
    picked = jnp.take(blocks, sources, axis=1)
    products = jnp.einsum("cbj,bji->cbi", picked, coeffs, preferred_element_type=jnp.float32)
    live_mask = (jnp.arange(slots) < live_count).astype(jnp.float32)
    placing = (targets[:, None] == jnp.arange(out_blocks)[None, :]).astype(jnp.float32) * live_mask[
        :, None
    ]
    return jnp.einsum("cbi,bo->coi", products, placing).reshape(width, edge_count)


def transform(rows, agg_low, w_up_l, w_in_l, w_out_l, gain_l):
    summed = rows.astype(jnp.float32) + jnp.einsum(
        "ce,cd->ed", agg_low, w_up_l, preferred_element_type=jnp.float32
    )
    scale_inv = lax.rsqrt(jnp.mean(summed * summed, axis=-1, keepdims=True) + 1e-06)
    normed = (gain_l * summed * scale_inv).astype(jnp.bfloat16)
    activated = jax.nn.silu(jnp.dot(normed, w_in_l, preferred_element_type=jnp.float32)).astype(
        jnp.bfloat16
    )
    branch = jnp.dot(activated, w_out_l, preferred_element_type=jnp.float32).astype(jnp.bfloat16)
    return (summed, branch)


def local(
    edge_states,
    triplet_coeff,
    block_target,
    block_source,
    block_count,
    reverse_slot,
    w_proj,
    w_up,
    w_in,
    w_out,
    norm_gain,
):
    state = edge_states[0, 0]
    coeffs = triplet_coeff[0, 0]
    targets = block_target[0, 0]
    sources = block_source[0, 0]
    live_count = block_count[0, 0]
    reverse_rows = reverse_slot[0, 0]
    edge_count = state.shape[0]
    pairings = bit_pairings()
    mirrored = jnp.take(mirror_inputs(state, pairings), reverse_rows, axis=0)
    for layer_index in range(LAYERS):
        projected = jnp.einsum(
            "ed,dc->ce", state, w_proj[layer_index], preferred_element_type=jnp.float32
        ).astype(jnp.bfloat16)
        pooled = lax.all_gather(projected, "src", axis=1, tiled=True)
        agg_low = triplet_sums(pooled, coeffs, targets, sources, live_count, edge_count).astype(
            jnp.bfloat16
        )
        summed, branch = transform(
            state,
            agg_low,
            w_up[layer_index],
            w_in[layer_index],
            w_out[layer_index],
            norm_gain[layer_index],
        )
        agg_mirror = jnp.take(mirror_mixed(agg_low, pairings), reverse_rows, axis=1)
        summed_mirror, branch_mirror = transform(
            mirrored,
            agg_mirror,
            w_up[layer_index],
            w_in[layer_index],
            w_out[layer_index],
            norm_gain[layer_index],
        )
        state = (summed + branch.astype(jnp.float32) + branch_mirror.astype(jnp.float32)).astype(
            jnp.bfloat16
        )
        mirrored = (
            summed_mirror + branch_mirror.astype(jnp.float32) + branch.astype(jnp.float32)
        ).astype(jnp.bfloat16)
    return state[None, None]


def solution(mesh):
    return jax.shard_map(
        local,
        mesh=mesh,
        in_specs=(
            P("src", "tgt", None, None),
            P("src", "tgt", None, None, None),
            P("src", "tgt", None),
            P("src", "tgt", None),
            P("src", "tgt"),
            P("src", "tgt", None),
            P(),
            P(),
            P(),
            P(),
            P(),
        ),
        out_specs=P("src", "tgt", None, None),
        check_vma=False,
    )
```

profile of v0, /device:TPU:6, one launch (start us, length us, event | category | flops | bytes accessed | tf_op | source)
XLA Modules:
  0.0 182.4 jit_solution(321154064980947400)
XLA Ops:
  6.5 2.4 %convolution_convert_fusion.1 = bf16[64,512]{1,0:T(8,128)(2,1)} fusion(bf16[2,1024,64]{1,2,0:T(8,128)(2,1)} %param.21, bf16[1,1,512,1024]{3,2,1,0:T(8,128)(2,1)} %param.15), kind=kOutput, calls=%fused_computation.57 | convolution fusion | flops 67141632 | bytes 1245184 | tf_op jit(solution)/shard_map/ed,dc->ce/dot_general | solution.py:97
  9.0 0.0 all-gather.3.cloned.1.call-update
  9.0 0.0 all-gather.5.cloned.1.call-start
  9.0 0.6 collective-permute-start
  10.3 0.7 compare_select_fusion.1
  11.0 0.7 compare_select_fusion
  11.7 0.7 compare_select_fusion.2
  12.4 0.7 compare_and_fusion
  13.1 0.7 compare_and_fusion.1
  13.8 0.8 fusion.132
  14.5 0.0 copy-start.3
  14.6 19.8 %collective-permute-done = bf16[512,1024]{1,0:T(8,128)(2,1)} collective-permute-done((bf16[512,1024]{1,0:T(8,128)(2,1)}, bf16[512,1024]{1,0:T(8,128)(2,1)}, u32[]{:S(2)}, u32[]{:S(2)}) %collective-permute-start) | collective-permute-done | bytes 1048608 | tf_op jit(solution)/shard_map/ppermute | solution.py:11
  34.3 2.6 %collective-permute-start.1 = (bf16[512,1024]{1,0:T(8,128)(2,1)}, bf16[512,1024]{1,0:T(8,128)(2,1)}, u32[]{:S(2)}, u32[]{:S(2)}) collective-permute-start(bf16[512,1024]{1,0:T(8,128)(2,1)} %collective-permute-done), channel_id=1, source_target_pairs={{0,16},{1,17},{2,18},{3,19},{4,20},{5,21},{6,22},{7,23},{8,24},{9,... | collective-permute-start | bytes 3145736 | tf_op jit(solution)/shard_map/ppermute | solution.py:11
  36.9 31.2 %all-gather.3.cloned.1.call-done = bf16[64,8192]{1,0:T(8,128)(2,1)} async-done(((bf16[64,512]{1,0:T(8,128)(2,1)}), bf16[64,8192]{1,0:T(8,128)(2,1)}) %all-gather.3.cloned.1.call-update) | async-done | bytes 1048592 | tf_op jit(solution)/shard_map/all_gather | solution.py:100
  68.1 1.5 copy_bitcast_fusion.1
  69.6 0.6 gather_fusion.1
  70.2 0.3 fusion.76
  70.6 0.3 convolution_convert_fusion.3
  70.8 0.1 copy.17
  71.0 0.6 collective-permute-start.2
  71.6 1.8 multiply_reduce_fusion.3
  73.4 6.4 %fusion.26 = bf16[512,1024]{1,0:T(8,128)(2,1)} fusion(bf16[2,1024,1024]{2,1,0:T(8,128)(2,1)} %param.24, bf16[2,1024,1024]{2,1,0:T(8,128)(2,1)} %param.23, f32[512,1024]{1,0:T(8,128)} %get-tuple-element.12, f32[512]{0:T(512)S(1)} %add_rsqrt_fusion.3, f32[1024]{0:T(1024)S(1)} %bitcast.171), kind=kOutput, calls=%fused_computation.52 | convolution fusion | flops 2152202240 | bytes 7346176 | tf_op jit(solution)/shard_map/dot_general | solution.py:70
  79.8 2.3 %collective-permute-start.3 = (bf16[64,512]{0,1:T(8,128)(2,1)S(1)}, bf16[64,512]{0,1:T(8,128)(2,1)S(1)}, u32[]{:S(2)}, u32[]{:S(2)}) collective-permute-start(bf16[64,512]{0,1:T(8,128)(2,1)S(1)} %collective-permute-done.2), channel_id=1, source_target_pairs={{0,16},{1,17},{2,18},{3,19},{4,20},{5,21},{6,22},{7,23},{8,24},{9,... | collective-permute-start | bytes 196616 | tf_op jit(solution)/shard_map/ppermute | solution.py:11
  82.0 7.6 %collective-permute-done.1 = bf16[512,1024]{1,0:T(8,128)(2,1)} collective-permute-done((bf16[512,1024]{1,0:T(8,128)(2,1)}, bf16[512,1024]{1,0:T(8,128)(2,1)}, u32[]{:S(2)}, u32[]{:S(2)}) %collective-permute-start.1) | collective-permute-done | bytes 1048608 | tf_op jit(solution)/shard_map/ppermute | solution.py:11
  89.7 1.3 broadcast_select_fusion
  91.0 3.0 %gather_fusion = bf16[512,1024]{1,0:T(8,128)(2,1)} fusion(bf16[512,1024]{1,0:T(8,128)(2,1)S(1)} %broadcast_select_fusion, s32[1024]{0:T(1024)S(1)} %pad_clamp_fusion.1), kind=kCustom, calls=%fused_computation.4 | custom fusion | bytes 2099200 | tf_op jit(solution)/shard_map/jit(_take)/gather | solution.py:95
  94.0 1.3 gather_fusion.2
  95.3 1.8 %multiply_reduce_fusion.2 = (f32[512]{0:T(512)S(1)}, f32[512,1024]{1,0:T(8,128)S(1)}) fusion(bf16[2,64,1024]{2,1,0:T(8,128)(2,1)S(1)} %copy-done.3, bf16[512,64]{1,0:T(8,128)(2,1)S(1)} %gather_fusion.2, pred[512]{0:T(512)(128)(4,1)S(1)} %compare_and_fusion.1, bf16[512,1024]{1,0:T(8,128)(2,1)} %gather_fusion), kind=kOutput, calls=%fused_computation.38 | convolution fusion | flops 69762560 | bytes 3410944 | tf_op jit(solution)/shard_map/ce,cd->ed/dot_general | solution.py:62
  97.2 0.0 copy-start.4
  97.2 7.0 %fusion.1 = (bf16[512,1024]{1,0:T(8,128)(2,1)}, bf16[512,1024]{1,0:T(8,128)(2,1)}) fusion(f32[512,1024]{1,0:T(8,128)} %get-tuple-element.12, bf16[512,1024]{1,0:T(8,128)(2,1)} %fusion.26, bf16[2,1024,1024]{2,1,0:T(8,128)(2,1)} %param.24, bf16[2,1024,1024]{2,1,0:T(8,128)(2,1)} %param.23, f32[512,1024]{1,0:T(8,128)S(1)} %get-tuple-element.10, ...), kind=kOutput, calls=%fused_computation.10 | convolution fusion | flops 2154823680 | bytes 11540480 | tf_op jit(solution)/shard_map/dot_general | solution.py:70
  104.2 2.3 %fusion.38 = bf16[64,512]{1,0:T(8,128)(2,1)} fusion(bf16[512,1024]{1,0:T(8,128)(2,1)} %get-tuple-element.13, bf16[2,1024,64]{1,2,0:T(8,128)(2,1)S(1)} %copy-done.4), kind=kOutput, calls=%fused_computation.60 | convolution fusion | flops 67141632 | bytes 1245184 | tf_op jit(solution)/shard_map/ed,dc->ce/dot_general | solution.py:97
  106.5 0.0 all-gather.5.cloned.1.call-update
  106.6 35.1 %all-gather.5.cloned.1.call-done = bf16[64,8192]{1,0:T(8,128)(2,1)} async-done(((bf16[64,512]{1,0:T(8,128)(2,1)}), bf16[64,8192]{1,0:T(8,128)(2,1)}) %all-gather.5.cloned.1.call-update) | async-done | bytes 1048592 | tf_op jit(solution)/shard_map/all_gather | solution.py:100
  141.7 2.5 %copy_bitcast_fusion = bf16[64,64,128]{2,0,1:T(8,128)(2,1)} fusion(bf16[64,8192]{1,0:T(8,128)(2,1)} %all-gather.5.cloned.1.call-done), kind=kLoop, calls=%fused_computation.62 | loop fusion | bytes 2097152 | tf_op jit(solution)/shard_map/reshape | solution.py:51
  144.2 1.8 gather_fusion.3
  146.0 0.3 fusion.74
  146.3 0.3 convolution_convert_fusion.2
  146.6 0.6 copy-done.2
  147.2 1.8 multiply_reduce_fusion.1
  149.0 0.1 copy.20
  149.1 0.6 collective-permute-start.4
  149.8 5.1 %collective-permute-done.4 = bf16[64,512]{0,1:T(8,128)(2,1)S(1)} collective-permute-done((bf16[64,512]{0,1:T(8,128)(2,1)S(1)}, bf16[64,512]{0,1:T(8,128)(2,1)S(1)}, u32[]{:S(2)}, u32[]{:S(2)}) %collective-permute-start.4) | collective-permute-done | bytes 65568 | tf_op jit(solution)/shard_map/ppermute | solution.py:11
  154.9 1.8 collective-permute-start.5
  156.6 6.4 %fusion.32 = bf16[512,1024]{1,0:T(8,128)(2,1)} fusion(bf16[2,1024,1024]{2,1,0:T(8,128)(2,1)} %param.24, bf16[2,1024,1024]{2,1,0:T(8,128)(2,1)} %param.23, f32[512,1024]{1,0:T(8,128)} %get-tuple-element.16, f32[512]{0:T(512)S(1)} %add_rsqrt_fusion.1, f32[1024]{0:T(1024)S(1)} %bitcast.169), kind=kOutput, calls=%fused_computation.54 | convolution fusion | flops 2152202240 | bytes 7346176 | tf_op jit(solution)/shard_map/dot_general | solution.py:70
  163.0 0.4 collective-permute-done.5
  163.4 1.3 gather_fusion.4
  164.8 3.5 %multiply_reduce_fusion = (f32[512]{0:T(512)S(1)}, f32[512,1024]{1,0:T(8,128)}) fusion(bf16[2,64,1024]{2,1,0:T(8,128)(2,1)S(1)} %copy-done.3, bf16[512,64]{1,0:T(8,128)(2,1)S(1)} %gather_fusion.4, pred[512]{0:T(512)(128)(4,1)S(1)} %compare_and_fusion.1, bf16[512,1024]{1,0:T(8,128)(2,1)} %fusion.26, f32[512,1024]{1,0:T(8,128)S(1)} %get-tuple-element.10, ...), kind=kOutput, calls=%fused_computation.30 | convolution fusion | flops 71859712 | bytes 6556160 | tf_op jit(solution)/shard_map/ce,cd->ed/dot_general | solution.py:62
  168.3 7.2 %fusion.41 = bf16[1,1,512,1024]{3,2,1,0:T(8,128)(2,1)} fusion(bf16[2,1024,1024]{2,1,0:T(8,128)(2,1)} %param.24, f32[512,1024]{1,0:T(8,128)} %get-tuple-element.16, bf16[512,1024]{1,0:T(8,128)(2,1)} %fusion.32, bf16[2,1024,1024]{2,1,0:T(8,128)(2,1)} %param.23, f32[512,1024]{1,0:T(8,128)} %get-tuple-element.18, f32[512]{0:T(512)S(1)} %add_rsqrt_fusion, ...), kind=kOutput, calls=%fused_computation.61 | convolution fusion | flops 2154823680 | bytes 10491904 | tf_op jit(solution)/shard_map/dot_general | solution.py:70
  (24 shorter events, 0.1 us)
Async XLA Ops:
  6.5 63.7 %copy-start = (bf16[1,1,16,128,128]{4,3,2,1,0:T(8,128)(2,1)S(1)}, bf16[1,1,16,128,128]{4,3,2,1,0:T(8,128)(2,1)}, u32[]{:S(2)}) copy-start(bf16[1,1,16,128,128]{4,3,2,1,0:T(8,128)(2,1)} %param.16) | copy-start | bytes 1572868
  6.5 61.5 %all-gather.3.cloned.1.call-start = ((), (), s32[]{:S(2)}) async-start(), calls=%async_computation | async-start | bytes 1114112 | tf_op jit(solution)/shard_map/all_gather | solution.py:100
  9.0 61.6 %copy-start.5 = (s32[1,1,16]{2,1,0:T(1,128)S(1)}, s32[1,1,16]{2,1,0:T(1,128)}, u32[]{:S(2)}) copy-start(s32[1,1,16]{2,1,0:T(1,128)} %param.17) | copy-start | bytes 196
  9.0 132.7 %all-gather.5.cloned.1.call-start = ((), (), s32[]{:S(2)}) async-start(), calls=%async_computation.1 | async-start | bytes 1114112 | tf_op jit(solution)/shard_map/all_gather | solution.py:100
  9.0 25.3 %collective-permute-start = (bf16[512,1024]{1,0:T(8,128)(2,1)}, bf16[512,1024]{1,0:T(8,128)(2,1)}, u32[]{:S(2)}, u32[]{:S(2)}) collective-permute-start(bf16[512,1024]{1,0:T(8,128)(2,1)} %bitcast.159), channel_id=1, source_target_pairs={{0,1},{1,0},{2,3},{3,2},{4,5},{5,4},{6,7},{7,6},{8,9},{9,8},{10,11... | collective-permute-start | bytes 3145736 | tf_op jit(solution)/shard_map/ppermute | solution.py:11
  14.5 57.0 %copy-start.1 = (bf16[1,1,512,1024]{3,2,1,0:T(8,128)(2,1)S(1)}, bf16[1,1,512,1024]{3,2,1,0:T(8,128)(2,1)}, u32[]{:S(2)}) copy-start(bf16[1,1,512,1024]{3,2,1,0:T(8,128)(2,1)} %param.15) | copy-start | bytes 3145732
  14.5 57.0 %copy-start.3 = (bf16[2,64,1024]{2,1,0:T(8,128)(2,1)S(1)}, bf16[2,64,1024]{2,1,0:T(8,128)(2,1)}, u32[]{:S(2)}) copy-start(bf16[2,64,1024]{2,1,0:T(8,128)(2,1)} %param.22) | copy-start | bytes 786436
  34.3 55.3 %collective-permute-start.1 = (bf16[512,1024]{1,0:T(8,128)(2,1)}, bf16[512,1024]{1,0:T(8,128)(2,1)}, u32[]{:S(2)}, u32[]{:S(2)}) collective-permute-start(bf16[512,1024]{1,0:T(8,128)(2,1)} %collective-permute-done), channel_id=1, source_target_pairs={{0,16},{1,17},{2,18},{3,19},{4,20},{5,21},{6,22},{7,23},{8,24},{9,... | collective-permute-start | bytes 3145736 | tf_op jit(solution)/shard_map/ppermute | solution.py:11
  71.0 8.8 %collective-permute-start.2 = (bf16[64,512]{0,1:T(8,128)(2,1)S(1)}, bf16[64,512]{0,1:T(8,128)(2,1)S(1)}, u32[]{:S(2)}, u32[]{:S(2)}) collective-permute-start(bf16[64,512]{0,1:T(8,128)(2,1)S(1)} %copy.17), channel_id=1, source_target_pairs={{0,1},{1,0},{2,3},{3,2},{4,5},{5,4},{6,7},{7,6},{8,9},{9,8},{10,11... | collective-permute-start | bytes 196616 | tf_op jit(solution)/shard_map/ppermute | solution.py:11
  79.8 14.2 %collective-permute-start.3 = (bf16[64,512]{0,1:T(8,128)(2,1)S(1)}, bf16[64,512]{0,1:T(8,128)(2,1)S(1)}, u32[]{:S(2)}, u32[]{:S(2)}) collective-permute-start(bf16[64,512]{0,1:T(8,128)(2,1)S(1)} %collective-permute-done.2), channel_id=1, source_target_pairs={{0,16},{1,17},{2,18},{3,19},{4,20},{5,21},{6,22},{7,23},{8,24},{9,... | collective-permute-start | bytes 196616 | tf_op jit(solution)/shard_map/ppermute | solution.py:11
  97.2 7.0 %copy-start.4 = (bf16[2,1024,64]{1,2,0:T(8,128)(2,1)S(1)}, bf16[2,1024,64]{1,2,0:T(8,128)(2,1)}, u32[]{:S(2)}) copy-start(bf16[2,1024,64]{1,2,0:T(8,128)(2,1)} %param.21) | copy-start | bytes 786436
  146.0 1.2 copy-start.2
  149.1 5.7 %collective-permute-start.4 = (bf16[64,512]{0,1:T(8,128)(2,1)S(1)}, bf16[64,512]{0,1:T(8,128)(2,1)S(1)}, u32[]{:S(2)}, u32[]{:S(2)}) collective-permute-start(bf16[64,512]{0,1:T(8,128)(2,1)S(1)} %copy.20), channel_id=1, source_target_pairs={{0,1},{1,0},{2,3},{3,2},{4,5},{5,4},{6,7},{7,6},{8,9},{9,8},{10,11... | collective-permute-start | bytes 196616 | tf_op jit(solution)/shard_map/ppermute | solution.py:11
  154.9 8.6 %collective-permute-start.5 = (bf16[64,512]{0,1:T(8,128)(2,1)S(1)}, bf16[64,512]{0,1:T(8,128)(2,1)S(1)}, u32[]{:S(2)}, u32[]{:S(2)}) collective-permute-start(bf16[64,512]{0,1:T(8,128)(2,1)S(1)} %collective-permute-done.4), channel_id=1, source_target_pairs={{0,16},{1,17},{2,18},{3,19},{4,20},{5,21},{6,22},{7,23},{8,24},{9,... | collective-permute-start | bytes 196616 | tf_op jit(solution)/shard_map/ppermute | solution.py:11
Sparse Core Ops, SparseCore 0:
  9.5 58.5 all-gather.2
  106.7 34.9 all-gather.4
where the time goes:
time: 185 us; the launch traced here: 182 us
  waiting for transfers between devices  99.2 us (54%)
  matrix products  41.9 us (23%)
  between operations  14.3 us (8%)
  local copies, waits for them, and re-layouts  13.8 us (7%)
  starting transfers between devices  8.48 us (5%)
  other arithmetic  4.81 us (3%)
    all_gather x2, waiting for transfers between devices, local(): pooled = lax.all_gather(projected, 'src', axis=1, tiled=True)  66.3 us
    ppermute x6, waiting for transfers between devices, partner(): lax.ppermute(value, axis, [(i, i ^ 1 << bit) for i in range(lax.axis_size...  32.9 us
    dot_general x4, matrix products, transform(): jnp.dot(activated, w_out_l, preferred_element_type=jnp.float32)  27.1 us
    dot_general x4, matrix products, transform(): jnp.einsum('ce,cd->ed', agg_low, w_up_l, preferred_element_type=jnp.float32)  8.93 us
    ppermute x6, starting transfers between devices, partner(): lax.ppermute(value, axis, [(i, i ^ 1 << bit) for i in range(lax.axis_size...  8.44 us
    dot_general x2, matrix products, local(): jnp.einsum('ed,dc->ce', state, w_proj[layer_index], preferred_element_typ...  4.72 us
    reshape x2, local copies, waits for them, and re-layouts, triplet_sums(): blocks = pooled.reshape(width, pooled.shape[1] // BLK, BLK)  4 us
  transfers between devices with their start and end apart: 8, of which 6 were waited for; matrix products, arithmetic and copies ran while one was open for 14% of the time, Pallas kernels for 0%

commit v1 on v0

--- a/solution.py
+++ b/solution.py
@@ -7,49 +7,61 @@
 LAYERS = 2
 
 
-def partner(value, axis, bit):
-    return lax.ppermute(value, axis, [(i, i ^ 1 << bit) for i in range(lax.axis_size(axis))])
+def mirror_pairs():
+    groups = lax.axis_size("tgt")
+    copies = lax.axis_size("src") // groups
+    pairs = []
+    for p in range(groups * copies):
+        a, r = divmod(p, copies)
+        for q in range(groups):
+            if a != q:
+                pairs.append((p * groups + q, (q * copies + r) * groups + a))
+    return pairs
 
 
-def bit_pairings():
-    groups = lax.axis_size("tgt")
-    width = groups.bit_length() - 1
-    src_bits = lax.axis_size("src").bit_length() - 1
-    position = lax.axis_index("src") * groups + lax.axis_index("tgt")
-    pairings = []
-    for bit_index in range(width):
-        upper = bit_index + src_bits
-        differ = position // 2**bit_index % 2 != position // 2**upper % 2
-        pairings.append(((bit_index, upper), differ))
-    return pairings
+def mirror_tile(values):
+    copies = lax.axis_size("src") // lax.axis_size("tgt")
+    same = lax.axis_index("src") // copies == lax.axis_index("tgt")
+    moved = lax.ppermute(values, ("src", "tgt"), mirror_pairs())
+    return jnp.where(same, values, moved)
 
 
-def mirror_inputs(values, pairings):
-    carried = values
-    for bit_pair, differ in pairings:
-        hopped = carried
-        for bit_index in bit_pair:
-            hopped = partner(hopped, ("src", "tgt"), bit_index)
-        carried = jnp.where(differ, hopped, carried)
-    return carried
+def gather_pool(projected):
+    size = lax.axis_size("src")
+    held = projected[None]
+    bit = size // 2
+    while bit:
+        held = jnp.concatenate(
+            [held, lax.ppermute(held, "src", [(i, i ^ bit) for i in range(size)])], axis=0
+        )
+        bit //= 2
+    return held
 
 
-def mirror_mixed(values, pairings):
-    carried = values
-    for bit_pair, differ in pairings:
-        hopped = carried
-        for bit_index in bit_pair:
-            hopped = partner(hopped, ("src", "tgt"), bit_index)
-        carried = jnp.where(differ, hopped, carried)
-    return carried
+def pool_slots(sources, blocks_per_tile):
+    size = lax.axis_size("src")
+    relative = (sources // blocks_per_tile) ^ lax.axis_index("src")
+    slots = jnp.zeros_like(relative)
+    bit, place = size // 2, 1
+    while bit:
+        slots = slots + jnp.where((relative & bit) != 0, place, 0)
+        bit //= 2
+        place *= 2
+    return slots, sources % blocks_per_tile
 
 
 def triplet_sums(pooled, coeffs, targets, sources, live_count, edge_count):
-    width = pooled.shape[0]
+    width = pooled.shape[1]
     slots = coeffs.shape[0]
     out_blocks = edge_count // BLK
-    blocks = pooled.reshape(width, pooled.shape[1] // BLK, BLK)
-    picked = jnp.take(blocks, sources, axis=1)
+    tile, block = pool_slots(sources, out_blocks)
+    picked = jnp.stack(
+        [
+            lax.dynamic_slice(pooled, (tile[b], 0, block[b] * BLK), (1, width, BLK))[0]
+            for b in range(slots)
+        ],
+        axis=1,
+    )
     products = jnp.einsum("cbj,bji->cbi", picked, coeffs, preferred_element_type=jnp.float32)
     live_mask = (jnp.arange(slots) < live_count).astype(jnp.float32)
     placing = (targets[:, None] == jnp.arange(out_blocks)[None, :]).astype(jnp.float32) * live_mask[
@@ -91,13 +103,12 @@
     live_count = block_count[0, 0]
     reverse_rows = reverse_slot[0, 0]
     edge_count = state.shape[0]
-    pairings = bit_pairings()
-    mirrored = jnp.take(mirror_inputs(state, pairings), reverse_rows, axis=0)
+    mirrored = jnp.take(mirror_tile(state), reverse_rows, axis=0)
     for layer_index in range(LAYERS):
         projected = jnp.einsum(
             "ed,dc->ce", state, w_proj[layer_index], preferred_element_type=jnp.float32
         ).astype(jnp.bfloat16)
-        pooled = lax.all_gather(projected, "src", axis=1, tiled=True)
+        pooled = gather_pool(projected)
         agg_low = triplet_sums(pooled, coeffs, targets, sources, live_count, edge_count).astype(
             jnp.bfloat16
         )
@@ -109,7 +120,7 @@
             w_out[layer_index],
             norm_gain[layer_index],
         )
-        agg_mirror = jnp.take(mirror_mixed(agg_low, pairings), reverse_rows, axis=1)
+        agg_mirror = jnp.take(mirror_tile(agg_low), reverse_rows, axis=1)
         summed_mirror, branch_mirror = transform(
             mirrored,
             agg_mirror,

time: 185 us -> 193 us (1.043)
  waiting for transfers between devices: 99.2 us -> 40.1 us
  starting transfers between devices: 8.48 us -> 41 us
  between operations: 14.3 us -> 41.3 us
  local copies, waits for them, and re-layouts: 13.8 us -> 22 us
    all_gather x2 -> x0, waiting for transfers between devices: 66.3 us -> none  [local(): pooled = lax.all_gather(projected, 'src', axis=1, tiled=True)]
    ppermute x6 -> x11, starting transfers between devices: 8.44 us -> 41 us  [the longest x8 27.8 us: gather_pool(): lax.ppermute(held, 'src', [(i, i ^ bit) for i in range(size)])]
    unnamed x14 -> x54, local copies, waits for them, and re-layouts: 0.66 us -> 13.3 us
    ppermute x6 -> x11, waiting for transfers between devices: 32.9 us -> 40.1 us  [the longest x8 40.1 us: gather_pool(): lax.ppermute(held, 'src', [(i, i ^ bit) for i in range(size)])]
    reshape x2 -> x0, local copies, waits for them, and re-layouts: 4 us -> none  [triplet_sums(): blocks = pooled.reshape(width, pooled.shape[1] // BLK, BLK)]
    gather x5 -> x3, local copies, waits for them, and re-layouts: 8.07 us -> 5.46 us  [the longest x1 2.78 us: local(): mirrored = jnp.take(mirror_tile(state), reverse_rows, axis=0)]
  transfers between devices with their start and end apart: 8 -> 11, of which waited for: 6 -> 6; matrix products, arithmetic and copies ran while one was open for 14% -> 21% of each run, Pallas kernels for 0% -> 0%
where the time goes in v1:
time: 193 us; the launch traced here: 189 us
  between operations  41.3 us (21%)
  matrix products  41.1 us (21%)
  starting transfers between devices  41 us (21%)
  waiting for transfers between devices  40.1 us (21%)
  local copies, waits for them, and re-layouts  22 us (11%)
  other arithmetic  3.65 us (2%)
    ppermute x8, waiting for transfers between devices, gather_pool(): lax.ppermute(held, 'src', [(i, i ^ bit) for i in range(size)])  40.1 us
    ppermute x8, starting transfers between devices, gather_pool(): lax.ppermute(held, 'src', [(i, i ^ bit) for i in range(size)])  27.8 us
    dot_general x4, matrix products, transform(): jnp.dot(activated, w_out_l, preferred_element_type=jnp.float32)  27.1 us
    unnamed x54, local copies, waits for them, and re-layouts  13.3 us
    ppermute x3, starting transfers between devices, mirror_tile(): moved = lax.ppermute(values, ('src', 'tgt'), mirror_pairs())  13.2 us
    dot_general x4, matrix products, transform(): jnp.einsum('ce,cd->ed', agg_low, w_up_l, preferred_element_type=jnp.float32)  8.96 us
    dot_general x2, matrix products, local(): jnp.einsum('ed,dc->ce', state, w_proj[layer_index], preferred_element_typ...  4.05 us
  transfers between devices with their start and end apart: 11, of which 6 were waited for; matrix products, arithmetic and copies ran while one was open for 21% of the time, Pallas kernels for 0%

profile of v1, /device:TPU:6, one launch (start us, length us, event | category | flops | bytes accessed | tf_op | source)
XLA Modules:
  0.0 189.2 jit_solution(8835319379248686966)
XLA Ops:
  0.0 4.6 %collective-permute-start.4 = (bf16[512,1024]{1,0:T(8,128)(2,1)}, bf16[512,1024]{1,0:T(8,128)(2,1)}, u32[]{:S(2)}, u32[]{:S(2)}) collective-permute-start(bf16[512,1024]{1,0:T(8,128)(2,1)} %bitcast.264), channel_id=1, source_target_pairs={{1,16},{3,18},{5,20},{7,22},{9,24},{11,26},{13,28},{15,30},{16,1},... | collective-permute-start | bytes 3145736 | tf_op jit(solution)/shard_map/ppermute | solution.py:25
  4.6 2.4 %constant_dynamic-update-slice_fusion.4 = (bf16[16,64,512]{2,1,0:T(8,128)(2,1)}, bf16[1,64,512]{2,1,0:T(8,128)(2,1)S(1)}) fusion(bf16[1,1,512,1024]{3,2,1,0:T(8,128)(2,1)} %param.13, bf16[2,1024,64]{1,2,0:T(8,128)(2,1)} %param.19), kind=kOutput, calls=%fused_computation.113 | convolution fusion | flops 67141632 | bytes 1310720 | tf_op jit(solution)/shard_map/ed,dc->ce/dot_general | solution.py:108
  7.0 0.7 compare_select_fusion
  7.7 0.7 compare_select_fusion.1
  8.4 0.7 and_select_fusion
  9.0 0.7 fusion.127
  9.8 18.9 %collective-permute-done = bf16[1,64,512]{2,1,0:T(8,128)(2,1)S(1)} collective-permute-done((bf16[1,64,512]{2,1,0:T(8,128)(2,1)S(1)}, bf16[1,64,512]{2,1,0:T(8,128)(2,1)S(1)}, u32[]{:S(2)}, u32[]{:S(2)}) %collective-permute-start) | collective-permute-done | bytes 65568 | tf_op jit(solution)/shard_map/ppermute | solution.py:35
  28.7 25.4 %collective-permute-start.1 = (bf16[2,64,512]{2,1,0:T(8,128)(2,1)S(1)}, bf16[2,64,512]{2,1,0:T(8,128)(2,1)S(1)}, u32[]{:S(2)}, u32[]{:S(2)}) collective-permute-start(bf16[2,64,512]{2,1,0:T(8,128)(2,1)S(1)} %pad_maximum_fusion.4), channel_id=1, source_target_pairs={{0,8},{2,10},{4,12},{6,14},{8,0},{10,2},{12,4},{14,6},{16,24},{18,... | collective-permute-start | bytes 393224 | tf_op jit(solution)/shard_map/ppermute | solution.py:35
  54.7 0.7 fusion.128
  55.4 2.3 %collective-permute-done.1 = bf16[2,64,512]{2,1,0:T(8,128)(2,1)S(1)} collective-permute-done((bf16[2,64,512]{2,1,0:T(8,128)(2,1)S(1)}, bf16[2,64,512]{2,1,0:T(8,128)(2,1)S(1)}, u32[]{:S(2)}, u32[]{:S(2)}) %collective-permute-start.1) | collective-permute-done | bytes 131104 | tf_op jit(solution)/shard_map/ppermute | solution.py:35
  100.2 0.7 constant_dynamic-update-slice_fusion.1
  100.9 0.8 constant_dynamic-update-slice_fusion
  101.7 0.7 constant_dynamic-update-slice_fusion.20
  102.4 0.7 constant_dynamic-update-slice_fusion.19
  103.2 0.7 constant_dynamic-update-slice_fusion.18
  103.9 0.7 constant_dynamic-update-slice_fusion.17
  104.6 0.7 constant_dynamic-update-slice_fusion.16
  105.3 0.7 constant_dynamic-update-slice_fusion.15
  106.1 0.7 constant_dynamic-update-slice_fusion.14
  106.8 0.7 constant_dynamic-update-slice_fusion.13
  107.5 0.7 constant_dynamic-update-slice_fusion.12
  108.2 0.7 constant_dynamic-update-slice_fusion.11
  109.0 0.7 constant_dynamic-update-slice_fusion.10
  109.7 0.7 constant_dynamic-update-slice_fusion.9
  110.4 0.7 constant_dynamic-update-slice_fusion.8
  111.1 0.7 constant_dynamic-update-slice_fusion.7
  111.9 0.7 constant_dynamic-update-slice_fusion.6
  112.6 0.7 constant_dynamic-update-slice_fusion.5
  114.0 3.0 %collective-permute-start.5 = (bf16[64,512]{0,1:T(8,128)(2,1)S(1)}, bf16[64,512]{0,1:T(8,128)(2,1)S(1)}, u32[]{:S(2)}, u32[]{:S(2)}) collective-permute-start(bf16[64,512]{0,1:T(8,128)(2,1)S(1)} %copy.17), channel_id=1, source_target_pairs={{1,16},{3,18},{5,20},{7,22},{9,24},{11,26},{13,28},{15,30},{16,1},... | collective-permute-start | bytes 196616 | tf_op jit(solution)/shard_map/ppermute | solution.py:25
  117.0 1.8 multiply_reduce_fusion.3
  118.8 6.4 %fusion.26 = bf16[512,1024]{1,0:T(8,128)(2,1)} fusion(bf16[2,1024,1024]{2,1,0:T(8,128)(2,1)} %param.22, bf16[2,1024,1024]{2,1,0:T(8,128)(2,1)} %param.21, f32[512,1024]{1,0:T(8,128)} %get-tuple-element.47, f32[512]{0:T(512)S(1)} %add_rsqrt_fusion.3, f32[1024]{0:T(1024)S(1)} %bitcast.276), kind=kOutput, calls=%fused_computation.50 | convolution fusion | flops 2152202240 | bytes 7346176 | tf_op jit(solution)/shard_map/dot_general | solution.py:82
  125.2 1.3 broadcast_select_fusion
  126.6 2.8 %gather_fusion = bf16[512,1024]{1,0:T(8,128)(2,1)} fusion(bf16[512,1024]{1,0:T(8,128)(2,1)S(1)} %broadcast_select_fusion, s32[1024]{0:T(1024)S(1)} %get-tuple-element.57), kind=kCustom, calls=%fused_computation.2 | custom fusion | bytes 2099200 | tf_op jit(solution)/shard_map/jit(_take)/gather | solution.py:106
  129.4 1.3 gather_fusion.1
  130.7 1.9 multiply_reduce_fusion.2
  132.6 7.0 %fusion.1 = (bf16[512,1024]{1,0:T(8,128)(2,1)}, bf16[512,1024]{1,0:T(8,128)(2,1)}) fusion(f32[512,1024]{1,0:T(8,128)} %get-tuple-element.47, bf16[512,1024]{1,0:T(8,128)(2,1)} %fusion.26, bf16[2,1024,1024]{2,1,0:T(8,128)(2,1)} %param.22, bf16[2,1024,1024]{2,1,0:T(8,128)(2,1)} %param.21, f32[512,1024]{1,0:T(8,128)S(1)} %get-tuple-element.45, ...), kind=kOutput, calls=%fused_computation.8 | convolution fusion | flops 2154823680 | bytes 11540480 | tf_op jit(solution)/shard_map/dot_general | solution.py:82
  139.6 1.7 constant_dynamic-update-slice_fusion.25
  141.4 6.5 %collective-permute-done.6 = bf16[1,64,512]{2,1,0:T(8,128)(2,1)S(1)} collective-permute-done((bf16[1,64,512]{2,1,0:T(8,128)(2,1)S(1)}, bf16[1,64,512]{2,1,0:T(8,128)(2,1)S(1)}, u32[]{:S(2)}, u32[]{:S(2)}) %collective-permute-start.6) | collective-permute-done | bytes 65568 | tf_op jit(solution)/shard_map/ppermute | solution.py:35
  148.0 5.1 %collective-permute-done.7 = bf16[2,64,512]{2,1,0:T(8,128)(2,1)S(1)} collective-permute-done((bf16[2,64,512]{2,1,0:T(8,128)(2,1)S(1)}, bf16[2,64,512]{2,1,0:T(8,128)(2,1)S(1)}, u32[]{:S(2)}, u32[]{:S(2)}) %collective-permute-start.7) | collective-permute-done | bytes 131104 | tf_op jit(solution)/shard_map/ppermute | solution.py:35
  153.1 1.6 collective-permute-start.8
  154.6 5.5 %collective-permute-done.8 = bf16[4,64,512]{2,1,0:T(8,128)(2,1)S(1)} collective-permute-done((bf16[4,64,512]{2,1,0:T(8,128)(2,1)S(1)}, bf16[4,64,512]{2,1,0:T(8,128)(2,1)S(1)}, u32[]{:S(2)}, u32[]{:S(2)}) %collective-permute-start.8) | collective-permute-done | bytes 262176 | tf_op jit(solution)/shard_map/ppermute | solution.py:35
  160.3 1.8 collective-permute-done.9
  163.1 1.8 multiply_reduce_fusion.1
  165.1 5.6 %collective-permute-start.10 = (bf16[64,512]{0,1:T(8,128)(2,1)S(1)}, bf16[64,512]{0,1:T(8,128)(2,1)S(1)}, u32[]{:S(2)}, u32[]{:S(2)}) collective-permute-start(bf16[64,512]{0,1:T(8,128)(2,1)S(1)} %copy.19), channel_id=1, source_target_pairs={{1,16},{3,18},{5,20},{7,22},{9,24},{11,26},{13,28},{15,30},{16,1},... | collective-permute-start | bytes 196616 | tf_op jit(solution)/shard_map/ppermute | solution.py:25
  170.7 6.4 %fusion.32 = bf16[512,1024]{1,0:T(8,128)(2,1)} fusion(bf16[2,1024,1024]{2,1,0:T(8,128)(2,1)} %param.22, bf16[2,1024,1024]{2,1,0:T(8,128)(2,1)} %param.21, f32[512,1024]{1,0:T(8,128)} %get-tuple-element.53, f32[512]{0:T(512)S(1)} %add_rsqrt_fusion.1, f32[1024]{0:T(1024)S(1)} %bitcast.274), kind=kOutput, calls=%fused_computation.52 | convolution fusion | flops 2152202240 | bytes 7346176 | tf_op jit(solution)/shard_map/dot_general | solution.py:82
  177.2 1.3 gather_fusion.2
  178.5 3.5 %multiply_reduce_fusion = (f32[512]{0:T(512)S(1)}, f32[512,1024]{1,0:T(8,128)}) fusion(bf16[2,64,1024]{2,1,0:T(8,128)(2,1)S(1)} %copy-done.3, bf16[512,64]{1,0:T(8,128)(2,1)S(1)} %gather_fusion.2, pred[512]{0:T(512)(128)(4,1)S(1)} %compare_and_fusion, bf16[512,1024]{1,0:T(8,128)(2,1)} %fusion.26, f32[512,1024]{1,0:T(8,128)S(1)} %get-tuple-element.45, ...), kind=kOutput, calls=%fused_computation.28 | convolution fusion | flops 71859712 | bytes 6556160 | tf_op jit(solution)/shard_map/ce,cd->ed/dot_general | solution.py:74
  182.0 7.2 %fusion.42 = bf16[1,1,512,1024]{3,2,1,0:T(8,128)(2,1)} fusion(bf16[2,1024,1024]{2,1,0:T(8,128)(2,1)} %param.22, f32[512,1024]{1,0:T(8,128)} %get-tuple-element.53, bf16[512,1024]{1,0:T(8,128)(2,1)} %fusion.32, bf16[2,1024,1024]{2,1,0:T(8,128)(2,1)} %param.21, f32[512,1024]{1,0:T(8,128)} %get-tuple-element.55, f32[512]{0:T(512)S(1)} %add_rsqrt_fusion, ...), kind=kOutput, calls=%fused_computation.60 | convolution fusion | flops 2154823680 | bytes 10491904 | tf_op jit(solution)/shard_map/dot_general | solution.py:82
  (73 shorter events, 4.2 us)
Async XLA Ops:
  0.0 113.3 %copy-start = (bf16[1,1,16,128,128]{4,3,2,1,0:T(8,128)(2,1)S(1)}, bf16[1,1,16,128,128]{4,3,2,1,0:T(8,128)(2,1)}, u32[]{:S(2)}) copy-start(bf16[1,1,16,128,128]{4,3,2,1,0:T(8,128)(2,1)} %param.14) | copy-start | bytes 1572868
  0.0 98.8 %copy-start.5 = (s32[1,1,512]{2,1,0:T(1,128)S(1)}, s32[1,1,512]{2,1,0:T(1,128)}, u32[]{:S(2)}) copy-start(s32[1,1,512]{2,1,0:T(1,128)} %param.18) | copy-start | bytes 6148
  0.0 98.6 %copy-start.6 = (f32[2,1024]{1,0:T(2,128)S(1)}, f32[2,1024]{1,0:T(2,128)}, u32[]{:S(2)}) copy-start(f32[2,1024]{1,0:T(2,128)} %param.23) | copy-start | bytes 24580
  0.0 125.2 %collective-permute-start.4 = (bf16[512,1024]{1,0:T(8,128)(2,1)}, bf16[512,1024]{1,0:T(8,128)(2,1)}, u32[]{:S(2)}, u32[]{:S(2)}) collective-permute-start(bf16[512,1024]{1,0:T(8,128)(2,1)} %bitcast.264), channel_id=1, source_target_pairs={{1,16},{3,18},{5,20},{7,22},{9,24},{11,26},{13,28},{15,30},{16,1},... | collective-permute-start | bytes 3145736 | tf_op jit(solution)/shard_map/ppermute | solution.py:25
  7.0 21.7 %collective-permute-start = (bf16[1,64,512]{2,1,0:T(8,128)(2,1)S(1)}, bf16[1,64,512]{2,1,0:T(8,128)(2,1)S(1)}, u32[]{:S(2)}, u32[]{:S(2)}) collective-permute-start(bf16[1,64,512]{2,1,0:T(8,128)(2,1)S(1)} %get-tuple-element.43), channel_id=1, source_target_pairs={{0,16},{2,18},{4,20},{6,22},{8,24},{10,26},{12,28},{14,30},{16,0},... | collective-permute-start | bytes 196616 | tf_op jit(solution)/shard_map/ppermute | solution.py:35
  28.7 29.0 %collective-permute-start.1 = (bf16[2,64,512]{2,1,0:T(8,128)(2,1)S(1)}, bf16[2,64,512]{2,1,0:T(8,128)(2,1)S(1)}, u32[]{:S(2)}, u32[]{:S(2)}) collective-permute-start(bf16[2,64,512]{2,1,0:T(8,128)(2,1)S(1)} %pad_maximum_fusion.4), channel_id=1, source_target_pairs={{0,8},{2,10},{4,12},{6,14},{8,0},{10,2},{12,4},{14,6},{16,24},{18,... | collective-permute-start | bytes 393224 | tf_op jit(solution)/shard_map/ppermute | solution.py:35
  57.8 40.9 %collective-permute-start.2 = (bf16[4,64,512]{2,1,0:T(8,128)(2,1)S(1)}, bf16[4,64,512]{2,1,0:T(8,128)(2,1)S(1)}, u32[]{:S(2)}, u32[]{:S(2)}) collective-permute-start(bf16[4,64,512]{2,1,0:T(8,128)(2,1)S(1)} %pad_maximum_fusion.2), channel_id=1, source_target_pairs={{0,4},{2,6},{4,0},{6,2},{8,12},{10,14},{12,8},{14,10},{16,20},{18,... | collective-permute-start | bytes 786440 | tf_op jit(solution)/shard_map/ppermute | solution.py:35
  98.6 14.9 %copy-start.7 = (s32[1,1,16]{2,1,0:T(1,128)S(1)}, s32[1,1,16]{2,1,0:T(1,128)}, u32[]{:S(2)}) copy-start(s32[1,1,16]{2,1,0:T(1,128)} %param.15) | copy-start | bytes 196
  98.7 2.2 %collective-permute-start.3 = (bf16[8,64,512]{2,1,0:T(8,128)(2,1)S(1)}, bf16[8,64,512]{2,1,0:T(8,128)(2,1)S(1)}, u32[]{:S(2)}, u32[]{:S(2)}) collective-permute-start(bf16[8,64,512]{2,1,0:T(8,128)(2,1)S(1)} %pad_maximum_fusion), channel_id=1, source_target_pairs={{0,2},{2,0},{4,6},{6,4},{8,10},{10,8},{12,14},{14,12},{16,18},{18,... | collective-permute-start | bytes 1572872 | tf_op jit(solution)/shard_map/ppermute | solution.py:35
  98.8 18.2 %copy-start.1 = (bf16[1,1,512,1024]{3,2,1,0:T(8,128)(2,1)S(1)}, bf16[1,1,512,1024]{3,2,1,0:T(8,128)(2,1)}, u32[]{:S(2)}) copy-start(bf16[1,1,512,1024]{3,2,1,0:T(8,128)(2,1)} %param.13) | copy-start | bytes 3145732
  98.8 18.2 %copy-start.3 = (bf16[2,64,1024]{2,1,0:T(8,128)(2,1)S(1)}, bf16[2,64,1024]{2,1,0:T(8,128)(2,1)}, u32[]{:S(2)}) copy-start(bf16[2,64,1024]{2,1,0:T(8,128)(2,1)} %param.20) | copy-start | bytes 786436
  114.0 15.4 %collective-permute-start.5 = (bf16[64,512]{0,1:T(8,128)(2,1)S(1)}, bf16[64,512]{0,1:T(8,128)(2,1)S(1)}, u32[]{:S(2)}, u32[]{:S(2)}) collective-permute-start(bf16[64,512]{0,1:T(8,128)(2,1)S(1)} %copy.17), channel_id=1, source_target_pairs={{1,16},{3,18},{5,20},{7,22},{9,24},{11,26},{13,28},{15,30},{16,1},... | collective-permute-start | bytes 196616 | tf_op jit(solution)/shard_map/ppermute | solution.py:25
  132.6 7.0 %copy-start.4 = (bf16[2,1024,64]{1,2,0:T(8,128)(2,1)S(1)}, bf16[2,1024,64]{1,2,0:T(8,128)(2,1)}, u32[]{:S(2)}) copy-start(bf16[2,1024,64]{1,2,0:T(8,128)(2,1)} %param.19) | copy-start | bytes 786436
  141.3 6.6 %collective-permute-start.6 = (bf16[1,64,512]{2,1,0:T(8,128)(2,1)S(1)}, bf16[1,64,512]{2,1,0:T(8,128)(2,1)S(1)}, u32[]{:S(2)}, u32[]{:S(2)}) collective-permute-start(bf16[1,64,512]{2,1,0:T(8,128)(2,1)S(1)} %get-tuple-element.51), channel_id=1, source_target_pairs={{0,16},{2,18},{4,20},{6,22},{8,24},{10,26},{12,28},{14,30},{16,0},... | collective-permute-start | bytes 196616 | tf_op jit(solution)/shard_map/ppermute | solution.py:35
  147.9 5.1 %collective-permute-start.7 = (bf16[2,64,512]{2,1,0:T(8,128)(2,1)S(1)}, bf16[2,64,512]{2,1,0:T(8,128)(2,1)S(1)}, u32[]{:S(2)}, u32[]{:S(2)}) collective-permute-start(bf16[2,64,512]{2,1,0:T(8,128)(2,1)S(1)} %pad_maximum_fusion.5), channel_id=1, source_target_pairs={{0,8},{2,10},{4,12},{6,14},{8,0},{10,2},{12,4},{14,6},{16,24},{18,... | collective-permute-start | bytes 393224 | tf_op jit(solution)/shard_map/ppermute | solution.py:35
  153.1 7.0 %collective-permute-start.8 = (bf16[4,64,512]{2,1,0:T(8,128)(2,1)S(1)}, bf16[4,64,512]{2,1,0:T(8,128)(2,1)S(1)}, u32[]{:S(2)}, u32[]{:S(2)}) collective-permute-start(bf16[4,64,512]{2,1,0:T(8,128)(2,1)S(1)} %pad_maximum_fusion.3), channel_id=1, source_target_pairs={{0,4},{2,6},{4,0},{6,2},{8,12},{10,14},{12,8},{14,10},{16,20},{18,... | collective-permute-start | bytes 786440 | tf_op jit(solution)/shard_map/ppermute | solution.py:35
  160.2 3.0 %copy-start.2 = (bf16[512,1024]{1,0:T(8,128)(2,1)S(1)}, bf16[512,1024]{1,0:T(8,128)(2,1)}, u32[]{:S(2)}) copy-start(bf16[512,1024]{1,0:T(8,128)(2,1)} %get-tuple-element.48) | copy-start | bytes 3145732
  160.2 2.0 %collective-permute-start.9 = (bf16[8,64,512]{2,1,0:T(8,128)(2,1)S(1)}, bf16[8,64,512]{2,1,0:T(8,128)(2,1)S(1)}, u32[]{:S(2)}, u32[]{:S(2)}) collective-permute-start(bf16[8,64,512]{2,1,0:T(8,128)(2,1)S(1)} %pad_maximum_fusion.1), channel_id=1, source_target_pairs={{0,2},{2,0},{4,6},{6,4},{8,10},{10,8},{12,14},{14,12},{16,18},{18,... | collective-permute-start | bytes 1572872 | tf_op jit(solution)/shard_map/ppermute | solution.py:35
  165.1 12.1 %collective-permute-start.10 = (bf16[64,512]{0,1:T(8,128)(2,1)S(1)}, bf16[64,512]{0,1:T(8,128)(2,1)S(1)}, u32[]{:S(2)}, u32[]{:S(2)}) collective-permute-start(bf16[64,512]{0,1:T(8,128)(2,1)S(1)} %copy.19), channel_id=1, source_target_pairs={{1,16},{3,18},{5,20},{7,22},{9,24},{11,26},{13,28},{15,30},{16,1},... | collective-permute-start | bytes 196616 | tf_op jit(solution)/shard_map/ppermute | solution.py:25

commit v2 on v1

v2 whole, which is shorter than its diff:
```python
import functools

import jax
import jax.numpy as jnp
from jax import lax
from jax.experimental import pallas as pl
from jax.experimental.pallas import tpu as pltpu
from jax.sharding import PartitionSpec as P

BLK = 128
LAYERS = 2
ROWS = 256
EXCHANGE_BITS = 2
VMEM_LIMIT = 24 * 2**20
F32 = jnp.float32
BF16 = jnp.bfloat16


def dot(x, y):
    return jnp.dot(x, y, preferred_element_type=F32)


def dot_nt(x, y):
    return lax.dot_general(x, y, (((1,), (1,)), ((), ())), preferred_element_type=F32)


def reversed_bits(value, bits):
    return sum((value >> i & 1) << bits - 1 - i for i in range(bits))


def hop(values, bit):
    size = lax.axis_size("src")
    return lax.ppermute(values, "src", [(i, i ^ bit) for i in range(size)])


def mirror_pairs():
    groups = lax.axis_size("tgt")
    copies = lax.axis_size("src") // groups
    pairs = []
    for p in range(groups * copies):
        a, r = divmod(p, copies)
        for q in range(groups):
            if a != q:
                pairs.append((p * groups + q, (q * copies + r) * groups + a))
    return pairs


def to_mirror(values):
    return lax.ppermute(values, ("src", "tgt"), mirror_pairs())


def call(body, name, outs, scalars, arrays, scratch=(), flops=0, moved=0):
    smem = pl.BlockSpec(memory_space=pltpu.SMEM)
    vmem = pl.BlockSpec(memory_space=pltpu.VMEM)
    return pl.pallas_call(
        body,
        in_specs=[smem] * len(scalars) + [vmem] * len(arrays),
        out_specs=[vmem] * len(outs),
        scratch_shapes=list(scratch),
        out_shape=list(outs),
        name=name,
        compiler_params=pltpu.CompilerParams(vmem_limit_bytes=VMEM_LIMIT),
        cost_estimate=pl.CostEstimate(flops=flops, bytes_accessed=moved, transcendentals=0),
    )(*scalars, *arrays)


def reverse_column(reverse_row):
    return jnp.broadcast_to(reverse_row[...], (8, reverse_row.shape[1])).T[:, :1]


def own_mirror():
    copies = lax.axis_size("src") // lax.axis_size("tgt")
    return lax.axis_index("src") // copies == lax.axis_index("tgt")


def like(shape, dtype):
    return jax.ShapeDtypeStruct(shape, dtype)


def project_body(w_proj_t, state, out):
    out[...] = dot_nt(w_proj_t[0], state[...]).astype(BF16)


def project(w_proj_t, state):
    shape = (w_proj_t.shape[1], state.shape[0])
    return call(
        project_body,
        "project",
        [like(shape, BF16)],
        [],
        [w_proj_t, state],
        flops=2 * state.size * shape[0],
        moved=2 * state.size,
    )[0]


def triplet_body(low_bits, slots, blocks, index, pool, coeffs, kept, sent, acc):
    acc[...] = jnp.zeros_like(acc)
    mine = lax.axis_index("src")
    low_mask = (1 << low_bits) - 1
    for tile in range(1 << low_bits):
        at = reversed_bits(tile, low_bits)

        def one(slot, carry):
            source = index[at, slots + slot]
            relative = (source // blocks) ^ mine

            @pl.when((relative & low_mask) == 0)
            def _():
                held_tile = jnp.int32(0)
                high = pool.shape[0]
                place, bit = 1, (high // 2) << low_bits
                while place < high:
                    held_tile = held_tile + jnp.where((relative & bit) != 0, place, 0)
                    place, bit = place * 2, bit // 2
                start = pl.multiple_of((source % blocks) * BLK, BLK)
                picked = pool[held_tile, :, pl.ds(start, BLK)]
                product = dot(picked, coeffs[at, slot])
                place_at = pl.multiple_of(index[at, slot] * BLK, BLK)
                acc[tile, :, pl.ds(place_at, BLK)] += product

            return carry

        lax.fori_loop(0, jnp.minimum(index[at, 2 * slots], slots), one, 0)
    half = acc.shape[0] // 2
    kept[...] = acc[:half]
    sent[...] = acc[half:].astype(BF16)


def triplet_partials(index, pool, coeffs):
    tiles, slots = coeffs.shape[:2]
    width, edges = pool.shape[1:]
    body = functools.partial(triplet_body, tiles.bit_length() - 1, slots, edges // BLK)
    return call(
        body,
        "triplets",
        [
            like((tiles // 2, width, edges), F32),
            like((tiles // 2, width, edges), BF16),
        ],
        [index],
        [pool, coeffs],
        scratch=[pltpu.VMEM((tiles, width, edges), F32)],
        flops=2 * coeffs.size * width,
        moved=2 * coeffs.size,
    )


def branch_of(x, agg, w_up, w_in, w_out, gain):
    summed = x.astype(F32) + dot(agg, w_up[...])
    scale_inv = lax.rsqrt(jnp.mean(summed * summed, axis=-1, keepdims=True) + 1e-06)
    normed = (gain[...] * summed * scale_inv).astype(BF16)
    u = dot(normed, w_in[...])
    activated = (u / (1.0 + jnp.exp(-u))).astype(BF16)
    return summed, dot(activated, w_out[...]).astype(BF16)


def chunks(edges):
    step = min(ROWS, edges)
    return [pl.ds(i, step) for i in range(0, edges, step)]


def weights_of(layer_index, w_up, w_in, w_out, gain):
    return [w.at[layer_index] for w in (w_up, w_in, w_out)] + [gain.at[pl.ds(layer_index, 1)]]


def one_hot(column):
    lanes = lax.broadcasted_iota(jnp.int32, (column.shape[0], column.shape[0]), 1)
    return (column == lanes).astype(BF16)


def picking(column, rows, edges):
    lanes = lax.broadcasted_iota(jnp.int32, (rows.size, edges), 1)
    return (column[rows.start : rows.start + rows.size] == lanes).astype(BF16)


def first_body(w_up, w_in, w_out, gain, w_proj_t, state, agg_t, reverse, total, branch, v_t, u_t):
    weights = weights_of(0, w_up, w_in, w_out, gain)
    agg = agg_t[...].astype(F32).T.astype(BF16)
    w_next = w_proj_t[1]
    for rows in chunks(state.shape[0]):
        summed, out = branch_of(state[rows, :], agg[rows.start : rows.start + rows.size], *weights)
        branch[rows, :] = out
        moved = summed + out.astype(F32)
        total[rows, :] = moved
        v_t[:, rows] = dot_nt(w_next, moved.astype(BF16)).astype(BF16)
    u = dot_nt(w_next, branch[...]).astype(BF16)
    u_t[...] = dot(u, one_hot(reverse_column(reverse))).astype(BF16)


def second_body(
    w_up, w_in, w_out, gain, own, other_low, other_high, agg_t, agg_other, reverse, total, branch, state, mirrored
):
    edges = total.shape[0]
    weights = weights_of(0, w_up, w_in, w_out, gain)
    here = own_mirror()
    other = jnp.concatenate([other_low[...], other_high[...]], axis=0)
    source = jnp.where(here, own[...], other)
    low = jnp.where(here, agg_t[...], agg_other[...])
    column = reverse_column(reverse)
    for rows in chunks(edges):
        pick = picking(column, rows, edges)
        summed, out = branch_of(dot(pick, source), dot_nt(pick, low).astype(BF16), *weights)
        state[rows, :] = (total[rows, :] + out.astype(F32)).astype(BF16)
        mirrored[rows, :] = (summed + out.astype(F32) + branch[rows, :].astype(F32)).astype(BF16)


def third_body(w_up, w_in, w_out, gain, state, agg_t, total):
    weights = weights_of(1, w_up, w_in, w_out, gain)
    agg = agg_t[...].astype(F32).T.astype(BF16)
    for rows in chunks(state.shape[0]):
        summed, out = branch_of(state[rows, :], agg[rows.start : rows.start + rows.size], *weights)
        total[rows, :] = summed + out.astype(F32)


def last_body(w_up, w_in, w_out, gain, mirrored, agg_t, agg_other, reverse, total, state):
    edges = total.shape[0]
    weights = weights_of(1, w_up, w_in, w_out, gain)
    low = jnp.where(own_mirror(), agg_t[...], agg_other[...])
    column = reverse_column(reverse)
    for rows in chunks(edges):
        agg = dot_nt(picking(column, rows, edges), low).astype(BF16)
        summed, out = branch_of(mirrored[rows, :], agg, *weights)
        state[rows, :] = (total[rows, :] + out.astype(F32)).astype(BF16)


def gather_step(held, bit):
    return jnp.concatenate([held, hop(held, bit)], axis=0)


def gather_low(values):
    held = values[None]
    for bit in reversed(range(EXCHANGE_BITS)):
        held = gather_step(held, 1 << bit)
    return held


def second_route_x(values):
    groups, size = lax.axis_size("tgt"), lax.axis_size("src")
    if groups != 2:
        return values
    copies = size // groups
    pairs = [
        ((a * copies + r) * 2 + 1 - a, (a * copies + r) * 2 + a)
        for a in range(2)
        for r in range(copies)
    ]
    return lax.ppermute(values, ("src", "tgt"), pairs)


def second_route_z(turned, values):
    groups, size = lax.axis_size("tgt"), lax.axis_size("src")
    if groups != 2:
        return to_mirror(values)
    copies = size // groups
    pairs = [
        ((a * copies + r) * 2 + a, ((1 - a) * copies + r) * 2 + a)
        for a in range(2)
        for r in range(copies)
    ]
    return lax.ppermute(turned, ("src", "tgt"), pairs)


def gather_high(projected):
    size = lax.axis_size("src")
    held = projected[None]
    bit = size // 2
    while bit >= 1 << EXCHANGE_BITS:
        held = jnp.concatenate([held, hop(held, bit)], axis=0)
        bit //= 2
    return held


def exchange_sums(kept, sent):
    bit = 1 << (EXCHANGE_BITS - 1)
    while True:
        summed = kept + hop(sent, bit).astype(F32)
        half = summed.shape[0] // 2
        if half == 0:
            return summed[0].astype(BF16)
        kept, sent = summed[:half], summed[half:].astype(BF16)
        bit //= 2


def local(
    edge_states,
    triplet_coeff,
    block_target,
    block_source,
    block_count,
    reverse_slot,
    w_proj,
    w_up,
    w_in,
    w_out,
    norm_gain,
):
    state0 = edge_states[0, 0]
    edges, features = state0.shape
    width = w_proj.shape[2]
    reverse = reverse_slot[0]
    w_proj_t = jnp.swapaxes(w_proj, 1, 2)
    weights = [w_up, w_in, w_out, norm_gain]

    proj0 = project(w_proj_t, state0)
    own_index = jnp.concatenate([block_target[0, 0], block_source[0, 0], block_count[0]])
    own_coeffs, own_index, held_state, proj0 = lax.optimization_barrier(
        (triplet_coeff[0, 0], own_index, state0, proj0)
    )
    index = gather_low(own_index)
    half = edges // 2
    turned = second_route_x(held_state[half:])
    coeffs_y = gather_step(own_coeffs[None], 1 << (EXCHANGE_BITS - 1))
    pool = gather_high(proj0)
    coeffs_y, held_state, turned, pool = lax.optimization_barrier(
        (coeffs_y, held_state, turned, pool)
    )
    coeffs = gather_step(coeffs_y, 1)
    other_low = to_mirror(held_state[:half])
    other_high = second_route_z(turned, held_state[half:])
    kept, sent = triplet_partials(index, pool, coeffs)
    agg0 = exchange_sums(kept, sent)
    work = 4 * edges * features * features
    total0, branch0, v_t, u_t = call(
        first_body,
        "first",
        [
            like((edges, features), F32),
            like((edges, features), BF16),
            like((width, edges), BF16),
            like((width, edges), BF16),
        ],
        [],
        weights + [w_proj_t, state0, agg0, reverse],
        flops=work,
        moved=8 * 2**20,
    )
    u_t, other_low, other_high = lax.optimization_barrier((u_t, other_low, other_high))
    u_other = to_mirror(u_t)
    agg0_other = to_mirror(agg0)
    mirrored_u = jnp.where(own_mirror(), u_t, u_other)
    proj1 = (v_t.astype(F32) + mirrored_u.astype(F32)).astype(BF16)
    pool1 = gather_high(proj1)
    kept, sent = triplet_partials(index, pool1, coeffs)
    agg1 = exchange_sums(kept, sent)
    agg1_other = to_mirror(agg1)
    state1, mirrored1 = call(
        second_body,
        "second",
        [like((edges, features), BF16), like((edges, features), BF16)],
        [],
        weights + [state0, other_low, other_high, agg0, agg0_other, reverse, total0, branch0],
        flops=work + 2 * edges * edges * features,
        moved=10 * 2**20,
    )
    total1 = call(
        third_body,
        "third",
        [like((edges, features), F32)],
        [],
        weights + [state1, agg1],
        flops=work,
        moved=8 * 2**20,
    )[0]
    final = call(
        last_body,
        "last",
        [like((edges, features), BF16)],
        [],
        weights + [mirrored1, agg1, agg1_other, reverse, total1],
        flops=work,
        moved=8 * 2**20,
    )[0]
    return final[None, None]


def solution(mesh):
    return jax.shard_map(
        local,
        mesh=mesh,
        in_specs=(
            P("src", "tgt", None, None),
            P("src", "tgt", None, None, None),
            P("src", "tgt", None),
            P("src", "tgt", None),
            P("src", "tgt"),
            P("src", "tgt", None),
            P(),
            P(),
            P(),
            P(),
            P(),
        ),
        out_specs=P("src", "tgt", None, None),
        check_vma=False,
    )
```

time: 193 us -> 118 us (0.61)
  matrix products: 41.1 us -> 0 us
  between operations: 41.3 us -> 1.01 us
  Pallas kernels: 0 us -> 21 us
  starting transfers between devices: 41 us -> 24.6 us
  waiting for transfers between devices: 40.1 us -> 53.4 us
  local copies, waits for them, and re-layouts: 22 us -> 13.6 us
    dot_general x14 -> x0, matrix products: 41.1 us -> none  [the longest x4 27.1 us: transform(): jnp.dot(activated, w_out_l, preferred_element_type=jnp.float32)]
    pallas_call x0 -> x7, Pallas kernels: none -> 21 us  [call(): pl.pallas_call(body, in_specs=[smem] * len(scalars) + [vmem] * len(arrays...]
    ppermute x11 -> x18, starting transfers between devices: 41 us -> 24.6 us  [the longest x4 11.5 us: to_mirror(): return lax.ppermute(values, ('src', 'tgt'), mirror_pairs())]
    ppermute x11 -> x18, waiting for transfers between devices: 40.1 us -> 53.4 us  [the longest x4 26.8 us: to_mirror(): return lax.ppermute(values, ('src', 'tgt'), mirror_pairs())]
    gather x3 -> x0, local copies, waits for them, and re-layouts: 5.46 us -> none  [the longest x1 2.78 us: local(): mirrored = jnp.take(mirror_tile(state), reverse_rows, axis=0)]
    select_n x6 -> x0, other arithmetic: 3.41 us -> none  [the longest x2 1.37 us: local(): mirrored = jnp.take(mirror_tile(state), reverse_rows, axis=0)]
    unnamed x54 -> x41, local copies, waits for them, and re-layouts: 13.3 us -> 13.3 us
  transfers between devices with their start and end apart: 11 -> 18, of which waited for: 6 -> 15; matrix products, arithmetic and copies ran while one was open for 21% -> 0% of each run, Pallas kernels for 0% -> 11%
where the time goes in v2:
time: 118 us; the launch traced here: 116 us
  waiting for transfers between devices  53.4 us (45%)
  starting transfers between devices  24.6 us (21%)
  Pallas kernels  21 us (18%)
  local copies, waits for them, and re-layouts  13.6 us (12%)
  other arithmetic  2.08 us (2%)
    ppermute x4, waiting for transfers between devices, to_mirror(): return lax.ppermute(values, ('src', 'tgt'), mirror_pairs())  26.8 us
    ppermute x12, waiting for transfers between devices, hop(): return lax.ppermute(values, 'src', [(i, i ^ bit) for i in range(size)])  22.5 us
    pallas_call x7, Pallas kernels, call(): pl.pallas_call(body, in_specs=[smem] * len(scalars) + [vmem] * len(arrays...  21 us
    unnamed x41, local copies, waits for them, and re-layouts  13.3 us
    ppermute x4, starting transfers between devices, to_mirror(): return lax.ppermute(values, ('src', 'tgt'), mirror_pairs())  11.5 us
    ppermute x12, starting transfers between devices, hop(): return lax.ppermute(values, 'src', [(i, i ^ bit) for i in range(size)])  9.39 us
    ppermute x1, starting transfers between devices, second_route_x(): return lax.ppermute(values, ('src', 'tgt'), pairs)  2.47 us
  transfers between devices with their start and end apart: 18, of which 15 were waited for; matrix products, arithmetic and copies ran while one was open for 0% of the time, Pallas kernels for 11%

profile of v2, /device:TPU:6, one launch (start us, length us, event | category | flops | bytes accessed | tf_op | source)
XLA Modules:
  0.0 115.6 jit_solution(7966551151643784874)
XLA Ops:
  0.7 1.2 %copy-done.4 = bf16[1,1,512,1024]{3,2,1,0:T(8,128)(2,1)S(1)} copy-done((bf16[1,1,512,1024]{3,2,1,0:T(8,128)(2,1)S(1)}, bf16[1,1,512,1024]{3,2,1,0:T(8,128)(2,1)}, u32[]{:S(2)}) %copy-start.4) | copy-done | bytes 1048600
  1.9 0.9 copy-done.9
  2.8 0.4 project.1
  3.3 0.8 pad_add_fusion.2
  4.0 0.5 collective-permute-start.2
  4.5 2.6 %collective-permute-start.4 = (bf16[1,64,512]{2,1,0:T(8,128)(2,1)S(1)}, bf16[1,64,512]{2,1,0:T(8,128)(2,1)S(1)}, u32[]{:S(2)}, u32[]{:S(2)}) collective-permute-start(bf16[1,64,512]{2,1,0:T(8,128)(2,1)S(1)} %bitcast.25), channel_id=1, source_target_pairs={{0,16},{2,18},{4,20},{6,22},{8,24},{10,26},{12,28},{14,30},{16,0},... | collective-permute-start | bytes 196616 | tf_op jit(solution)/shard_map/ppermute | solution.py:33
  7.2 2.5 %collective-permute-start.3 = (bf16[256,1024]{1,0:T(8,128)(2,1)S(1)}, bf16[256,1024]{1,0:T(8,128)(2,1)S(1)}, u32[]{:S(2)}, u32[]{:S(2)}) collective-permute-start(bf16[256,1024]{1,0:T(8,128)(2,1)S(1)} %slice.20), channel_id=1, source_target_pairs={{1,0},{3,2},{5,4},{7,6},{9,8},{11,10},{13,12},{15,14},{16,17},{18,... | collective-permute-start | bytes 1572872 | tf_op jit(solution)/shard_map/ppermute | solution.py:248
  9.6 0.4 collective-permute-done.4
  10.0 1.3 %collective-permute-start.5 = (bf16[2,64,512]{2,1,0:T(8,128)(2,1)S(1)}, bf16[2,64,512]{2,1,0:T(8,128)(2,1)S(1)}, u32[]{:S(2)}, u32[]{:S(2)}) collective-permute-start(bf16[2,64,512]{2,1,0:T(8,128)(2,1)S(1)} %pad_maximum_fusion.3), channel_id=1, source_target_pairs={{0,8},{2,10},{4,12},{6,14},{8,0},{10,2},{12,4},{14,6},{16,24},{18,... | collective-permute-start | bytes 393224 | tf_op jit(solution)/shard_map/ppermute | solution.py:33
  11.4 3.7 %collective-permute-done.5 = bf16[2,64,512]{2,1,0:T(8,128)(2,1)S(1)} collective-permute-done((bf16[2,64,512]{2,1,0:T(8,128)(2,1)S(1)}, bf16[2,64,512]{2,1,0:T(8,128)(2,1)S(1)}, u32[]{:S(2)}, u32[]{:S(2)}) %collective-permute-start.5) | collective-permute-done | bytes 131104 | tf_op jit(solution)/shard_map/ppermute | solution.py:33
  15.1 2.8 %collective-permute-done.2 = bf16[1,16,128,128]{3,2,1,0:T(8,128)(2,1)S(1)} collective-permute-done((bf16[1,16,128,128]{3,2,1,0:T(8,128)(2,1)}, bf16[1,16,128,128]{3,2,1,0:T(8,128)(2,1)S(1)}, u32[]{:S(2)}, u32[]{:S(2)}) %collective-permute-start.2) | collective-permute-done | bytes 524320 | tf_op jit(solution)/shard_map/ppermute | solution.py:33
  18.0 2.2 %collective-permute-done.3 = bf16[256,1024]{1,0:T(8,128)(2,1)S(1)} collective-permute-done((bf16[256,1024]{1,0:T(8,128)(2,1)S(1)}, bf16[256,1024]{1,0:T(8,128)(2,1)S(1)}, u32[]{:S(2)}, u32[]{:S(2)}) %collective-permute-start.3) | collective-permute-done | bytes 524320 | tf_op jit(solution)/shard_map/ppermute | solution.py:248
  20.2 1.5 %collective-permute-start = (s32[1,33]{1,0:T(1,128)S(1)}, s32[1,33]{1,0:T(1,128)S(1)}, u32[]{:S(2)}, u32[]{:S(2)}) collective-permute-start(s32[1,33]{1,0:T(1,128)S(1)} %bitcast.33), channel_id=1, source_target_pairs={{0,4},{2,6},{4,0},{6,2},{8,12},{10,14},{12,8},{14,10},{16,20},{18,... | collective-permute-start | bytes 404 | tf_op jit(solution)/shard_map/ppermute | solution.py:33
  21.7 2.0 %collective-permute-done = s32[1,33]{1,0:T(1,128)S(1)} collective-permute-done((s32[1,33]{1,0:T(1,128)S(1)}, s32[1,33]{1,0:T(1,128)S(1)}, u32[]{:S(2)}, u32[]{:S(2)}) %collective-permute-start) | collective-permute-done | bytes 164 | tf_op jit(solution)/shard_map/ppermute | solution.py:33
  23.8 1.1 collective-permute-done.1
  25.1 0.2 constant_dynamic-update-slice_fusion.coeffs
  25.3 1.4 %triplets.2 = (f32[2,64,512]{2,1,0:T(8,128)S(1)}, bf16[2,64,512]{2,1,0:T(8,128)(2,1)S(1)}) custom-call(s32[4,33]{1,0:T(4,128)S(1)} %pad_add_fusion.index, bf16[4,64,512]{2,1,0:T(8,128)(2,1)S(1)} %pad_maximum_fusion.1.pool, bf16[4,16,128,128]{3,2,1,0:T(8,128)(2,1)S(1)} %constant_dynamic-update-slice_fusion.coeffs), custom_call_target="tpu_custom_call" | custom-call | flops 134217728 | bytes 2097152 | tf_op jit(solution)/shard_map/triplets/pallas_call | solution.py:55
  26.7 2.1 %collective-permute-start.7 = (bf16[2,64,512]{2,1,0:T(8,128)(2,1)S(1)}, bf16[2,64,512]{2,1,0:T(8,128)(2,1)S(1)}, u32[]{:S(2)}, u32[]{:S(2)}) collective-permute-start(bf16[2,64,512]{2,1,0:T(8,128)(2,1)S(1)} %get-tuple-element.33), channel_id=1, source_target_pairs={{0,4},{2,6},{4,0},{6,2},{8,12},{10,14},{12,8},{14,10},{16,20},{18,... | collective-permute-start | bytes 393224 | tf_op jit(solution)/shard_map/ppermute | solution.py:33
  28.8 3.3 %collective-permute-start.9 = (bf16[256,1024]{1,0:T(8,128)(2,1)S(1)}, bf16[256,1024]{1,0:T(8,128)(2,1)S(1)}, u32[]{:S(2)}, u32[]{:S(2)}) collective-permute-start(bf16[256,1024]{1,0:T(8,128)(2,1)S(1)} %slice.23), channel_id=1, source_target_pairs={{1,16},{3,18},{5,20},{7,22},{9,24},{11,26},{13,28},{15,30},{16,1},... | collective-permute-start | bytes 1572872 | tf_op jit(solution)/shard_map/ppermute | solution.py:49
  32.1 1.3 %collective-permute-start.10 = (bf16[256,1024]{1,0:T(8,128)(2,1)S(1)}, bf16[256,1024]{1,0:T(8,128)(2,1)S(1)}, u32[]{:S(2)}, u32[]{:S(2)}) collective-permute-start(bf16[256,1024]{1,0:T(8,128)(2,1)S(1)} %collective-permute-done.3), channel_id=1, source_target_pairs={{0,16},{2,18},{4,20},{6,22},{8,24},{10,26},{12,28},{14,30},{17,1},... | collective-permute-start | bytes 1572872 | tf_op jit(solution)/shard_map/ppermute | solution.py:261
  33.6 1.2 %collective-permute-done.8 = bf16[1,64,512]{2,1,0:T(8,128)(2,1)S(1)} collective-permute-done((bf16[1,64,512]{2,1,0:T(8,128)(2,1)S(1)}, bf16[1,64,512]{2,1,0:T(8,128)(2,1)S(1)}, u32[]{:S(2)}, u32[]{:S(2)}) %collective-permute-start.8) | collective-permute-done | bytes 65568 | tf_op jit(solution)/shard_map/ppermute | solution.py:33
  34.9 4.9 %first.1 = (f32[512,1024]{1,0:T(8,128)S(1)}, bf16[512,1024]{1,0:T(8,128)(2,1)S(1)}, bf16[64,512]{1,0:T(8,128)(2,1)S(1)}, bf16[64,512]{1,0:T(8,128)(2,1)}) custom-call(bf16[2,64,1024]{2,1,0:T(8,128)(2,1)S(1)} %copy-done.6, bf16[2,1024,1024]{2,1,0:T(8,128)(2,1)S(1)} %copy-done, bf16[2,1024,1024]{2,1,0:T(8,128)(2,1)S(1)} %copy-done.2, ...), custom_call_target="tpu_custom_call" | custom-call | flops 2147483648 | bytes 8388608 | tf_op jit(solution)/shard_map/first/pallas_call | solution.py:55
  39.7 1.4 %copy-done.7 = f32[512,1024]{1,0:T(8,128)} copy-done((f32[512,1024]{1,0:T(8,128)}, f32[512,1024]{1,0:T(8,128)S(1)}, u32[]{:S(2)}) %copy-start.7) | copy-done | bytes 2097176
  41.1 1.0 copy-done.11
  42.1 14.8 %collective-permute-done.9.other_low = bf16[256,1024]{1,0:T(8,128)(2,1)S(1)} collective-permute-done((bf16[256,1024]{1,0:T(8,128)(2,1)S(1)}, bf16[256,1024]{1,0:T(8,128)(2,1)S(1)}, u32[]{:S(2)}, u32[]{:S(2)}) %collective-permute-start.9) | collective-permute-done | bytes 524320 | tf_op jit(solution)/shard_map/ppermute | solution.py:49
  56.9 0.8 copy-done.13
  57.7 1.9 %collective-permute-done.10.other_high = bf16[256,1024]{1,0:T(8,128)(2,1)S(1)} collective-permute-done((bf16[256,1024]{1,0:T(8,128)(2,1)S(1)}, bf16[256,1024]{1,0:T(8,128)(2,1)S(1)}, u32[]{:S(2)}, u32[]{:S(2)}) %collective-permute-start.10) | collective-permute-done | bytes 524320 | tf_op jit(solution)/shard_map/ppermute | solution.py:261
  59.6 0.8 copy-done.15
  60.3 1.9 %collective-permute-start.12 = (bf16[64,512]{1,0:T(8,128)(2,1)}, bf16[64,512]{1,0:T(8,128)(2,1)}, u32[]{:S(2)}, u32[]{:S(2)}) collective-permute-start(bf16[64,512]{1,0:T(8,128)(2,1)} %get-tuple-element.43), channel_id=1, source_target_pairs={{1,16},{3,18},{5,20},{7,22},{9,24},{11,26},{13,28},{15,30},{16,1},... | collective-permute-start | bytes 196616 | tf_op jit(solution)/shard_map/ppermute | solution.py:49
  62.3 6.8 %collective-permute-done.12 = bf16[64,512]{1,0:T(8,128)(2,1)} collective-permute-done((bf16[64,512]{1,0:T(8,128)(2,1)}, bf16[64,512]{1,0:T(8,128)(2,1)}, u32[]{:S(2)}, u32[]{:S(2)}) %collective-permute-start.12) | collective-permute-done | bytes 65568 | tf_op jit(solution)/shard_map/ppermute | solution.py:49
  69.0 1.0 fusion.2
  70.1 5.2 %collective-permute-done.13 = bf16[1,64,512]{2,1,0:T(8,128)(2,1)S(1)} collective-permute-done((bf16[1,64,512]{2,1,0:T(8,128)(2,1)S(1)}, bf16[1,64,512]{2,1,0:T(8,128)(2,1)S(1)}, u32[]{:S(2)}, u32[]{:S(2)}) %collective-permute-start.13) | collective-permute-done | bytes 65568 | tf_op jit(solution)/shard_map/ppermute | solution.py:33
  75.5 5.0 %collective-permute-done.14 = bf16[2,64,512]{2,1,0:T(8,128)(2,1)S(1)} collective-permute-done((bf16[2,64,512]{2,1,0:T(8,128)(2,1)S(1)}, bf16[2,64,512]{2,1,0:T(8,128)(2,1)S(1)}, u32[]{:S(2)}, u32[]{:S(2)}) %collective-permute-start.14) | collective-permute-done | bytes 131104 | tf_op jit(solution)/shard_map/ppermute | solution.py:33
  80.5 1.4 %triplets.3 = (f32[2,64,512]{2,1,0:T(8,128)S(1)}, bf16[2,64,512]{2,1,0:T(8,128)(2,1)S(1)}) custom-call(s32[4,33]{1,0:T(4,128)S(1)} %pad_add_fusion.index, bf16[4,64,512]{2,1,0:T(8,128)(2,1)S(1)} %pad_maximum_fusion.2.pool, bf16[4,16,128,128]{3,2,1,0:T(8,128)(2,1)S(1)} %constant_dynamic-update-slice_fusion.coeffs), custom_call_target="tpu_custom_call" | custom-call | flops 134217728 | bytes 2097152 | tf_op jit(solution)/shard_map/triplets/pallas_call | solution.py:55
  81.8 1.0 collective-permute-start.15
  82.8 3.0 %collective-permute-start.11 = (bf16[64,512]{1,0:T(8,128)(2,1)S(1)}, bf16[64,512]{1,0:T(8,128)(2,1)S(1)}, u32[]{:S(2)}, u32[]{:S(2)}) collective-permute-start(bf16[64,512]{1,0:T(8,128)(2,1)S(1)} %fusion.3.agg_t), channel_id=1, source_target_pairs={{1,16},{3,18},{5,20},{7,22},{9,24},{11,26},{13,28},{15,30},{16,1},... | collective-permute-start | bytes 196616 | tf_op jit(solution)/shard_map/ppermute | solution.py:49
  85.8 1.1 collective-permute-done.15
  87.0 3.7 %collective-permute-done.11.agg_other = bf16[64,512]{1,0:T(8,128)(2,1)S(1)} collective-permute-done((bf16[64,512]{1,0:T(8,128)(2,1)S(1)}, bf16[64,512]{1,0:T(8,128)(2,1)S(1)}, u32[]{:S(2)}, u32[]{:S(2)}) %collective-permute-start.11) | collective-permute-done | bytes 65568 | tf_op jit(solution)/shard_map/ppermute | solution.py:49
  90.8 2.2 %copy-done.3 = bf16[2,1024,1024]{2,1,0:T(8,128)(2,1)S(1)} copy-done((bf16[2,1024,1024]{2,1,0:T(8,128)(2,1)S(1)}, bf16[2,1024,1024]{2,1,0:T(8,128)(2,1)}, u32[]{:S(2)}) %copy-start.3) | copy-done | bytes 4194328
  93.0 1.6 %copy-done.8 = f32[512,1024]{1,0:T(8,128)S(1)} copy-done((f32[512,1024]{1,0:T(8,128)S(1)}, f32[512,1024]{1,0:T(8,128)}, u32[]{:S(2)}) %copy-start.8) | copy-done | bytes 2097176
  94.5 1.2 %copy-done.12 = bf16[512,1024]{1,0:T(8,128)(2,1)S(1)} copy-done((bf16[512,1024]{1,0:T(8,128)(2,1)S(1)}, bf16[512,1024]{1,0:T(8,128)(2,1)}, u32[]{:S(2)}) %copy-start.12) | copy-done | bytes 1048600
  95.8 1.0 copy-done.14
  96.8 1.0 copy-done.16
  97.9 4.9 %second.1 = (bf16[512,1024]{1,0:T(8,128)(2,1)S(1)}, bf16[512,1024]{1,0:T(8,128)(2,1)S(1)}) custom-call(bf16[2,64,1024]{2,1,0:T(8,128)(2,1)S(1)} %copy-done.6, bf16[2,1024,1024]{2,1,0:T(8,128)(2,1)S(1)} %copy-done.1, bf16[2,1024,1024]{2,1,0:T(8,128)(2,1)S(1)} %copy-done.3, f32[2,1024]{1,0:T(2,128)S(1)} %copy-done.17, bf16[512,1024]{1,0:T(8,128)(2,1)S(1)} %bitcast.22, ...), custom_call_target="tpu_custom_call" | custom-call | flops 2684354560 | bytes 10485760 | tf_op jit(solution)/shard_map/second/pallas_call | solution.py:55
  102.8 3.3 %collective-permute-start.17 = (bf16[64,512]{1,0:T(8,128)(2,1)S(1)}, bf16[64,512]{1,0:T(8,128)(2,1)S(1)}, u32[]{:S(2)}, u32[]{:S(2)}) collective-permute-start(bf16[64,512]{1,0:T(8,128)(2,1)S(1)} %fusion.4.agg_t), channel_id=1, source_target_pairs={{1,16},{3,18},{5,20},{7,22},{9,24},{11,26},{13,28},{15,30},{16,1},... | collective-permute-start | bytes 196616 | tf_op jit(solution)/shard_map/ppermute | solution.py:49
  106.1 3.1 %third.1.total = f32[512,1024]{1,0:T(8,128)S(1)} custom-call(bf16[2,64,1024]{2,1,0:T(8,128)(2,1)S(1)} %copy-done.6, bf16[2,1024,1024]{2,1,0:T(8,128)(2,1)S(1)} %copy-done.1, bf16[2,1024,1024]{2,1,0:T(8,128)(2,1)S(1)} %copy-done.3, f32[2,1024]{1,0:T(2,128)S(1)} %copy-done.17, bf16[512,1024]{1,0:T(8,128)(2,1)S(1)} %get-tuple-element.46.state, ...), custom_call_target="tpu_custom_call" | custom-call | flops 2147483648 | bytes 8388608 | tf_op jit(solution)/shard_map/third/pallas_call | solution.py:55
  109.3 1.5 %collective-permute-done.17.agg_other = bf16[64,512]{1,0:T(8,128)(2,1)S(1)} collective-permute-done((bf16[64,512]{1,0:T(8,128)(2,1)S(1)}, bf16[64,512]{1,0:T(8,128)(2,1)S(1)}, u32[]{:S(2)}, u32[]{:S(2)}) %collective-permute-start.17) | collective-permute-done | bytes 65568 | tf_op jit(solution)/shard_map/ppermute | solution.py:49
  110.8 4.8 %last.1 = bf16[512,1024]{1,0:T(8,128)(2,1)} custom-call(bf16[2,64,1024]{2,1,0:T(8,128)(2,1)S(1)} %copy-done.6, bf16[2,1024,1024]{2,1,0:T(8,128)(2,1)S(1)} %copy-done.1, bf16[2,1024,1024]{2,1,0:T(8,128)(2,1)S(1)} %copy-done.3, f32[2,1024]{1,0:T(2,128)S(1)} %copy-done.17, bf16[512,1024]{1,0:T(8,128)(2,1)S(1)} %get-tuple-element.41.mirrored, ...), custom_call_target="tpu_custom_call" | custom-call | flops 2147483648 | bytes 8388608 | tf_op jit(solution)/shard_map/last/pallas_call | solution.py:55
  (54 shorter events, 0.9 us)
Async XLA Ops:
  0.7 1.2 %copy-start.4 = (bf16[1,1,512,1024]{3,2,1,0:T(8,128)(2,1)S(1)}, bf16[1,1,512,1024]{3,2,1,0:T(8,128)(2,1)}, u32[]{:S(2)}) copy-start(bf16[1,1,512,1024]{3,2,1,0:T(8,128)(2,1)} %param.11) | copy-start | bytes 3145732
  1.9 0.9 copy-start.9
  2.8 15.1 %copy-start.19 = (bf16[1,1,16,128,128]{4,3,2,1,0:T(8,128)(2,1)S(1)}, bf16[1,1,16,128,128]{4,3,2,1,0:T(8,128)(2,1)}, u32[]{:S(2)}) copy-start(bf16[1,1,16,128,128]{4,3,2,1,0:T(8,128)(2,1)} %param.12) | copy-start | bytes 1572868
  4.0 13.9 %collective-permute-start.2 = (bf16[1,16,128,128]{3,2,1,0:T(8,128)(2,1)}, bf16[1,16,128,128]{3,2,1,0:T(8,128)(2,1)S(1)}, u32[]{:S(2)}, u32[]{:S(2)}) collective-permute-start(bf16[1,16,128,128]{3,2,1,0:T(8,128)(2,1)} %bitcast.31), channel_id=1, source_target_pairs={{0,4},{2,6},{4,0},{6,2},{8,12},{10,14},{12,8},{14,10},{16,20},{18,... | collective-permute-start | bytes 1572872 | tf_op jit(solution)/shard_map/ppermute | solution.py:33
  4.5 5.5 %collective-permute-start.4 = (bf16[1,64,512]{2,1,0:T(8,128)(2,1)S(1)}, bf16[1,64,512]{2,1,0:T(8,128)(2,1)S(1)}, u32[]{:S(2)}, u32[]{:S(2)}) collective-permute-start(bf16[1,64,512]{2,1,0:T(8,128)(2,1)S(1)} %bitcast.25), channel_id=1, source_target_pairs={{0,16},{2,18},{4,20},{6,22},{8,24},{10,26},{12,28},{14,30},{16,0},... | collective-permute-start | bytes 196616 | tf_op jit(solution)/shard_map/ppermute | solution.py:33
  7.2 13.1 %collective-permute-start.3 = (bf16[256,1024]{1,0:T(8,128)(2,1)S(1)}, bf16[256,1024]{1,0:T(8,128)(2,1)S(1)}, u32[]{:S(2)}, u32[]{:S(2)}) collective-permute-start(bf16[256,1024]{1,0:T(8,128)(2,1)S(1)} %slice.20), channel_id=1, source_target_pairs={{1,0},{3,2},{5,4},{7,6},{9,8},{11,10},{13,12},{15,14},{16,17},{18,... | collective-permute-start | bytes 1572872 | tf_op jit(solution)/shard_map/ppermute | solution.py:248
  10.0 5.0 %collective-permute-start.5 = (bf16[2,64,512]{2,1,0:T(8,128)(2,1)S(1)}, bf16[2,64,512]{2,1,0:T(8,128)(2,1)S(1)}, u32[]{:S(2)}, u32[]{:S(2)}) collective-permute-start(bf16[2,64,512]{2,1,0:T(8,128)(2,1)S(1)} %pad_maximum_fusion.3), channel_id=1, source_target_pairs={{0,8},{2,10},{4,12},{6,14},{8,0},{10,2},{12,4},{14,6},{16,24},{18,... | collective-permute-start | bytes 393224 | tf_op jit(solution)/shard_map/ppermute | solution.py:33
  17.9 10.9 %copy-start.5 = (bf16[1,1,512,1024]{3,2,1,0:T(8,128)(2,1)S(1)}, bf16[1,1,512,1024]{3,2,1,0:T(8,128)(2,1)}, u32[]{:S(2)}) copy-start(bf16[1,1,512,1024]{3,2,1,0:T(8,128)(2,1)} %param.11) | copy-start | bytes 3145732
  17.9 16.9 %copy-start.10 = (bf16[2,1024,64]{1,2,0:T(8,128)(2,1)S(1)}, bf16[2,1024,64]{1,2,0:T(8,128)(2,1)}, u32[]{:S(2)}) copy-start(bf16[2,1024,64]{1,2,0:T(8,128)(2,1)} %param.17) | copy-start | bytes 786436
  17.9 16.9 %copy-start.17 = (f32[2,1024]{1,0:T(2,128)S(1)}, f32[2,1024]{1,0:T(2,128)}, u32[]{:S(2)}) copy-start(f32[2,1024]{1,0:T(2,128)} %gain.7) | copy-start | bytes 24580
  20.2 4.9 %collective-permute-start.6 = (bf16[2,16,128,128]{3,2,1,0:T(8,128)(2,1)S(1)}, bf16[2,16,128,128]{3,2,1,0:T(8,128)(2,1)S(1)}, u32[]{:S(2)}, u32[]{:S(2)}) collective-permute-start(bf16[2,16,128,128]{3,2,1,0:T(8,128)(2,1)S(1)} %pad_maximum_fusion), channel_id=1, source_target_pairs={{0,2},{2,0},{4,6},{6,4},{8,10},{10,8},{12,14},{14,12},{16,18},{18,... | collective-permute-start | bytes 3145736 | tf_op jit(solution)/shard_map/ppermute | solution.py:33
  20.2 3.5 %collective-permute-start = (s32[1,33]{1,0:T(1,128)S(1)}, s32[1,33]{1,0:T(1,128)S(1)}, u32[]{:S(2)}, u32[]{:S(2)}) collective-permute-start(s32[1,33]{1,0:T(1,128)S(1)} %bitcast.33), channel_id=1, source_target_pairs={{0,4},{2,6},{4,0},{6,2},{8,12},{10,14},{12,8},{14,10},{16,20},{18,... | collective-permute-start | bytes 404 | tf_op jit(solution)/shard_map/ppermute | solution.py:33
  23.8 1.2 %collective-permute-start.1 = (s32[2,33]{1,0:T(2,128)S(1)}, s32[2,33]{1,0:T(2,128)S(1)}, u32[]{:S(2)}, u32[]{:S(2)}) collective-permute-start(s32[2,33]{1,0:T(2,128)S(1)} %pad_add_fusion.1), channel_id=1, source_target_pairs={{0,2},{2,0},{4,6},{6,4},{8,10},{10,8},{12,14},{14,12},{16,18},{18,... | collective-permute-start | bytes 800 | tf_op jit(solution)/shard_map/ppermute | solution.py:33
  25.0 9.9 %copy-start.2 = (bf16[2,1024,1024]{2,1,0:T(8,128)(2,1)S(1)}, bf16[2,1024,1024]{2,1,0:T(8,128)(2,1)}, u32[]{:S(2)}) copy-start(bf16[2,1024,1024]{2,1,0:T(8,128)(2,1)} %w_out.7) | copy-start | bytes 12582916
  25.3 9.6 %copy-start = (bf16[2,1024,1024]{2,1,0:T(8,128)(2,1)S(1)}, bf16[2,1024,1024]{2,1,0:T(8,128)(2,1)}, u32[]{:S(2)}) copy-start(bf16[2,1024,1024]{2,1,0:T(8,128)(2,1)} %w_in.7) | copy-start | bytes 12582916
  25.3 9.6 %copy-start.6 = (bf16[2,64,1024]{2,1,0:T(8,128)(2,1)S(1)}, bf16[2,64,1024]{2,1,0:T(8,128)(2,1)}, u32[]{:S(2)}) copy-start(bf16[2,64,1024]{2,1,0:T(8,128)(2,1)} %w_up.7) | copy-start | bytes 786436
  25.3 9.6 %copy-start.18 = (s32[1,1,512]{2,1,0:T(1,128)S(1)}, s32[1,1,512]{2,1,0:T(1,128)}, u32[]{:S(2)}) copy-start(s32[1,1,512]{2,1,0:T(1,128)} %param.16) | copy-start | bytes 6148
  26.7 6.7 %collective-permute-start.7 = (bf16[2,64,512]{2,1,0:T(8,128)(2,1)S(1)}, bf16[2,64,512]{2,1,0:T(8,128)(2,1)S(1)}, u32[]{:S(2)}, u32[]{:S(2)}) collective-permute-start(bf16[2,64,512]{2,1,0:T(8,128)(2,1)S(1)} %get-tuple-element.33), channel_id=1, source_target_pairs={{0,4},{2,6},{4,0},{6,2},{8,12},{10,14},{12,8},{14,10},{16,20},{18,... | collective-permute-start | bytes 393224 | tf_op jit(solution)/shard_map/ppermute | solution.py:33
  28.8 28.0 %collective-permute-start.9 = (bf16[256,1024]{1,0:T(8,128)(2,1)S(1)}, bf16[256,1024]{1,0:T(8,128)(2,1)S(1)}, u32[]{:S(2)}, u32[]{:S(2)}) collective-permute-start(bf16[256,1024]{1,0:T(8,128)(2,1)S(1)} %slice.23), channel_id=1, source_target_pairs={{1,16},{3,18},{5,20},{7,22},{9,24},{11,26},{13,28},{15,30},{16,1},... | collective-permute-start | bytes 1572872 | tf_op jit(solution)/shard_map/ppermute | solution.py:49
  32.1 27.4 %collective-permute-start.10 = (bf16[256,1024]{1,0:T(8,128)(2,1)S(1)}, bf16[256,1024]{1,0:T(8,128)(2,1)S(1)}, u32[]{:S(2)}, u32[]{:S(2)}) collective-permute-start(bf16[256,1024]{1,0:T(8,128)(2,1)S(1)} %collective-permute-done.3), channel_id=1, source_target_pairs={{0,16},{2,18},{4,20},{6,22},{8,24},{10,26},{12,28},{14,30},{17,1},... | collective-permute-start | bytes 1572872 | tf_op jit(solution)/shard_map/ppermute | solution.py:261
  33.5 1.3 %collective-permute-start.8 = (bf16[1,64,512]{2,1,0:T(8,128)(2,1)S(1)}, bf16[1,64,512]{2,1,0:T(8,128)(2,1)S(1)}, u32[]{:S(2)}, u32[]{:S(2)}) collective-permute-start(bf16[1,64,512]{2,1,0:T(8,128)(2,1)S(1)} %slice.43), channel_id=1, source_target_pairs={{0,2},{2,0},{4,6},{6,4},{8,10},{10,8},{12,14},{14,12},{16,18},{18,... | collective-permute-start | bytes 196616 | tf_op jit(solution)/shard_map/ppermute | solution.py:33
  39.7 1.4 %copy-start.7 = (f32[512,1024]{1,0:T(8,128)}, f32[512,1024]{1,0:T(8,128)S(1)}, u32[]{:S(2)}) copy-start(f32[512,1024]{1,0:T(8,128)S(1)} %get-tuple-element.39.total) | copy-start | bytes 6291460
  41.1 1.0 copy-start.11
  56.9 0.8 copy-start.13
  59.5 0.8 copy-start.15
  60.3 8.7 %collective-permute-start.12 = (bf16[64,512]{1,0:T(8,128)(2,1)}, bf16[64,512]{1,0:T(8,128)(2,1)}, u32[]{:S(2)}, u32[]{:S(2)}) collective-permute-start(bf16[64,512]{1,0:T(8,128)(2,1)} %get-tuple-element.43), channel_id=1, source_target_pairs={{1,16},{3,18},{5,20},{7,22},{9,24},{11,26},{13,28},{15,30},{16,1},... | collective-permute-start | bytes 196616 | tf_op jit(solution)/shard_map/ppermute | solution.py:49
  69.0 21.7 %copy-start.1 = (bf16[2,1024,1024]{2,1,0:T(8,128)(2,1)S(1)}, bf16[2,1024,1024]{2,1,0:T(8,128)(2,1)}, u32[]{:S(2)}) copy-start(bf16[2,1024,1024]{2,1,0:T(8,128)(2,1)} %w_in.7) | copy-start | bytes 12582916
  70.1 5.3 %collective-permute-start.13 = (bf16[1,64,512]{2,1,0:T(8,128)(2,1)S(1)}, bf16[1,64,512]{2,1,0:T(8,128)(2,1)S(1)}, u32[]{:S(2)}, u32[]{:S(2)}) collective-permute-start(bf16[1,64,512]{2,1,0:T(8,128)(2,1)S(1)} %fusion.2), channel_id=1, source_target_pairs={{0,16},{2,18},{4,20},{6,22},{8,24},{10,26},{12,28},{14,30},{16,0},... | collective-permute-start | bytes 196616 | tf_op jit(solution)/shard_map/ppermute | solution.py:33
  75.4 5.0 %collective-permute-start.14 = (bf16[2,64,512]{2,1,0:T(8,128)(2,1)S(1)}, bf16[2,64,512]{2,1,0:T(8,128)(2,1)S(1)}, u32[]{:S(2)}, u32[]{:S(2)}) collective-permute-start(bf16[2,64,512]{2,1,0:T(8,128)(2,1)S(1)} %pad_maximum_fusion.4), channel_id=1, source_target_pairs={{0,8},{2,10},{4,12},{6,14},{8,0},{10,2},{12,4},{14,6},{16,24},{18,... | collective-permute-start | bytes 393224 | tf_op jit(solution)/shard_map/ppermute | solution.py:33
  81.8 5.0 %collective-permute-start.15 = (bf16[2,64,512]{2,1,0:T(8,128)(2,1)S(1)}, bf16[2,64,512]{2,1,0:T(8,128)(2,1)S(1)}, u32[]{:S(2)}, u32[]{:S(2)}) collective-permute-start(bf16[2,64,512]{2,1,0:T(8,128)(2,1)S(1)} %get-tuple-element.45), channel_id=1, source_target_pairs={{0,4},{2,6},{4,0},{6,2},{8,12},{10,14},{12,8},{14,10},{16,20},{18,... | collective-permute-start | bytes 393224 | tf_op jit(solution)/shard_map/ppermute | solution.py:33
  82.8 7.9 %collective-permute-start.11 = (bf16[64,512]{1,0:T(8,128)(2,1)S(1)}, bf16[64,512]{1,0:T(8,128)(2,1)S(1)}, u32[]{:S(2)}, u32[]{:S(2)}) collective-permute-start(bf16[64,512]{1,0:T(8,128)(2,1)S(1)} %fusion.3.agg_t), channel_id=1, source_target_pairs={{1,16},{3,18},{5,20},{7,22},{9,24},{11,26},{13,28},{15,30},{16,1},... | collective-permute-start | bytes 196616 | tf_op jit(solution)/shard_map/ppermute | solution.py:49
  86.9 15.8 %collective-permute-start.16 = (bf16[1,64,512]{2,1,0:T(8,128)(2,1)S(1)}, bf16[1,64,512]{2,1,0:T(8,128)(2,1)S(1)}, u32[]{:S(2)}, u32[]{:S(2)}) collective-permute-start(bf16[1,64,512]{2,1,0:T(8,128)(2,1)S(1)} %slice.42), channel_id=1, source_target_pairs={{0,2},{2,0},{4,6},{6,4},{8,10},{10,8},{12,14},{14,12},{16,18},{18,... | collective-permute-start | bytes 196616 | tf_op jit(solution)/shard_map/ppermute | solution.py:33
  90.8 2.2 %copy-start.3 = (bf16[2,1024,1024]{2,1,0:T(8,128)(2,1)S(1)}, bf16[2,1024,1024]{2,1,0:T(8,128)(2,1)}, u32[]{:S(2)}) copy-start(bf16[2,1024,1024]{2,1,0:T(8,128)(2,1)} %w_out.7) | copy-start | bytes 12582916
  93.0 1.6 %copy-start.8 = (f32[512,1024]{1,0:T(8,128)S(1)}, f32[512,1024]{1,0:T(8,128)}, u32[]{:S(2)}) copy-start(f32[512,1024]{1,0:T(8,128)} %copy-done.7) | copy-start | bytes 6291460
  94.5 1.2 %copy-start.12 = (bf16[512,1024]{1,0:T(8,128)(2,1)S(1)}, bf16[512,1024]{1,0:T(8,128)(2,1)}, u32[]{:S(2)}) copy-start(bf16[512,1024]{1,0:T(8,128)(2,1)} %copy-done.11) | copy-start | bytes 3145732
  95.8 1.0 copy-start.14
  96.8 1.0 copy-start.16
  102.8 8.0 %collective-permute-start.17 = (bf16[64,512]{1,0:T(8,128)(2,1)S(1)}, bf16[64,512]{1,0:T(8,128)(2,1)S(1)}, u32[]{:S(2)}, u32[]{:S(2)}) collective-permute-start(bf16[64,512]{1,0:T(8,128)(2,1)S(1)} %fusion.4.agg_t), channel_id=1, source_target_pairs={{1,16},{3,18},{5,20},{7,22},{9,24},{11,26},{13,28},{15,30},{16,1},... | collective-permute-start | bytes 196616 | tf_op jit(solution)/shard_map/ppermute | solution.py:49

commit v3 on v2

--- a/solution.py
+++ b/solution.py
@@ -11,7 +11,7 @@
 LAYERS = 2
 ROWS = 256
 EXCHANGE_BITS = 2
-VMEM_LIMIT = 24 * 2**20
+MIB = 2**20
 F32 = jnp.float32
 BF16 = jnp.bfloat16
 
@@ -49,7 +49,7 @@
     return lax.ppermute(values, ("src", "tgt"), mirror_pairs())
 
 
-def call(body, name, outs, scalars, arrays, scratch=(), flops=0, moved=0):
+def call(body, name, outs, scalars, arrays, scratch=(), flops=0, moved=0, limit=18):
     smem = pl.BlockSpec(memory_space=pltpu.SMEM)
     vmem = pl.BlockSpec(memory_space=pltpu.VMEM)
     return pl.pallas_call(
@@ -59,7 +59,7 @@
         scratch_shapes=list(scratch),
         out_shape=list(outs),
         name=name,
-        compiler_params=pltpu.CompilerParams(vmem_limit_bytes=VMEM_LIMIT),
+        compiler_params=pltpu.CompilerParams(vmem_limit_bytes=limit * MIB),
         cost_estimate=pl.CostEstimate(flops=flops, bytes_accessed=moved, transcendentals=0),
     )(*scalars, *arrays)
 
@@ -91,6 +91,7 @@
         [w_proj_t, state],
         flops=2 * state.size * shape[0],
         moved=2 * state.size,
+        limit=8,
     )[0]
 
 
@@ -143,6 +144,7 @@
         scratch=[pltpu.VMEM((tiles, width, edges), F32)],
         flops=2 * coeffs.size * width,
         moved=2 * coeffs.size,
+        limit=8,
     )
 
 
@@ -162,11 +164,6 @@
 
 def weights_of(layer_index, w_up, w_in, w_out, gain):
     return [w.at[layer_index] for w in (w_up, w_in, w_out)] + [gain.at[pl.ds(layer_index, 1)]]
-
-
-def one_hot(column):
-    lanes = lax.broadcasted_iota(jnp.int32, (column.shape[0], column.shape[0]), 1)
-    return (column == lanes).astype(BF16)
 
 
 def picking(column, rows, edges):
@@ -185,7 +182,14 @@
         total[rows, :] = moved
         v_t[:, rows] = dot_nt(w_next, moved.astype(BF16)).astype(BF16)
     u = dot_nt(w_next, branch[...]).astype(BF16)
-    u_t[...] = dot(u, one_hot(reverse_column(reverse))).astype(BF16)
+    edges = u.shape[1]
+    rows = lax.broadcasted_iota(jnp.int32, (edges, edges), 0)
+    u_t[...] = dot_nt(u, (reverse[...] == rows).astype(BF16)).astype(BF16)
+
+
+def combine_body(v_t, u_t, u_other, out):
+    mirrored = jnp.where(own_mirror(), u_t[...], u_other[...])
+    out[...] = (v_t[...].astype(F32) + mirrored.astype(F32)).astype(BF16)
 
 
 def second_body(
@@ -217,10 +221,12 @@
     edges = total.shape[0]
     weights = weights_of(1, w_up, w_in, w_out, gain)
     low = jnp.where(own_mirror(), agg_t[...], agg_other[...])
-    column = reverse_column(reverse)
+    at = lax.broadcasted_iota(jnp.int32, (edges, edges), 0)
+    agg = dot(low, (reverse[...] == at).astype(BF16)).T.astype(BF16)
     for rows in chunks(edges):
-        agg = dot_nt(picking(column, rows, edges), low).astype(BF16)
-        summed, out = branch_of(mirrored[rows, :], agg, *weights)
+        summed, out = branch_of(
+            mirrored[rows, :], agg[rows.start : rows.start + rows.size], *weights
+        )
         state[rows, :] = (total[rows, :] + out.astype(F32)).astype(BF16)
 
 
@@ -302,20 +308,23 @@
     w_proj_t = jnp.swapaxes(w_proj, 1, 2)
     weights = [w_up, w_in, w_out, norm_gain]
 
-    proj0 = project(w_proj_t, state0)
+    high, low = 1 << (EXCHANGE_BITS - 1), 1
     own_index = jnp.concatenate([block_target[0, 0], block_source[0, 0], block_count[0]])
-    own_coeffs, own_index, held_state, proj0 = lax.optimization_barrier(
-        (triplet_coeff[0, 0], own_index, state0, proj0)
-    )
-    index = gather_low(own_index)
+    index_y = gather_step(own_index[None], high)
+    index_y, state_in = lax.optimization_barrier((index_y, state0))
+    proj0 = project(w_proj_t, state_in)
+    index_y, own_coeffs, held_state, proj0 = lax.optimization_barrier(
+        (index_y, triplet_coeff[0, 0], state0, proj0)
+    )
     half = edges // 2
     turned = second_route_x(held_state[half:])
-    coeffs_y = gather_step(own_coeffs[None], 1 << (EXCHANGE_BITS - 1))
+    coeffs_y = gather_step(own_coeffs[None], high)
+    index = gather_step(index_y, low)
     pool = gather_high(proj0)
-    coeffs_y, held_state, turned, pool = lax.optimization_barrier(
-        (coeffs_y, held_state, turned, pool)
-    )
-    coeffs = gather_step(coeffs_y, 1)
+    index, coeffs_y, held_state, turned, pool = lax.optimization_barrier(
+        (index, coeffs_y, held_state, turned, pool)
+    )
+    coeffs = gather_step(coeffs_y, low)
     other_low = to_mirror(held_state[:half])
     other_high = second_route_z(turned, held_state[half:])
     kept, sent = triplet_partials(index, pool, coeffs)
@@ -335,15 +344,13 @@
         flops=work,
         moved=8 * 2**20,
     )
-    u_t, other_low, other_high = lax.optimization_barrier((u_t, other_low, other_high))
+    agg0_other = to_mirror(agg0)
+    u_t, other_low, other_high, agg0_other = lax.optimization_barrier(
+        (u_t, other_low, other_high, agg0_other)
+    )
     u_other = to_mirror(u_t)
-    agg0_other = to_mirror(agg0)
-    mirrored_u = jnp.where(own_mirror(), u_t, u_other)
-    proj1 = (v_t.astype(F32) + mirrored_u.astype(F32)).astype(BF16)
+    proj1 = call(combine_body, "combine", [like(u_t.shape, BF16)], [], [v_t, u_t, u_other], limit=4)[0]
     pool1 = gather_high(proj1)
-    kept, sent = triplet_partials(index, pool1, coeffs)
-    agg1 = exchange_sums(kept, sent)
-    agg1_other = to_mirror(agg1)
     state1, mirrored1 = call(
         second_body,
         "second",
@@ -353,6 +360,10 @@
         flops=work + 2 * edges * edges * features,
         moved=10 * 2**20,
     )
+    state1, mirrored1, pool1 = lax.optimization_barrier((state1, mirrored1, pool1))
+    kept, sent = triplet_partials(index, pool1, coeffs)
+    agg1 = exchange_sums(kept, sent)
+    agg1_other = to_mirror(agg1)
     total1 = call(
         third_body,
         "third",

time: 118 us -> 101 us (0.86); the launches traced: 116 us -> 101 us
  local copies, waits for them, and re-layouts: 13.6 us -> 2.55 us
  waiting for transfers between devices: 53.4 us -> 50.4 us
    unnamed x41 -> x21, local copies, waits for them, and re-layouts: 13.3 us -> 2.28 us
    ppermute x4, starting transfers between devices: 11.5 us -> 14.1 us  [to_mirror(): return lax.ppermute(values, ('src', 'tgt'), mirror_pairs())]
    ppermute x1, waiting for transfers between devices: 1.89 us -> 0.01 us  [second_route_z(): return lax.ppermute(turned, ('src', 'tgt'), pairs)]
    ppermute x4, waiting for transfers between devices: 26.8 us -> 25 us  [to_mirror(): return lax.ppermute(values, ('src', 'tgt'), mirror_pairs())]
    ppermute x12, starting transfers between devices: 9.39 us -> 7.72 us  [hop(): return lax.ppermute(values, 'src', [(i, i ^ bit) for i in range(size)])]
    pallas_call x7 -> x8, Pallas kernels: 21 us -> 20.4 us  [call(): pl.pallas_call(body, in_specs=[smem] * len(scalars) + [vmem] * len(arrays...]
  transfers between devices with their start and end apart: 18 -> 18, of which waited for: 15 -> 16; matrix products, arithmetic and copies ran while one was open for 0% -> 0% of each run, Pallas kernels for 11% -> 12%
where the time goes in v3:
time: 101 us
  waiting for transfers between devices  50.4 us (50%)
  starting transfers between devices  25.6 us (25%)
  Pallas kernels  20.4 us (20%)
  local copies, waits for them, and re-layouts  2.55 us (3%)
  other arithmetic  1.04 us (1%)
    ppermute x4, waiting for transfers between devices, to_mirror(): return lax.ppermute(values, ('src', 'tgt'), mirror_pairs())  25 us
    ppermute x12, waiting for transfers between devices, hop(): return lax.ppermute(values, 'src', [(i, i ^ bit) for i in range(size)])  23.2 us
    pallas_call x8, Pallas kernels, call(): pl.pallas_call(body, in_specs=[smem] * len(scalars) + [vmem] * len(arrays...  20.4 us
    ppermute x4, starting transfers between devices, to_mirror(): return lax.ppermute(values, ('src', 'tgt'), mirror_pairs())  14.1 us
    ppermute x12, starting transfers between devices, hop(): return lax.ppermute(values, 'src', [(i, i ^ bit) for i in range(size)])  7.72 us
    ppermute x1, starting transfers between devices, second_route_x(): return lax.ppermute(values, ('src', 'tgt'), pairs)  2.47 us
    unnamed x21, local copies, waits for them, and re-layouts  2.28 us
    ppermute x1, waiting for transfers between devices, second_route_x(): return lax.ppermute(values, ('src', 'tgt'), pairs)  2.19 us
  transfers between devices with their start and end apart: 18, of which 16 were waited for; matrix products, arithmetic and copies ran while one was open for 0% of the time, Pallas kernels for 12%

profile of v3, /device:TPU:6, one launch (start us, length us, event | category | flops | bytes accessed | tf_op | source)
XLA Modules:
  0.0 100.9 jit_solution(3502840181101135860)
XLA Ops:
  0.7 0.7 add_bitcast_fusion
  1.4 0.5 collective-permute-start
  1.9 3.0 %collective-permute-done = s32[1,33]{1,0:T(1,128)S(1)} collective-permute-done((s32[1,33]{1,0:T(1,128)S(1)}, s32[1,33]{1,0:T(1,128)S(1)}, u32[]{:S(2)}, u32[]{:S(2)}) %collective-permute-start) | collective-permute-done | bytes 164 | tf_op jit(solution)/shard_map/ppermute | solution.py:33
  5.0 1.2 %copy-done.2 = bf16[1,1,512,1024]{3,2,1,0:T(8,128)(2,1)S(1)} copy-done((bf16[1,1,512,1024]{3,2,1,0:T(8,128)(2,1)S(1)}, bf16[1,1,512,1024]{3,2,1,0:T(8,128)(2,1)}, u32[]{:S(2)}) %copy-start.2) | copy-done | bytes 1048600
  6.2 0.9 copy-done.5
  7.1 0.4 project.1
  7.6 0.6 collective-permute-start.2
  8.1 2.6 %collective-permute-start.4 = (bf16[1,64,512]{2,1,0:T(8,128)(2,1)S(1)}, bf16[1,64,512]{2,1,0:T(8,128)(2,1)S(1)}, u32[]{:S(2)}, u32[]{:S(2)}) collective-permute-start(bf16[1,64,512]{2,1,0:T(8,128)(2,1)S(1)} %bitcast.28), channel_id=1, source_target_pairs={{0,16},{2,18},{4,20},{6,22},{8,24},{10,26},{12,28},{14,30},{16,0},... | collective-permute-start | bytes 196616 | tf_op jit(solution)/shard_map/ppermute | solution.py:33
  10.8 2.5 %collective-permute-start.3 = (bf16[256,1024]{1,0:T(8,128)(2,1)S(1)}, bf16[256,1024]{1,0:T(8,128)(2,1)S(1)}, u32[]{:S(2)}, u32[]{:S(2)}) collective-permute-start(bf16[256,1024]{1,0:T(8,128)(2,1)S(1)} %slice.20), channel_id=1, source_target_pairs={{1,0},{3,2},{5,4},{7,6},{9,8},{11,10},{13,12},{15,14},{16,17},{18,... | collective-permute-start | bytes 1572872 | tf_op jit(solution)/shard_map/ppermute | solution.py:254
  13.2 0.1 collective-permute-done.4
  13.3 1.6 %collective-permute-start.5 = (bf16[2,64,512]{2,1,0:T(8,128)(2,1)S(1)}, bf16[2,64,512]{2,1,0:T(8,128)(2,1)S(1)}, u32[]{:S(2)}, u32[]{:S(2)}) collective-permute-start(bf16[2,64,512]{2,1,0:T(8,128)(2,1)S(1)} %pad_maximum_fusion.3), channel_id=1, source_target_pairs={{0,8},{2,10},{4,12},{6,14},{8,0},{10,2},{12,4},{14,6},{16,24},{18,... | collective-permute-start | bytes 393224 | tf_op jit(solution)/shard_map/ppermute | solution.py:33
  15.0 1.1 %collective-permute-done.1 = s32[2,33]{1,0:T(2,128)S(1)} collective-permute-done((s32[2,33]{1,0:T(2,128)S(1)}, s32[2,33]{1,0:T(2,128)S(1)}, u32[]{:S(2)}, u32[]{:S(2)}) %collective-permute-start.1) | collective-permute-done | bytes 296 | tf_op jit(solution)/shard_map/ppermute | solution.py:33
  16.1 2.2 %collective-permute-done.5 = bf16[2,64,512]{2,1,0:T(8,128)(2,1)S(1)} collective-permute-done((bf16[2,64,512]{2,1,0:T(8,128)(2,1)S(1)}, bf16[2,64,512]{2,1,0:T(8,128)(2,1)S(1)}, u32[]{:S(2)}, u32[]{:S(2)}) %collective-permute-start.5) | collective-permute-done | bytes 131104 | tf_op jit(solution)/shard_map/ppermute | solution.py:33
  18.4 2.0 %collective-permute-done.2 = bf16[1,16,128,128]{3,2,1,0:T(8,128)(2,1)S(1)} collective-permute-done((bf16[1,16,128,128]{3,2,1,0:T(8,128)(2,1)}, bf16[1,16,128,128]{3,2,1,0:T(8,128)(2,1)S(1)}, u32[]{:S(2)}, u32[]{:S(2)}) %collective-permute-start.2) | collective-permute-done | bytes 524320 | tf_op jit(solution)/shard_map/ppermute | solution.py:33
  20.4 0.1 pad_maximum_fusion
  20.5 2.2 %collective-permute-done.3 = bf16[256,1024]{1,0:T(8,128)(2,1)S(1)} collective-permute-done((bf16[256,1024]{1,0:T(8,128)(2,1)S(1)}, bf16[256,1024]{1,0:T(8,128)(2,1)S(1)}, u32[]{:S(2)}, u32[]{:S(2)}) %collective-permute-start.3) | collective-permute-done | bytes 524320 | tf_op jit(solution)/shard_map/ppermute | solution.py:254
  22.7 0.1 constant_dynamic-update-slice_fusion.1
  22.8 2.6 %collective-permute-done.6 = bf16[2,16,128,128]{3,2,1,0:T(8,128)(2,1)S(1)} collective-permute-done((bf16[2,16,128,128]{3,2,1,0:T(8,128)(2,1)S(1)}, bf16[2,16,128,128]{3,2,1,0:T(8,128)(2,1)S(1)}, u32[]{:S(2)}, u32[]{:S(2)}) %collective-permute-start.6) | collective-permute-done | bytes 1048608 | tf_op jit(solution)/shard_map/ppermute | solution.py:33
  25.3 0.2 constant_dynamic-update-slice_fusion.coeffs
  25.5 0.0 copy-start
  25.5 0.0 copy-start.4
  25.5 0.0 copy-start.8
  25.6 1.8 %triplets.2 = (f32[2,64,512]{2,1,0:T(8,128)S(1)}, bf16[2,64,512]{2,1,0:T(8,128)(2,1)S(1)}) custom-call(s32[4,33]{1,0:T(4,128)S(1)} %pad_add_fusion.index, bf16[4,64,512]{2,1,0:T(8,128)(2,1)S(1)} %pad_maximum_fusion.1.pool, bf16[4,16,128,128]{3,2,1,0:T(8,128)(2,1)S(1)} %constant_dynamic-update-slice_fusion.coeffs), custom_call_target="tpu_custom_call" | custom-call | flops 134217728 | bytes 2097152 | tf_op jit(solution)/shard_map/triplets/pallas_call | solution.py:55
  27.4 1.6 %collective-permute-start.7 = (bf16[2,64,512]{2,1,0:T(8,128)(2,1)S(1)}, bf16[2,64,512]{2,1,0:T(8,128)(2,1)S(1)}, u32[]{:S(2)}, u32[]{:S(2)}) collective-permute-start(bf16[2,64,512]{2,1,0:T(8,128)(2,1)S(1)} %get-tuple-element.43), channel_id=1, source_target_pairs={{0,4},{2,6},{4,0},{6,2},{8,12},{10,14},{12,8},{14,10},{16,20},{18,... | collective-permute-start | bytes 393224 | tf_op jit(solution)/shard_map/ppermute | solution.py:33
  29.0 2.7 %collective-permute-start.9 = (bf16[256,1024]{1,0:T(8,128)(2,1)S(1)}, bf16[256,1024]{1,0:T(8,128)(2,1)S(1)}, u32[]{:S(2)}, u32[]{:S(2)}) collective-permute-start(bf16[256,1024]{1,0:T(8,128)(2,1)S(1)} %slice.23), channel_id=1, source_target_pairs={{1,16},{3,18},{5,20},{7,22},{9,24},{11,26},{13,28},{15,30},{16,1},... | collective-permute-start | bytes 1572872 | tf_op jit(solution)/shard_map/ppermute | solution.py:49
  31.7 1.3 %collective-permute-start.10 = (bf16[256,1024]{1,0:T(8,128)(2,1)S(1)}, bf16[256,1024]{1,0:T(8,128)(2,1)S(1)}, u32[]{:S(2)}, u32[]{:S(2)}) collective-permute-start(bf16[256,1024]{1,0:T(8,128)(2,1)S(1)} %collective-permute-done.3), channel_id=1, source_target_pairs={{0,16},{2,18},{4,20},{6,22},{8,24},{10,26},{12,28},{14,30},{17,1},... | collective-permute-start | bytes 1572872 | tf_op jit(solution)/shard_map/ppermute | solution.py:267
  33.0 0.1 collective-permute-start.8
  33.1 1.2 %collective-permute-done.8 = bf16[1,64,512]{2,1,0:T(8,128)(2,1)S(1)} collective-permute-done((bf16[1,64,512]{2,1,0:T(8,128)(2,1)S(1)}, bf16[1,64,512]{2,1,0:T(8,128)(2,1)S(1)}, u32[]{:S(2)}, u32[]{:S(2)}) %collective-permute-start.8) | collective-permute-done | bytes 65568 | tf_op jit(solution)/shard_map/ppermute | solution.py:33
  34.4 5.0 %collective-permute-start.11 = (bf16[64,512]{1,0:T(8,128)(2,1)S(1)}, bf16[64,512]{1,0:T(8,128)(2,1)S(1)}, u32[]{:S(2)}, u32[]{:S(2)}) collective-permute-start(bf16[64,512]{1,0:T(8,128)(2,1)S(1)} %fusion.2.agg_t), channel_id=1, source_target_pairs={{1,16},{3,18},{5,20},{7,22},{9,24},{11,26},{13,28},{15,30},{16,1},... | collective-permute-start | bytes 196616 | tf_op jit(solution)/shard_map/ppermute | solution.py:49
  39.4 4.1 %first.1 = (f32[512,1024]{1,0:T(8,128)S(1)}, bf16[512,1024]{1,0:T(8,128)(2,1)S(1)}, bf16[64,512]{1,0:T(8,128)(2,1)S(1)}, bf16[64,512]{1,0:T(8,128)(2,1)S(1)}) custom-call(bf16[2,64,1024]{2,1,0:T(8,128)(2,1)S(1)} %copy-done.4, bf16[2,1024,1024]{2,1,0:T(8,128)(2,1)S(1)} %copy-done, bf16[2,1024,1024]{2,1,0:T(8,128)(2,1)S(1)} %copy-done.1, ...), custom_call_target="tpu_custom_call" | custom-call | flops 2147483648 | bytes 8388608 | tf_op jit(solution)/shard_map/first/pallas_call | solution.py:55
  43.5 16.2 %collective-permute-done.9.other_low = bf16[256,1024]{1,0:T(8,128)(2,1)S(1)} collective-permute-done((bf16[256,1024]{1,0:T(8,128)(2,1)S(1)}, bf16[256,1024]{1,0:T(8,128)(2,1)S(1)}, u32[]{:S(2)}, u32[]{:S(2)}) %collective-permute-start.9) | collective-permute-done | bytes 524320 | tf_op jit(solution)/shard_map/ppermute | solution.py:49
  59.7 0.7 collective-permute-done.11.agg_other
  60.4 1.9 %collective-permute-start.12 = (bf16[64,512]{1,0:T(8,128)(2,1)S(1)}, bf16[64,512]{1,0:T(8,128)(2,1)S(1)}, u32[]{:S(2)}, u32[]{:S(2)}) collective-permute-start(bf16[64,512]{1,0:T(8,128)(2,1)S(1)} %get-tuple-element.55.u_t), channel_id=1, source_target_pairs={{1,16},{3,18},{5,20},{7,22},{9,24},{11,26},{13,28},{15,30},{16,1},... | collective-permute-start | bytes 196616 | tf_op jit(solution)/shard_map/ppermute | solution.py:49
  62.3 6.4 %collective-permute-done.12.u_other = bf16[64,512]{1,0:T(8,128)(2,1)S(1)} collective-permute-done((bf16[64,512]{1,0:T(8,128)(2,1)S(1)}, bf16[64,512]{1,0:T(8,128)(2,1)S(1)}, u32[]{:S(2)}, u32[]{:S(2)}) %collective-permute-start.12) | collective-permute-done | bytes 65568 | tf_op jit(solution)/shard_map/ppermute | solution.py:49
  68.7 0.1 collective-permute-start.13
  68.8 5.2 %collective-permute-done.13 = bf16[1,64,512]{2,1,0:T(8,128)(2,1)S(1)} collective-permute-done((bf16[1,64,512]{2,1,0:T(8,128)(2,1)S(1)}, bf16[1,64,512]{2,1,0:T(8,128)(2,1)S(1)}, u32[]{:S(2)}, u32[]{:S(2)}) %collective-permute-start.13) | collective-permute-done | bytes 65568 | tf_op jit(solution)/shard_map/ppermute | solution.py:33
  74.0 0.1 collective-permute-start.14
  74.1 4.8 %second.1 = (bf16[512,1024]{1,0:T(8,128)(2,1)S(1)}, bf16[512,1024]{1,0:T(8,128)(2,1)S(1)}) custom-call(bf16[2,64,1024]{2,1,0:T(8,128)(2,1)S(1)} %copy-done.4, bf16[2,1024,1024]{2,1,0:T(8,128)(2,1)S(1)} %copy-done, bf16[2,1024,1024]{2,1,0:T(8,128)(2,1)S(1)} %copy-done.1, f32[2,1024]{1,0:T(2,128)S(1)} %copy-done.7, bf16[512,1024]{1,0:T(8,128)(2,1)S(1)} %bitcast.22, ...), custom_call_target="tpu_custom_call" | custom-call | flops 2684354560 | bytes 10485760 | tf_op jit(solution)/shard_map/second/pallas_call | solution.py:55
  78.9 0.1 collective-permute-done.14
  79.0 1.8 %triplets.3 = (f32[2,64,512]{2,1,0:T(8,128)S(1)}, bf16[2,64,512]{2,1,0:T(8,128)(2,1)S(1)}) custom-call(s32[4,33]{1,0:T(4,128)S(1)} %pad_add_fusion.index, bf16[4,64,512]{2,1,0:T(8,128)(2,1)S(1)} %pad_maximum_fusion.2.pool, bf16[4,16,128,128]{3,2,1,0:T(8,128)(2,1)S(1)} %constant_dynamic-update-slice_fusion.coeffs), custom_call_target="tpu_custom_call" | custom-call | flops 134217728 | bytes 2097152 | tf_op jit(solution)/shard_map/triplets/pallas_call | solution.py:55
  80.9 0.5 collective-permute-start.15
  81.4 4.5 %collective-permute-done.15 = bf16[2,64,512]{2,1,0:T(8,128)(2,1)S(1)} collective-permute-done((bf16[2,64,512]{2,1,0:T(8,128)(2,1)S(1)}, bf16[2,64,512]{2,1,0:T(8,128)(2,1)S(1)}, u32[]{:S(2)}, u32[]{:S(2)}) %collective-permute-start.15) | collective-permute-done | bytes 131104 | tf_op jit(solution)/shard_map/ppermute | solution.py:33
  86.0 0.1 collective-permute-start.16
  86.0 1.2 %collective-permute-done.16 = bf16[1,64,512]{2,1,0:T(8,128)(2,1)S(1)} collective-permute-done((bf16[1,64,512]{2,1,0:T(8,128)(2,1)S(1)}, bf16[1,64,512]{2,1,0:T(8,128)(2,1)S(1)}, u32[]{:S(2)}, u32[]{:S(2)}) %collective-permute-start.16) | collective-permute-done | bytes 65568 | tf_op jit(solution)/shard_map/ppermute | solution.py:33
  87.3 4.6 %collective-permute-start.17 = (bf16[64,512]{1,0:T(8,128)(2,1)S(1)}, bf16[64,512]{1,0:T(8,128)(2,1)S(1)}, u32[]{:S(2)}, u32[]{:S(2)}) collective-permute-start(bf16[64,512]{1,0:T(8,128)(2,1)S(1)} %fusion.3.agg_t), channel_id=1, source_target_pairs={{1,16},{3,18},{5,20},{7,22},{9,24},{11,26},{13,28},{15,30},{16,1},... | collective-permute-start | bytes 196616 | tf_op jit(solution)/shard_map/ppermute | solution.py:49
  91.9 3.1 %third.1.total = f32[512,1024]{1,0:T(8,128)S(1)} custom-call(bf16[2,64,1024]{2,1,0:T(8,128)(2,1)S(1)} %copy-done.4, bf16[2,1024,1024]{2,1,0:T(8,128)(2,1)S(1)} %copy-done, bf16[2,1024,1024]{2,1,0:T(8,128)(2,1)S(1)} %copy-done.1, f32[2,1024]{1,0:T(2,128)S(1)} %copy-done.7, bf16[512,1024]{1,0:T(8,128)(2,1)S(1)} %get-tuple-element.60.state, ...), custom_call_target="tpu_custom_call" | custom-call | flops 2147483648 | bytes 8388608 | tf_op jit(solution)/shard_map/third/pallas_call | solution.py:55
  95.0 1.7 %collective-permute-done.17.agg_other = bf16[64,512]{1,0:T(8,128)(2,1)S(1)} collective-permute-done((bf16[64,512]{1,0:T(8,128)(2,1)S(1)}, bf16[64,512]{1,0:T(8,128)(2,1)S(1)}, u32[]{:S(2)}, u32[]{:S(2)}) %collective-permute-start.17) | collective-permute-done | bytes 65568 | tf_op jit(solution)/shard_map/ppermute | solution.py:49
  96.7 4.3 %last.1 = bf16[512,1024]{1,0:T(8,128)(2,1)} custom-call(bf16[2,64,1024]{2,1,0:T(8,128)(2,1)S(1)} %copy-done.4, bf16[2,1024,1024]{2,1,0:T(8,128)(2,1)S(1)} %copy-done, bf16[2,1024,1024]{2,1,0:T(8,128)(2,1)S(1)} %copy-done.1, f32[2,1024]{1,0:T(2,128)S(1)} %copy-done.7, bf16[512,1024]{1,0:T(8,128)(2,1)S(1)} %get-tuple-element.56.mirrored, ...), custom_call_target="tpu_custom_call" | custom-call | flops 2147483648 | bytes 8388608 | tf_op jit(solution)/shard_map/last/pallas_call | solution.py:55
  (34 shorter events, 0.3 us)
Async XLA Ops:
  1.4 3.5 %collective-permute-start = (s32[1,33]{1,0:T(1,128)S(1)}, s32[1,33]{1,0:T(1,128)S(1)}, u32[]{:S(2)}, u32[]{:S(2)}) collective-permute-start(s32[1,33]{1,0:T(1,128)S(1)} %add_bitcast_fusion), channel_id=1, source_target_pairs={{0,4},{2,6},{4,0},{6,2},{8,12},{10,14},{12,8},{14,10},{16,20},{18,... | collective-permute-start | bytes 404 | tf_op jit(solution)/shard_map/ppermute | solution.py:33
  5.0 1.2 %copy-start.2 = (bf16[1,1,512,1024]{3,2,1,0:T(8,128)(2,1)S(1)}, bf16[1,1,512,1024]{3,2,1,0:T(8,128)(2,1)}, u32[]{:S(2)}) copy-start(bf16[1,1,512,1024]{3,2,1,0:T(8,128)(2,1)} %param.11) | copy-start | bytes 3145732
  6.2 0.9 copy-start.5
  7.1 13.2 %copy-start.9 = (bf16[1,1,16,128,128]{4,3,2,1,0:T(8,128)(2,1)S(1)}, bf16[1,1,16,128,128]{4,3,2,1,0:T(8,128)(2,1)}, u32[]{:S(2)}) copy-start(bf16[1,1,16,128,128]{4,3,2,1,0:T(8,128)(2,1)} %param.12) | copy-start | bytes 1572868
  7.6 12.8 %collective-permute-start.2 = (bf16[1,16,128,128]{3,2,1,0:T(8,128)(2,1)}, bf16[1,16,128,128]{3,2,1,0:T(8,128)(2,1)S(1)}, u32[]{:S(2)}, u32[]{:S(2)}) collective-permute-start(bf16[1,16,128,128]{3,2,1,0:T(8,128)(2,1)} %bitcast.34), channel_id=1, source_target_pairs={{0,4},{2,6},{4,0},{6,2},{8,12},{10,14},{12,8},{14,10},{16,20},{18,... | collective-permute-start | bytes 1572872 | tf_op jit(solution)/shard_map/ppermute | solution.py:33
  8.1 5.2 %collective-permute-start.4 = (bf16[1,64,512]{2,1,0:T(8,128)(2,1)S(1)}, bf16[1,64,512]{2,1,0:T(8,128)(2,1)S(1)}, u32[]{:S(2)}, u32[]{:S(2)}) collective-permute-start(bf16[1,64,512]{2,1,0:T(8,128)(2,1)S(1)} %bitcast.28), channel_id=1, source_target_pairs={{0,16},{2,18},{4,20},{6,22},{8,24},{10,26},{12,28},{14,30},{16,0},... | collective-permute-start | bytes 196616 | tf_op jit(solution)/shard_map/ppermute | solution.py:33
  10.8 11.9 %collective-permute-start.3 = (bf16[256,1024]{1,0:T(8,128)(2,1)S(1)}, bf16[256,1024]{1,0:T(8,128)(2,1)S(1)}, u32[]{:S(2)}, u32[]{:S(2)}) collective-permute-start(bf16[256,1024]{1,0:T(8,128)(2,1)S(1)} %slice.20), channel_id=1, source_target_pairs={{1,0},{3,2},{5,4},{7,6},{9,8},{11,10},{13,12},{15,14},{16,17},{18,... | collective-permute-start | bytes 1572872 | tf_op jit(solution)/shard_map/ppermute | solution.py:254
  13.3 5.0 %collective-permute-start.5 = (bf16[2,64,512]{2,1,0:T(8,128)(2,1)S(1)}, bf16[2,64,512]{2,1,0:T(8,128)(2,1)S(1)}, u32[]{:S(2)}, u32[]{:S(2)}) collective-permute-start(bf16[2,64,512]{2,1,0:T(8,128)(2,1)S(1)} %pad_maximum_fusion.3), channel_id=1, source_target_pairs={{0,8},{2,10},{4,12},{6,14},{8,0},{10,2},{12,4},{14,6},{16,24},{18,... | collective-permute-start | bytes 393224 | tf_op jit(solution)/shard_map/ppermute | solution.py:33
  15.0 1.1 %collective-permute-start.1 = (s32[2,33]{1,0:T(2,128)S(1)}, s32[2,33]{1,0:T(2,128)S(1)}, u32[]{:S(2)}, u32[]{:S(2)}) collective-permute-start(s32[2,33]{1,0:T(2,128)S(1)} %pad_add_fusion.1), channel_id=1, source_target_pairs={{0,2},{2,0},{4,6},{6,4},{8,10},{10,8},{12,14},{14,12},{16,18},{18,... | collective-permute-start | bytes 800 | tf_op jit(solution)/shard_map/ppermute | solution.py:33
  20.4 8.6 %copy-start.3 = (bf16[1,1,512,1024]{3,2,1,0:T(8,128)(2,1)S(1)}, bf16[1,1,512,1024]{3,2,1,0:T(8,128)(2,1)}, u32[]{:S(2)}) copy-start(bf16[1,1,512,1024]{3,2,1,0:T(8,128)(2,1)} %param.11) | copy-start | bytes 3145732
  20.4 19.0 %copy-start.6 = (bf16[2,1024,64]{1,2,0:T(8,128)(2,1)S(1)}, bf16[2,1024,64]{1,2,0:T(8,128)(2,1)}, u32[]{:S(2)}) copy-start(bf16[2,1024,64]{1,2,0:T(8,128)(2,1)} %param.17) | copy-start | bytes 786436
  20.4 19.0 %copy-start.7 = (f32[2,1024]{1,0:T(2,128)S(1)}, f32[2,1024]{1,0:T(2,128)}, u32[]{:S(2)}) copy-start(f32[2,1024]{1,0:T(2,128)} %gain.7) | copy-start | bytes 24580
  22.7 2.7 %collective-permute-start.6 = (bf16[2,16,128,128]{3,2,1,0:T(8,128)(2,1)S(1)}, bf16[2,16,128,128]{3,2,1,0:T(8,128)(2,1)S(1)}, u32[]{:S(2)}, u32[]{:S(2)}) collective-permute-start(bf16[2,16,128,128]{3,2,1,0:T(8,128)(2,1)S(1)} %pad_maximum_fusion), channel_id=1, source_target_pairs={{0,2},{2,0},{4,6},{6,4},{8,10},{10,8},{12,14},{14,12},{16,18},{18,... | collective-permute-start | bytes 3145736 | tf_op jit(solution)/shard_map/ppermute | solution.py:33
  22.7 16.7 %copy-start.1 = (bf16[2,1024,1024]{2,1,0:T(8,128)(2,1)S(1)}, bf16[2,1024,1024]{2,1,0:T(8,128)(2,1)}, u32[]{:S(2)}) copy-start(bf16[2,1024,1024]{2,1,0:T(8,128)(2,1)} %w_out.7) | copy-start | bytes 12582916
  25.5 13.9 %copy-start = (bf16[2,1024,1024]{2,1,0:T(8,128)(2,1)S(1)}, bf16[2,1024,1024]{2,1,0:T(8,128)(2,1)}, u32[]{:S(2)}) copy-start(bf16[2,1024,1024]{2,1,0:T(8,128)(2,1)} %w_in.7) | copy-start | bytes 12582916
  25.5 13.9 %copy-start.4 = (bf16[2,64,1024]{2,1,0:T(8,128)(2,1)S(1)}, bf16[2,64,1024]{2,1,0:T(8,128)(2,1)}, u32[]{:S(2)}) copy-start(bf16[2,64,1024]{2,1,0:T(8,128)(2,1)} %w_up.7) | copy-start | bytes 786436
  25.5 13.9 %copy-start.8 = (s32[1,1,512]{2,1,0:T(1,128)S(1)}, s32[1,1,512]{2,1,0:T(1,128)}, u32[]{:S(2)}) copy-start(s32[1,1,512]{2,1,0:T(1,128)} %param.16) | copy-start | bytes 6148
  27.4 5.6 %collective-permute-start.7 = (bf16[2,64,512]{2,1,0:T(8,128)(2,1)S(1)}, bf16[2,64,512]{2,1,0:T(8,128)(2,1)S(1)}, u32[]{:S(2)}, u32[]{:S(2)}) collective-permute-start(bf16[2,64,512]{2,1,0:T(8,128)(2,1)S(1)} %get-tuple-element.43), channel_id=1, source_target_pairs={{0,4},{2,6},{4,0},{6,2},{8,12},{10,14},{12,8},{14,10},{16,20},{18,... | collective-permute-start | bytes 393224 | tf_op jit(solution)/shard_map/ppermute | solution.py:33
  29.0 30.7 %collective-permute-start.9 = (bf16[256,1024]{1,0:T(8,128)(2,1)S(1)}, bf16[256,1024]{1,0:T(8,128)(2,1)S(1)}, u32[]{:S(2)}, u32[]{:S(2)}) collective-permute-start(bf16[256,1024]{1,0:T(8,128)(2,1)S(1)} %slice.23), channel_id=1, source_target_pairs={{1,16},{3,18},{5,20},{7,22},{9,24},{11,26},{13,28},{15,30},{16,1},... | collective-permute-start | bytes 1572872 | tf_op jit(solution)/shard_map/ppermute | solution.py:49
  31.7 28.0 %collective-permute-start.10 = (bf16[256,1024]{1,0:T(8,128)(2,1)S(1)}, bf16[256,1024]{1,0:T(8,128)(2,1)S(1)}, u32[]{:S(2)}, u32[]{:S(2)}) collective-permute-start(bf16[256,1024]{1,0:T(8,128)(2,1)S(1)} %collective-permute-done.3), channel_id=1, source_target_pairs={{0,16},{2,18},{4,20},{6,22},{8,24},{10,26},{12,28},{14,30},{17,1},... | collective-permute-start | bytes 1572872 | tf_op jit(solution)/shard_map/ppermute | solution.py:267
  33.0 1.3 %collective-permute-start.8 = (bf16[1,64,512]{2,1,0:T(8,128)(2,1)S(1)}, bf16[1,64,512]{2,1,0:T(8,128)(2,1)S(1)}, u32[]{:S(2)}, u32[]{:S(2)}) collective-permute-start(bf16[1,64,512]{2,1,0:T(8,128)(2,1)S(1)} %slice.43), channel_id=1, source_target_pairs={{0,2},{2,0},{4,6},{6,4},{8,10},{10,8},{12,14},{14,12},{16,18},{18,... | collective-permute-start | bytes 196616 | tf_op jit(solution)/shard_map/ppermute | solution.py:33
  34.4 26.0 %collective-permute-start.11 = (bf16[64,512]{1,0:T(8,128)(2,1)S(1)}, bf16[64,512]{1,0:T(8,128)(2,1)S(1)}, u32[]{:S(2)}, u32[]{:S(2)}) collective-permute-start(bf16[64,512]{1,0:T(8,128)(2,1)S(1)} %fusion.2.agg_t), channel_id=1, source_target_pairs={{1,16},{3,18},{5,20},{7,22},{9,24},{11,26},{13,28},{15,30},{16,1},... | collective-permute-start | bytes 196616 | tf_op jit(solution)/shard_map/ppermute | solution.py:49
  60.4 8.3 %collective-permute-start.12 = (bf16[64,512]{1,0:T(8,128)(2,1)S(1)}, bf16[64,512]{1,0:T(8,128)(2,1)S(1)}, u32[]{:S(2)}, u32[]{:S(2)}) collective-permute-start(bf16[64,512]{1,0:T(8,128)(2,1)S(1)} %get-tuple-element.55.u_t), channel_id=1, source_target_pairs={{1,16},{3,18},{5,20},{7,22},{9,24},{11,26},{13,28},{15,30},{16,1},... | collective-permute-start | bytes 196616 | tf_op jit(solution)/shard_map/ppermute | solution.py:49
  68.7 5.2 %collective-permute-start.13 = (bf16[1,64,512]{2,1,0:T(8,128)(2,1)S(1)}, bf16[1,64,512]{2,1,0:T(8,128)(2,1)S(1)}, u32[]{:S(2)}, u32[]{:S(2)}) collective-permute-start(bf16[1,64,512]{2,1,0:T(8,128)(2,1)S(1)} %bitcast.25), channel_id=1, source_target_pairs={{0,16},{2,18},{4,20},{6,22},{8,24},{10,26},{12,28},{14,30},{16,0},... | collective-permute-start | bytes 196616 | tf_op jit(solution)/shard_map/ppermute | solution.py:33
  74.0 5.0 %collective-permute-start.14 = (bf16[2,64,512]{2,1,0:T(8,128)(2,1)S(1)}, bf16[2,64,512]{2,1,0:T(8,128)(2,1)S(1)}, u32[]{:S(2)}, u32[]{:S(2)}) collective-permute-start(bf16[2,64,512]{2,1,0:T(8,128)(2,1)S(1)} %pad_maximum_fusion.4), channel_id=1, source_target_pairs={{0,8},{2,10},{4,12},{6,14},{8,0},{10,2},{12,4},{14,6},{16,24},{18,... | collective-permute-start | bytes 393224 | tf_op jit(solution)/shard_map/ppermute | solution.py:33
  80.9 5.0 %collective-permute-start.15 = (bf16[2,64,512]{2,1,0:T(8,128)(2,1)S(1)}, bf16[2,64,512]{2,1,0:T(8,128)(2,1)S(1)}, u32[]{:S(2)}, u32[]{:S(2)}) collective-permute-start(bf16[2,64,512]{2,1,0:T(8,128)(2,1)S(1)} %get-tuple-element.59), channel_id=1, source_target_pairs={{0,4},{2,6},{4,0},{6,2},{8,12},{10,14},{12,8},{14,10},{16,20},{18,... | collective-permute-start | bytes 393224 | tf_op jit(solution)/shard_map/ppermute | solution.py:33
  86.0 1.3 %collective-permute-start.16 = (bf16[1,64,512]{2,1,0:T(8,128)(2,1)S(1)}, bf16[1,64,512]{2,1,0:T(8,128)(2,1)S(1)}, u32[]{:S(2)}, u32[]{:S(2)}) collective-permute-start(bf16[1,64,512]{2,1,0:T(8,128)(2,1)S(1)} %slice.42), channel_id=1, source_target_pairs={{0,2},{2,0},{4,6},{6,4},{8,10},{10,8},{12,14},{14,12},{16,18},{18,... | collective-permute-start | bytes 196616 | tf_op jit(solution)/shard_map/ppermute | solution.py:33
  87.3 9.4 %collective-permute-start.17 = (bf16[64,512]{1,0:T(8,128)(2,1)S(1)}, bf16[64,512]{1,0:T(8,128)(2,1)S(1)}, u32[]{:S(2)}, u32[]{:S(2)}) collective-permute-start(bf16[64,512]{1,0:T(8,128)(2,1)S(1)} %fusion.3.agg_t), channel_id=1, source_target_pairs={{1,16},{3,18},{5,20},{7,22},{9,24},{11,26},{13,28},{15,30},{16,1},... | collective-permute-start | bytes 196616 | tf_op jit(solution)/shard_map/ppermute | solution.py:49

commit v4 on v3

v4 whole, which is shorter than its diff:
```python
import functools

import jax
import jax.numpy as jnp
from jax import lax
from jax.experimental import pallas as pl
from jax.experimental.pallas import tpu as pltpu
from jax.sharding import PartitionSpec as P

BLK = 128
LAYERS = 2
ROWS = 256
EARLY = 12
PROJECT_FLOPS = 10 * 1153 * 10**6
MIB = 2**20
F32 = jnp.float32
BF16 = jnp.bfloat16


def dot(x, y):
    return jnp.dot(x, y, preferred_element_type=F32)


def dot_nt(x, y):
    return lax.dot_general(x, y, (((1,), (1,)), ((), ())), preferred_element_type=F32)


def hop(values, bit):
    size = lax.axis_size("src")
    return lax.ppermute(values, "src", [(i, i ^ bit) for i in range(size)])


def mirror_pairs():
    groups = lax.axis_size("tgt")
    copies = lax.axis_size("src") // groups
    pairs = []
    for p in range(groups * copies):
        a, r = divmod(p, copies)
        for q in range(groups):
            if a != q:
                pairs.append((p * groups + q, (q * copies + r) * groups + a))
    return pairs


def to_mirror(values):
    return lax.ppermute(values, ("src", "tgt"), mirror_pairs())


def call(body, name, outs, scalars, arrays, scratch=(), flops=0, limit=12):
    smem = pl.BlockSpec(memory_space=pltpu.SMEM)
    vmem = pl.BlockSpec(memory_space=pltpu.VMEM)
    return pl.pallas_call(
        body,
        in_specs=[smem] * len(scalars) + [vmem] * len(arrays),
        out_specs=[vmem] * len(outs),
        scratch_shapes=list(scratch),
        out_shape=list(outs),
        name=name,
        compiler_params=pltpu.CompilerParams(vmem_limit_bytes=limit * MIB),
        cost_estimate=pl.CostEstimate(flops=flops, bytes_accessed=0, transcendentals=0),
    )(*scalars, *arrays)


def reverse_column(reverse_row):
    return jnp.broadcast_to(reverse_row[...], (8, reverse_row.shape[1])).T[:, :1]


def own_mirror():
    copies = lax.axis_size("src") // lax.axis_size("tgt")
    return lax.axis_index("src") // copies == lax.axis_index("tgt")


def like(shape, dtype):
    return jax.ShapeDtypeStruct(shape, dtype)


def project_body(w_proj_t, state, out, *parts):
    out[...] = dot_nt(w_proj_t[0], state[...]).astype(BF16)
    start = 0
    for part in parts:
        part[...] = state[pl.ds(start, part.shape[0]), :]
        start += part.shape[0]


def project(w_proj_t, state, sizes):
    width, features = w_proj_t.shape[1:]
    return call(
        project_body,
        "project",
        [like((width, state.shape[0]), BF16)] + [like((n, features), BF16) for n in sizes],
        [],
        [w_proj_t, state],
        limit=8,
        flops=PROJECT_FLOPS,
    )


def add_blocks(index, slots, blocks, pool, add):
    mine = lax.axis_index("src")

    def one(slot, carry):
        source = index[slots + slot]
        relative = (source // blocks) ^ mine
        tile = jnp.int32(0)
        place, bit = 1, lax.axis_size("src") // 2
        while place < pool.shape[0]:
            tile = tile + jnp.where((relative & bit) != 0, place, 0)
            place, bit = place * 2, bit // 2
        start = pl.multiple_of((source % blocks) * BLK, BLK)
        into = pl.multiple_of(index[slot] * BLK, BLK)

        @pl.when((relative & 1) == 0)
        def _():
            add(slot, pool[tile, :, pl.ds(start, BLK)], into)

        return carry

    lax.fori_loop(0, jnp.minimum(index[2 * slots], slots), one, 0)


def triplet_body(blocks, own_index, other_index, pool, own_coeffs, other_coeffs, kept, sent, acc):
    acc[...] = jnp.zeros_like(acc)
    for tile, (index, coeffs) in enumerate(
        [(own_index, own_coeffs), (other_index, other_coeffs)]
    ):

        def add(slot, rows, into):
            acc[tile, :, pl.ds(into, BLK)] += dot(rows, coeffs[slot])

        add_blocks(index, coeffs.shape[0], blocks, pool, add)
    kept[...] = acc[0]
    sent[...] = acc[1].astype(BF16)


def triplet_partials(index, pool, coeffs):
    width, edges = pool.shape[1:]
    return call(
        functools.partial(triplet_body, edges // BLK),
        "triplets",
        [like((width, edges), F32), like((width, edges), BF16)],
        index,
        [pool] + coeffs,
        scratch=[pltpu.VMEM((2, width, edges), F32)],
        limit=8,
    )


def branch_of(x, agg, w_up, w_in, w_out, gain):
    summed = x.astype(F32) + dot(agg, w_up[...])
    scale_inv = lax.rsqrt(jnp.mean(summed * summed, axis=-1, keepdims=True) + 1e-06)
    normed = (gain[...] * summed * scale_inv).astype(BF16)
    u = dot(normed, w_in[...])
    activated = (u / (1.0 + jnp.exp(-u))).astype(BF16)
    return summed, dot(activated, w_out[...]).astype(BF16)


def chunks(edges):
    step = min(ROWS, edges)
    return [pl.ds(i, step) for i in range(0, edges, step)]


def weights_of(layer_index, w_up, w_in, w_out, gain):
    return [w.at[layer_index] for w in (w_up, w_in, w_out)] + [gain.at[pl.ds(layer_index, 1)]]


def picking(column, rows, edges):
    lanes = lax.broadcasted_iota(jnp.int32, (rows.size, edges), 1)
    return (column[rows.start : rows.start + rows.size] == lanes).astype(BF16)


def first_body(w_up, w_in, w_out, gain, w_proj_t, agg_t, reverse, *rest):
    weights = weights_of(0, w_up, w_in, w_out, gain)
    agg = agg_t[...].astype(F32).T.astype(BF16)
    w_next = w_proj_t[1]
    *parts, total, branch, v_t, u_t = rest
    state = jnp.concatenate([part[...] for part in parts], axis=0)
    edges = state.shape[0]
    for rows in chunks(edges):
        summed, out = branch_of(state[rows.start : rows.start + rows.size], agg[rows.start : rows.start + rows.size], *weights)
        branch[rows, :] = out
        total[rows, :] = summed + out.astype(F32)
    u = dot_nt(w_next, branch[...]).astype(BF16)
    at = lax.broadcasted_iota(jnp.int32, (edges, edges), 0)
    turned = dot_nt(u, (reverse[...] == at).astype(BF16))
    v = dot_nt(w_next, total[...].astype(BF16))
    u_t[...] = turned.astype(BF16)
    v_t[...] = jnp.where(own_mirror(), v + turned, v).astype(BF16)


def combine_body(v_t, u_mirror, out):
    v = v_t[...].astype(F32)
    out[0] = jnp.where(own_mirror(), v, v + u_mirror[...].astype(F32)).astype(BF16)


def combine_pair_body(v_t, v_other, u_mirror, u_across, out):
    v, other = v_t[...].astype(F32), v_other[...].astype(F32)
    here = own_mirror()
    out[0] = jnp.where(here, v, v + u_mirror[...].astype(F32)).astype(BF16)
    out[1] = jnp.where(here, other + u_across[...].astype(F32), other).astype(BF16)


def second_body(
    w_up, w_in, w_out, gain, agg_t, agg_other, reverse, total, branch, *rest
):
    edges = total.shape[0]
    weights = weights_of(0, w_up, w_in, w_out, gain)
    here = own_mirror()
    *parts, state, mirrored = rest
    own, other = parts[: len(parts) // 2], parts[len(parts) // 2 :]
    source = jnp.concatenate(
        [jnp.where(here, x[...], y[...]) for x, y in zip(own, other)], axis=0
    )
    low = jnp.where(here, agg_t[...], agg_other[...])
    column = reverse_column(reverse)
    for rows in chunks(edges):
        pick = picking(column, rows, edges)
        summed, out = branch_of(dot(pick, source), dot_nt(pick, low).astype(BF16), *weights)
        state[rows, :] = (total[rows, :] + out.astype(F32)).astype(BF16)
        mirrored[rows, :] = (summed + out.astype(F32) + branch[rows, :].astype(F32)).astype(BF16)


def third_body(w_up, w_in, w_out, gain, state, agg_t, total):
    weights = weights_of(1, w_up, w_in, w_out, gain)
    agg = agg_t[...].astype(F32).T.astype(BF16)
    for rows in chunks(state.shape[0]):
        summed, out = branch_of(state[rows, :], agg[rows.start : rows.start + rows.size], *weights)
        total[rows, :] = summed + out.astype(F32)


def last_body(w_up, w_in, w_out, gain, mirrored, agg_t, agg_other, reverse, total, state):
    edges = total.shape[0]
    weights = weights_of(1, w_up, w_in, w_out, gain)
    low = jnp.where(own_mirror(), agg_t[...], agg_other[...])
    at = lax.broadcasted_iota(jnp.int32, (edges, edges), 0)
    agg = dot(low, (reverse[...] == at).astype(BF16)).T.astype(BF16)
    for rows in chunks(edges):
        summed, out = branch_of(
            mirrored[rows, :], agg[rows.start : rows.start + rows.size], *weights
        )
        state[rows, :] = (total[rows, :] + out.astype(F32)).astype(BF16)


def gather_step(held, bit):
    return jnp.concatenate([held, hop(held, bit)], axis=0)


def part_sizes(edges):
    half = edges // 2
    cut = max(16, half * EARLY // 16 // 16 * 16)
    return [cut, half - cut, cut, half - cut]


def second_route_x(values):
    groups, size = lax.axis_size("tgt"), lax.axis_size("src")
    if groups != 2:
        return values
    copies = size // groups
    pairs = [
        ((a * copies + r) * 2 + 1 - a, (a * copies + r) * 2 + a)
        for a in range(2)
        for r in range(copies)
    ]
    return lax.ppermute(values, ("src", "tgt"), pairs)


def second_route_z(turned, values):
    groups, size = lax.axis_size("tgt"), lax.axis_size("src")
    if groups != 2:
        return to_mirror(values)
    copies = size // groups
    pairs = [
        ((a * copies + r) * 2 + a, ((1 - a) * copies + r) * 2 + a)
        for a in range(2)
        for r in range(copies)
    ]
    return lax.ppermute(turned, ("src", "tgt"), pairs)


def gather_down(held, last):
    bit = lax.axis_size("src") // 2 // held.shape[0]
    while bit >= last:
        held = gather_step(held, bit)
        bit //= 2
    return held


def next_pool(v_t, u_t):
    size, groups = lax.axis_size("src"), lax.axis_size("tgt")
    u_mirror = to_mirror(u_t)
    if groups != 2:
        held = call(combine_body, "combine", [like((1,) + v_t.shape, BF16)], [], [v_t, u_mirror])[0]
        return gather_down(held, 4)
    v_other = hop(v_t, size // 2)
    copies = size // 2
    pairs = [
        ((a * copies + r) * 2 + 1 - a, (a * copies + r) * 2 + a)
        for a in range(2)
        for r in range(copies)
    ]
    u_across = lax.ppermute(u_t, ("src", "tgt"), pairs)
    held = call(
        combine_pair_body,
        "combine",
        [like((2,) + v_t.shape, BF16)],
        [],
        [v_t, v_other, u_mirror, u_across],
        limit=4,
    )[0]
    return gather_down(held, 4)


def sum_over_cores(kept, sent):
    return (kept + hop(sent, 1).astype(F32)).astype(BF16)


def local(
    edge_states,
    triplet_coeff,
    block_target,
    block_source,
    block_count,
    reverse_slot,
    w_proj,
    w_up,
    w_in,
    w_out,
    norm_gain,
):
    state0 = edge_states[0, 0]
    edges, features = state0.shape
    width = w_proj.shape[2]
    reverse = reverse_slot[0]
    w_proj_t = jnp.swapaxes(w_proj, 1, 2)
    weights = [w_up, w_in, w_out, norm_gain]

    own_index = jnp.concatenate([block_target[0, 0], block_source[0, 0], block_count[0]])
    own_coeffs = triplet_coeff[0, 0]
    index, coeffs = [own_index, hop(own_index, 1)], [own_coeffs, hop(own_coeffs, 1)]
    proj0, *parts = project(w_proj_t, state0, part_sizes(edges))
    turned = [second_route_x(part) for part in parts[2:]]
    pool = gather_down(proj0[None], 4)
    index, coeffs, direct, turned[0], pool = lax.optimization_barrier(
        (index, coeffs, parts[0], turned[0], pool)
    )
    early = [to_mirror(direct), second_route_z(turned[0], parts[2])]
    agg0 = sum_over_cores(*triplet_partials(index, gather_down(pool, 2), coeffs))
    total0, branch0, v_t, u_t = call(
        first_body,
        "first",
        [
            like((edges, features), F32),
            like((edges, features), BF16),
            like((width, edges), BF16),
            like((width, edges), BF16),
        ],
        [],
        weights + [w_proj_t, agg0, reverse] + parts,
    )
    u_t, v_t, early, turned[1] = lax.optimization_barrier((u_t, v_t, early, turned[1]))
    pool1 = next_pool(v_t, u_t)
    direct, turned[1], agg0_held, pool1 = lax.optimization_barrier(
        (parts[1], turned[1], agg0, pool1)
    )
    agg0_other = to_mirror(agg0_held)
    late = [to_mirror(direct), second_route_z(turned[1], parts[3])]
    kept, sent = triplet_partials(index, gather_down(pool1, 2), coeffs)
    agg0_other, late, sent = lax.optimization_barrier((agg0_other, late, sent))
    agg1 = sum_over_cores(kept, sent)
    agg1_other = to_mirror(agg1)
    state1, mirrored1 = call(
        second_body,
        "second",
        [like((edges, features), BF16), like((edges, features), BF16)],
        [],
        weights
        + [agg0, agg0_other, reverse, total0, branch0]
        + parts
        + [early[0], late[0], early[1], late[1]],
    )
    total1 = call(
        third_body,
        "third",
        [like((edges, features), F32)],
        [],
        weights + [state1, agg1],
    )[0]
    final = call(
        last_body,
        "last",
        [like((edges, features), BF16)],
        [],
        weights + [mirrored1, agg1, agg1_other, reverse, total1],
    )[0]
    return final[None, None]


def solution(mesh):
    return jax.shard_map(
        local,
        mesh=mesh,
        in_specs=(
            P("src", "tgt", None, None),
            P("src", "tgt", None, None, None),
            P("src", "tgt", None),
            P("src", "tgt", None),
            P("src", "tgt"),
            P("src", "tgt", None),
            P(),
            P(),
            P(),
            P(),
            P(),
        ),
        out_specs=P("src", "tgt", None, None),
        check_vma=False,
    )
```

time: 101 us -> 89.2 us (0.88)
  waiting for transfers between devices: 50.4 us -> 31.2 us
  starting transfers between devices: 25.6 us -> 34.7 us
  Pallas kernels: 20.4 us -> 19.3 us
    ppermute x4 -> x5, waiting for transfers between devices: 25 us -> 11.2 us  [to_mirror(): return lax.ppermute(values, ('src', 'tgt'), mirror_pairs())]
    ppermute x12 -> x10, waiting for transfers between devices: 23.2 us -> 15 us  [hop(): return lax.ppermute(values, 'src', [(i, i ^ bit) for i in range(size)])]
    ppermute x1 -> x2, starting transfers between devices: 2.47 us -> 7.14 us  [second_route_x(): return lax.ppermute(values, ('src', 'tgt'), pairs)]
    ppermute x4 -> x5, starting transfers between devices: 14.1 us -> 17.3 us  [to_mirror(): return lax.ppermute(values, ('src', 'tgt'), mirror_pairs())]
    ppermute x1 -> x2, waiting for transfers between devices: 0.01 us -> 3.09 us  [second_route_z(): return lax.ppermute(turned, ('src', 'tgt'), pairs)]
    ppermute x0 -> x1, starting transfers between devices: none -> 1.29 us  [next_pool(): u_across = lax.ppermute(u_t, ('src', 'tgt'), pairs)]
    ppermute x1 -> x2, starting transfers between devices: 1.29 us -> 2.58 us  [second_route_z(): return lax.ppermute(turned, ('src', 'tgt'), pairs)]
    ppermute x12 -> x10, starting transfers between devices: 7.72 us -> 6.45 us  [hop(): return lax.ppermute(values, 'src', [(i, i ^ bit) for i in range(size)])]
  transfers between devices with their start and end apart: 18 -> 20, of which waited for: 16 -> 11; matrix products, arithmetic and copies ran while one was open for 0% -> 0% of each run, Pallas kernels for 12% -> 17%
where the time goes in v4:
time: 89.2 us; the launch traced here: 88.7 us
  starting transfers between devices  34.7 us (39%)
  waiting for transfers between devices  31.2 us (35%)
  Pallas kernels  19.3 us (22%)
  local copies, waits for them, and re-layouts  2.21 us (2%)
  between operations  0.99 us (1%)
    pallas_call x8, Pallas kernels, call(): pl.pallas_call(body, in_specs=[smem] * len(scalars) + [vmem] * len(arrays...  19.3 us
    ppermute x5, starting transfers between devices, to_mirror(): return lax.ppermute(values, ('src', 'tgt'), mirror_pairs())  17.3 us
    ppermute x10, waiting for transfers between devices, hop(): return lax.ppermute(values, 'src', [(i, i ^ bit) for i in range(size)])  15 us
    ppermute x5, waiting for transfers between devices, to_mirror(): return lax.ppermute(values, ('src', 'tgt'), mirror_pairs())  11.2 us
    ppermute x2, starting transfers between devices, second_route_x(): return lax.ppermute(values, ('src', 'tgt'), pairs)  7.14 us
    ppermute x10, starting transfers between devices, hop(): return lax.ppermute(values, 'src', [(i, i ^ bit) for i in range(size)])  6.45 us
    ppermute x2, waiting for transfers between devices, second_route_z(): return lax.ppermute(turned, ('src', 'tgt'), pairs)  3.09 us
    ppermute x2, starting transfers between devices, second_route_z(): return lax.ppermute(turned, ('src', 'tgt'), pairs)  2.58 us
  transfers between devices with their start and end apart: 20, of which 11 were waited for; matrix products, arithmetic and copies ran while one was open for 0% of the time, Pallas kernels for 17%

profile of v4, /device:TPU:6, one launch (start us, length us, event | category | flops | bytes accessed | tf_op | source)
XLA Modules:
  0.0 88.7 jit_solution(12259806399818867752)
XLA Ops:
  0.0 0.0 collective-permute-start.1
  0.0 0.9 %copy-done.4 = bf16[2,1024,64]{1,2,0:T(8,128)(2,1)S(1)} copy-done((bf16[2,1024,64]{1,2,0:T(8,128)(2,1)S(1)}, bf16[2,1024,64]{1,2,0:T(8,128)(2,1)}, u32[]{:S(2)}) %copy-start.4) | copy-done | bytes 262168
  1.0 1.2 %copy-done.8 = bf16[1,1,512,1024]{3,2,1,0:T(8,128)(2,1)S(1)} copy-done((bf16[1,1,512,1024]{3,2,1,0:T(8,128)(2,1)S(1)}, bf16[1,1,512,1024]{3,2,1,0:T(8,128)(2,1)}, u32[]{:S(2)}) %copy-start.8) | copy-done | bytes 1048600
  2.2 0.4 project.1
  2.7 2.7 %collective-permute-start.3 = (bf16[1,64,512]{2,1,0:T(8,128)(2,1)S(1)}, bf16[1,64,512]{2,1,0:T(8,128)(2,1)S(1)}, u32[]{:S(2)}, u32[]{:S(2)}) collective-permute-start(bf16[1,64,512]{2,1,0:T(8,128)(2,1)S(1)} %bitcast.15), channel_id=1, source_target_pairs={{0,16},{2,18},{4,20},{6,22},{8,24},{10,26},{12,28},{14,30},{16,0},... | collective-permute-start | bytes 196616 | tf_op jit(solution)/shard_map/ppermute | solution.py:30
  5.3 2.5 %collective-permute-start.2 = (bf16[192,1024]{1,0:T(8,128)(2,1)S(1)}, bf16[192,1024]{1,0:T(8,128)(2,1)S(1)}, u32[]{:S(2)}, u32[]{:S(2)}) collective-permute-start(bf16[192,1024]{1,0:T(8,128)(2,1)S(1)} %get-tuple-element.41.rest_2_), channel_id=1, source_target_pairs={{1,0},{3,2},{5,4},{7,6},{9,8},{11,10},{13,12},{15,14},{16,17},{18,... | collective-permute-start | bytes 1179656 | tf_op jit(solution)/shard_map/ppermute | solution.py:263
  7.8 1.8 %collective-permute-done.3 = bf16[1,64,512]{2,1,0:T(8,128)(2,1)S(1)} collective-permute-done((bf16[1,64,512]{2,1,0:T(8,128)(2,1)S(1)}, bf16[1,64,512]{2,1,0:T(8,128)(2,1)S(1)}, u32[]{:S(2)}, u32[]{:S(2)}) %collective-permute-start.3) | collective-permute-done | bytes 65568 | tf_op jit(solution)/shard_map/ppermute | solution.py:30
  9.6 0.8 collective-permute-start.4
  11.0 0.1 pad_add_fusion.own_index
  11.1 0.0 collective-permute-start
  11.1 3.5 %collective-permute-done.4 = bf16[2,64,512]{2,1,0:T(8,128)(2,1)S(1)} collective-permute-done((bf16[2,64,512]{2,1,0:T(8,128)(2,1)S(1)}, bf16[2,64,512]{2,1,0:T(8,128)(2,1)S(1)}, u32[]{:S(2)}, u32[]{:S(2)}) %collective-permute-start.4) | collective-permute-done | bytes 131104 | tf_op jit(solution)/shard_map/ppermute | solution.py:30
  14.6 0.0 collective-permute-done.other_index
  14.7 1.9 %collective-permute-done.2 = bf16[192,1024]{1,0:T(8,128)(2,1)S(1)} collective-permute-done((bf16[192,1024]{1,0:T(8,128)(2,1)S(1)}, bf16[192,1024]{1,0:T(8,128)(2,1)S(1)}, u32[]{:S(2)}, u32[]{:S(2)}) %collective-permute-start.2) | collective-permute-done | bytes 393248 | tf_op jit(solution)/shard_map/ppermute | solution.py:263
  16.5 0.0 collective-permute-done.1.other_coeffs
  16.5 0.5 collective-permute-start.5
  17.0 3.4 %collective-permute-start.7 = (bf16[192,1024]{1,0:T(8,128)(2,1)S(1)}, bf16[192,1024]{1,0:T(8,128)(2,1)S(1)}, u32[]{:S(2)}, u32[]{:S(2)}) collective-permute-start(bf16[192,1024]{1,0:T(8,128)(2,1)S(1)} %get-tuple-element.54.rest_0_), channel_id=1, source_target_pairs={{1,16},{3,18},{5,20},{7,22},{9,24},{11,26},{13,28},{15,30},{16,1},... | collective-permute-start | bytes 1179656 | tf_op jit(solution)/shard_map/ppermute | solution.py:46
  20.5 1.3 %collective-permute-start.8 = (bf16[192,1024]{1,0:T(8,128)(2,1)S(1)}, bf16[192,1024]{1,0:T(8,128)(2,1)S(1)}, u32[]{:S(2)}, u32[]{:S(2)}) collective-permute-start(bf16[192,1024]{1,0:T(8,128)(2,1)S(1)} %collective-permute-done.2), channel_id=1, source_target_pairs={{0,16},{2,18},{4,20},{6,22},{8,24},{10,26},{12,28},{14,30},{17,1},... | collective-permute-start | bytes 1179656 | tf_op jit(solution)/shard_map/ppermute | solution.py:276
  21.8 2.4 %collective-permute-done.5 = bf16[4,64,512]{2,1,0:T(8,128)(2,1)S(1)} collective-permute-done((bf16[4,64,512]{2,1,0:T(8,128)(2,1)S(1)}, bf16[4,64,512]{2,1,0:T(8,128)(2,1)S(1)}, u32[]{:S(2)}, u32[]{:S(2)}) %collective-permute-start.5) | collective-permute-done | bytes 262176 | tf_op jit(solution)/shard_map/ppermute | solution.py:30
  24.2 1.2 %triplets.2 = (f32[64,512]{1,0:T(8,128)S(1)}, bf16[64,512]{1,0:T(8,128)(2,1)S(1)}) custom-call(s32[33]{0:T(128)S(1)} %pad_add_fusion.own_index, s32[33]{0:T(128)S(1)} %collective-permute-done.other_index, bf16[8,64,512]{2,1,0:T(8,128)(2,1)S(1)} %pad_maximum_fusion.pool, bf16[16,128,128]{2,1,0:T(8,128)(2,1)S(1)} %bitcast.11, ...), custom_call_target="tpu_custom_call" | custom-call | tf_op jit(solution)/shard_map/triplets/pallas_call | solution.py:52
  25.4 0.1 collective-permute-start.6
  25.4 4.7 %collective-permute-start.9 = (bf16[64,1024]{1,0:T(8,128)(2,1)S(1)}, bf16[64,1024]{1,0:T(8,128)(2,1)S(1)}, u32[]{:S(2)}, u32[]{:S(2)}) collective-permute-start(bf16[64,1024]{1,0:T(8,128)(2,1)S(1)} %get-tuple-element.51.rest_3_), channel_id=1, source_target_pairs={{1,0},{3,2},{5,4},{7,6},{9,8},{11,10},{13,12},{15,14},{16,17},{18,... | collective-permute-start | bytes 393224 | tf_op jit(solution)/shard_map/ppermute | solution.py:263
  30.1 0.0 collective-permute-done.6
  30.2 3.9 %first.1 = (f32[512,1024]{1,0:T(8,128)S(1)}, bf16[512,1024]{1,0:T(8,128)(2,1)S(1)}, bf16[64,512]{1,0:T(8,128)(2,1)S(1)}, bf16[64,512]{1,0:T(8,128)(2,1)S(1)}) custom-call(bf16[2,64,1024]{2,1,0:T(8,128)(2,1)S(1)} %copy-done.2, bf16[2,1024,1024]{2,1,0:T(8,128)(2,1)S(1)} %copy-done, bf16[2,1024,1024]{2,1,0:T(8,128)(2,1)S(1)} %copy-done.1, ...), custom_call_target="tpu_custom_call" | custom-call | tf_op jit(solution)/shard_map/first/pallas_call | solution.py:52
  34.2 0.0 collective-permute-done.9
  34.2 5.7 %collective-permute-done.7.rest_4_ = bf16[192,1024]{1,0:T(8,128)(2,1)S(1)} collective-permute-done((bf16[192,1024]{1,0:T(8,128)(2,1)S(1)}, bf16[192,1024]{1,0:T(8,128)(2,1)S(1)}, u32[]{:S(2)}, u32[]{:S(2)}) %collective-permute-start.7) | collective-permute-done | bytes 393248 | tf_op jit(solution)/shard_map/ppermute | solution.py:46
  39.9 3.1 %collective-permute-done.8.rest_6_ = bf16[192,1024]{1,0:T(8,128)(2,1)S(1)} collective-permute-done((bf16[192,1024]{1,0:T(8,128)(2,1)S(1)}, bf16[192,1024]{1,0:T(8,128)(2,1)S(1)}, u32[]{:S(2)}, u32[]{:S(2)}) %collective-permute-start.8) | collective-permute-done | bytes 393248 | tf_op jit(solution)/shard_map/ppermute | solution.py:276
  43.0 0.0 collective-permute-start.10
  43.0 1.9 %collective-permute-start.11 = (bf16[64,512]{1,0:T(8,128)(2,1)S(1)}, bf16[64,512]{1,0:T(8,128)(2,1)S(1)}, u32[]{:S(2)}, u32[]{:S(2)}) collective-permute-start(bf16[64,512]{1,0:T(8,128)(2,1)S(1)} %get-tuple-element.58), channel_id=1, source_target_pairs={{1,16},{3,18},{5,20},{7,22},{9,24},{11,26},{13,28},{15,30},{16,1},... | collective-permute-start | bytes 196616 | tf_op jit(solution)/shard_map/ppermute | solution.py:46
  44.9 1.3 %collective-permute-start.12 = (bf16[64,512]{1,0:T(8,128)(2,1)S(1)}, bf16[64,512]{1,0:T(8,128)(2,1)S(1)}, u32[]{:S(2)}, u32[]{:S(2)}) collective-permute-start(bf16[64,512]{1,0:T(8,128)(2,1)S(1)} %get-tuple-element.58), channel_id=1, source_target_pairs={{1,0},{3,2},{5,4},{7,6},{9,8},{11,10},{13,12},{15,14},{16,17},{18,... | collective-permute-start | bytes 196616 | tf_op jit(solution)/shard_map/ppermute | solution.py:300
  46.2 1.9 %collective-permute-done.10.v_other = bf16[64,512]{1,0:T(8,128)(2,1)S(1)} collective-permute-done((bf16[64,512]{1,0:T(8,128)(2,1)S(1)}, bf16[64,512]{1,0:T(8,128)(2,1)S(1)}, u32[]{:S(2)}, u32[]{:S(2)}) %collective-permute-start.10) | collective-permute-done | bytes 65568 | tf_op jit(solution)/shard_map/ppermute | solution.py:30
  48.1 2.9 %collective-permute-done.11.u_mirror = bf16[64,512]{1,0:T(8,128)(2,1)S(1)} collective-permute-done((bf16[64,512]{1,0:T(8,128)(2,1)S(1)}, bf16[64,512]{1,0:T(8,128)(2,1)S(1)}, u32[]{:S(2)}, u32[]{:S(2)}) %collective-permute-start.11) | collective-permute-done | bytes 65568 | tf_op jit(solution)/shard_map/ppermute | solution.py:46
  51.0 0.0 collective-permute-done.12.u_across
  51.0 0.1 combine.1
  51.1 0.8 collective-permute-start.13
  51.9 4.2 %collective-permute-done.13 = bf16[2,64,512]{2,1,0:T(8,128)(2,1)S(1)} collective-permute-done((bf16[2,64,512]{2,1,0:T(8,128)(2,1)S(1)}, bf16[2,64,512]{2,1,0:T(8,128)(2,1)S(1)}, u32[]{:S(2)}, u32[]{:S(2)}) %collective-permute-start.13) | collective-permute-done | bytes 131104 | tf_op jit(solution)/shard_map/ppermute | solution.py:30
  56.1 1.6 %collective-permute-start.17 = (bf16[4,64,512]{2,1,0:T(8,128)(2,1)S(1)}, bf16[4,64,512]{2,1,0:T(8,128)(2,1)S(1)}, u32[]{:S(2)}, u32[]{:S(2)}) collective-permute-start(bf16[4,64,512]{2,1,0:T(8,128)(2,1)S(1)} %pad_maximum_fusion.3), channel_id=1, source_target_pairs={{0,4},{2,6},{4,0},{6,2},{8,12},{10,14},{12,8},{14,10},{16,20},{18,... | collective-permute-start | bytes 786440 | tf_op jit(solution)/shard_map/ppermute | solution.py:30
  57.7 3.5 %collective-permute-start.15 = (bf16[64,1024]{1,0:T(8,128)(2,1)S(1)}, bf16[64,1024]{1,0:T(8,128)(2,1)S(1)}, u32[]{:S(2)}, u32[]{:S(2)}) collective-permute-start(bf16[64,1024]{1,0:T(8,128)(2,1)S(1)} %get-tuple-element.60.rest_1_), channel_id=1, source_target_pairs={{1,16},{3,18},{5,20},{7,22},{9,24},{11,26},{13,28},{15,30},{16,1},... | collective-permute-start | bytes 393224 | tf_op jit(solution)/shard_map/ppermute | solution.py:46
  61.3 1.3 %collective-permute-start.16 = (bf16[64,1024]{1,0:T(8,128)(2,1)S(1)}, bf16[64,1024]{1,0:T(8,128)(2,1)S(1)}, u32[]{:S(2)}, u32[]{:S(2)}) collective-permute-start(bf16[64,1024]{1,0:T(8,128)(2,1)S(1)} %collective-permute-done.9), channel_id=1, source_target_pairs={{0,16},{2,18},{4,20},{6,22},{8,24},{10,26},{12,28},{14,30},{17,1},... | collective-permute-start | bytes 393224 | tf_op jit(solution)/shard_map/ppermute | solution.py:276
  62.6 4.1 %collective-permute-start.14 = (bf16[64,512]{1,0:T(8,128)(2,1)S(1)}, bf16[64,512]{1,0:T(8,128)(2,1)S(1)}, u32[]{:S(2)}, u32[]{:S(2)}) collective-permute-start(bf16[64,512]{1,0:T(8,128)(2,1)S(1)} %add_convert_fusion.1.agg_t), channel_id=1, source_target_pairs={{1,16},{3,18},{5,20},{7,22},{9,24},{11,26},{13,28},{15,30},{16,1},... | collective-permute-start | bytes 196616 | tf_op jit(solution)/shard_map/ppermute | solution.py:46
  66.7 0.0 collective-permute-done.17
  66.7 1.2 %triplets.3 = (f32[64,512]{1,0:T(8,128)S(1)}, bf16[64,512]{1,0:T(8,128)(2,1)S(1)}) custom-call(s32[33]{0:T(128)S(1)} %pad_add_fusion.own_index, s32[33]{0:T(128)S(1)} %collective-permute-done.other_index, bf16[8,64,512]{2,1,0:T(8,128)(2,1)S(1)} %pad_maximum_fusion.1.pool, bf16[16,128,128]{2,1,0:T(8,128)(2,1)S(1)} %bitcast.12, ...), custom_call_target="tpu_custom_call" | custom-call | tf_op jit(solution)/shard_map/triplets/pallas_call | solution.py:52
  67.9 2.6 %collective-permute-done.14.agg_other = bf16[64,512]{1,0:T(8,128)(2,1)S(1)} collective-permute-done((bf16[64,512]{1,0:T(8,128)(2,1)S(1)}, bf16[64,512]{1,0:T(8,128)(2,1)S(1)}, u32[]{:S(2)}, u32[]{:S(2)}) %collective-permute-start.14) | collective-permute-done | bytes 65568 | tf_op jit(solution)/shard_map/ppermute | solution.py:46
  70.5 1.2 %collective-permute-done.18 = bf16[64,512]{1,0:T(8,128)(2,1)S(1)} collective-permute-done((bf16[64,512]{1,0:T(8,128)(2,1)S(1)}, bf16[64,512]{1,0:T(8,128)(2,1)S(1)}, u32[]{:S(2)}, u32[]{:S(2)}) %collective-permute-start.18) | collective-permute-done | bytes 65568 | tf_op jit(solution)/shard_map/ppermute | solution.py:30
  71.8 4.3 %collective-permute-start.19 = (bf16[64,512]{1,0:T(8,128)(2,1)S(1)}, bf16[64,512]{1,0:T(8,128)(2,1)S(1)}, u32[]{:S(2)}, u32[]{:S(2)}) collective-permute-start(bf16[64,512]{1,0:T(8,128)(2,1)S(1)} %add_convert_fusion.agg_t), channel_id=1, source_target_pairs={{1,16},{3,18},{5,20},{7,22},{9,24},{11,26},{13,28},{15,30},{16,1},... | collective-permute-start | bytes 196616 | tf_op jit(solution)/shard_map/ppermute | solution.py:46
  76.1 5.0 %second.1 = (bf16[512,1024]{1,0:T(8,128)(2,1)S(1)}, bf16[512,1024]{1,0:T(8,128)(2,1)S(1)}) custom-call(bf16[2,64,1024]{2,1,0:T(8,128)(2,1)S(1)} %copy-done.2, bf16[2,1024,1024]{2,1,0:T(8,128)(2,1)S(1)} %copy-done, bf16[2,1024,1024]{2,1,0:T(8,128)(2,1)S(1)} %copy-done.1, f32[2,1024]{1,0:T(2,128)S(1)} %copy-done.6, ...), custom_call_target="tpu_custom_call" | custom-call | tf_op jit(solution)/shard_map/second/pallas_call | solution.py:52
  81.1 3.2 %third.1.total = f32[512,1024]{1,0:T(8,128)S(1)} custom-call(bf16[2,64,1024]{2,1,0:T(8,128)(2,1)S(1)} %copy-done.2, bf16[2,1024,1024]{2,1,0:T(8,128)(2,1)S(1)} %copy-done, bf16[2,1024,1024]{2,1,0:T(8,128)(2,1)S(1)} %copy-done.1, f32[2,1024]{1,0:T(2,128)S(1)} %copy-done.6, bf16[512,1024]{1,0:T(8,128)(2,1)S(1)} %get-tuple-element.74.state, ...), custom_call_target="tpu_custom_call" | custom-call | tf_op jit(solution)/shard_map/third/pallas_call | solution.py:52
  84.3 0.0 collective-permute-done.19.agg_other
  84.3 4.4 %last.1 = bf16[512,1024]{1,0:T(8,128)(2,1)} custom-call(bf16[2,64,1024]{2,1,0:T(8,128)(2,1)S(1)} %copy-done.2, bf16[2,1024,1024]{2,1,0:T(8,128)(2,1)S(1)} %copy-done, bf16[2,1024,1024]{2,1,0:T(8,128)(2,1)S(1)} %copy-done.1, f32[2,1024]{1,0:T(2,128)S(1)} %copy-done.6, bf16[512,1024]{1,0:T(8,128)(2,1)S(1)} %get-tuple-element.71.mirrored, ...), custom_call_target="tpu_custom_call" | custom-call | tf_op jit(solution)/shard_map/last/pallas_call | solution.py:52
  (30 shorter events, 0.2 us)
Async XLA Ops:
  0.0 16.5 %collective-permute-start.1 = (bf16[16,128,128]{2,1,0:T(8,128)(2,1)}, bf16[16,128,128]{2,1,0:T(8,128)(2,1)S(1)}, u32[]{:S(2)}, u32[]{:S(2)}) collective-permute-start(bf16[16,128,128]{2,1,0:T(8,128)(2,1)} %bitcast.10), channel_id=1, source_target_pairs={{0,2},{2,0},{4,6},{6,4},{8,10},{10,8},{12,14},{14,12},{16,18},{18,... | collective-permute-start | bytes 1572872 | tf_op jit(solution)/shard_map/ppermute | solution.py:30
  0.0 1.0 %copy-start.4 = (bf16[2,1024,64]{1,2,0:T(8,128)(2,1)S(1)}, bf16[2,1024,64]{1,2,0:T(8,128)(2,1)}, u32[]{:S(2)}) copy-start(bf16[2,1024,64]{1,2,0:T(8,128)(2,1)} %param.17) | copy-start | bytes 786436
  1.0 1.2 %copy-start.8 = (bf16[1,1,512,1024]{3,2,1,0:T(8,128)(2,1)S(1)}, bf16[1,1,512,1024]{3,2,1,0:T(8,128)(2,1)}, u32[]{:S(2)}) copy-start(bf16[1,1,512,1024]{3,2,1,0:T(8,128)(2,1)} %param.11) | copy-start | bytes 3145732
  2.2 8.8 %copy-start.9 = (s32[1,1,16]{2,1,0:T(1,128)S(1)}, s32[1,1,16]{2,1,0:T(1,128)}, u32[]{:S(2)}) copy-start(s32[1,1,16]{2,1,0:T(1,128)} %param.14) | copy-start | bytes 196
  2.2 8.8 %copy-start.10 = (s32[1,1,16]{2,1,0:T(1,128)S(1)}, s32[1,1,16]{2,1,0:T(1,128)}, u32[]{:S(2)}) copy-start(s32[1,1,16]{2,1,0:T(1,128)} %param.13) | copy-start | bytes 196
  2.2 22.0 %copy-start.3 = (bf16[1,1,16,128,128]{4,3,2,1,0:T(8,128)(2,1)S(1)}, bf16[1,1,16,128,128]{4,3,2,1,0:T(8,128)(2,1)}, u32[]{:S(2)}) copy-start(bf16[1,1,16,128,128]{4,3,2,1,0:T(8,128)(2,1)} %param.12) | copy-start | bytes 1572868
  2.2 28.0 %copy-start = (bf16[2,1024,1024]{2,1,0:T(8,128)(2,1)S(1)}, bf16[2,1024,1024]{2,1,0:T(8,128)(2,1)}, u32[]{:S(2)}) copy-start(bf16[2,1024,1024]{2,1,0:T(8,128)(2,1)} %w_in.7) | copy-start | bytes 12582916
  2.2 28.0 %copy-start.1 = (bf16[2,1024,1024]{2,1,0:T(8,128)(2,1)S(1)}, bf16[2,1024,1024]{2,1,0:T(8,128)(2,1)}, u32[]{:S(2)}) copy-start(bf16[2,1024,1024]{2,1,0:T(8,128)(2,1)} %w_out.7) | copy-start | bytes 12582916
  2.2 28.0 %copy-start.2 = (bf16[2,64,1024]{2,1,0:T(8,128)(2,1)S(1)}, bf16[2,64,1024]{2,1,0:T(8,128)(2,1)}, u32[]{:S(2)}) copy-start(bf16[2,64,1024]{2,1,0:T(8,128)(2,1)} %w_up.7) | copy-start | bytes 786436
  2.2 28.0 %copy-start.5 = (bf16[2,1024,64]{1,2,0:T(8,128)(2,1)S(1)}, bf16[2,1024,64]{1,2,0:T(8,128)(2,1)}, u32[]{:S(2)}) copy-start(bf16[2,1024,64]{1,2,0:T(8,128)(2,1)} %param.17) | copy-start | bytes 786436
  2.2 28.0 %copy-start.6 = (f32[2,1024]{1,0:T(2,128)S(1)}, f32[2,1024]{1,0:T(2,128)}, u32[]{:S(2)}) copy-start(f32[2,1024]{1,0:T(2,128)} %gain.7) | copy-start | bytes 24580
  2.2 28.0 %copy-start.7 = (s32[1,1,512]{2,1,0:T(1,128)S(1)}, s32[1,1,512]{2,1,0:T(1,128)}, u32[]{:S(2)}) copy-start(s32[1,1,512]{2,1,0:T(1,128)} %param.16) | copy-start | bytes 6148
  2.7 6.9 %collective-permute-start.3 = (bf16[1,64,512]{2,1,0:T(8,128)(2,1)S(1)}, bf16[1,64,512]{2,1,0:T(8,128)(2,1)S(1)}, u32[]{:S(2)}, u32[]{:S(2)}) collective-permute-start(bf16[1,64,512]{2,1,0:T(8,128)(2,1)S(1)} %bitcast.15), channel_id=1, source_target_pairs={{0,16},{2,18},{4,20},{6,22},{8,24},{10,26},{12,28},{14,30},{16,0},... | collective-permute-start | bytes 196616 | tf_op jit(solution)/shard_map/ppermute | solution.py:30
  5.3 11.2 %collective-permute-start.2 = (bf16[192,1024]{1,0:T(8,128)(2,1)S(1)}, bf16[192,1024]{1,0:T(8,128)(2,1)S(1)}, u32[]{:S(2)}, u32[]{:S(2)}) collective-permute-start(bf16[192,1024]{1,0:T(8,128)(2,1)S(1)} %get-tuple-element.41.rest_2_), channel_id=1, source_target_pairs={{1,0},{3,2},{5,4},{7,6},{9,8},{11,10},{13,12},{15,14},{16,17},{18,... | collective-permute-start | bytes 1179656 | tf_op jit(solution)/shard_map/ppermute | solution.py:263
  9.6 5.0 %collective-permute-start.4 = (bf16[2,64,512]{2,1,0:T(8,128)(2,1)S(1)}, bf16[2,64,512]{2,1,0:T(8,128)(2,1)S(1)}, u32[]{:S(2)}, u32[]{:S(2)}) collective-permute-start(bf16[2,64,512]{2,1,0:T(8,128)(2,1)S(1)} %pad_maximum_fusion.4), channel_id=1, source_target_pairs={{0,8},{2,10},{4,12},{6,14},{8,0},{10,2},{12,4},{14,6},{16,24},{18,... | collective-permute-start | bytes 393224 | tf_op jit(solution)/shard_map/ppermute | solution.py:30
  11.1 3.6 %collective-permute-start = (s32[33]{0:T(128)S(1)}, s32[33]{0:T(128)S(1)}, u32[]{:S(2)}, u32[]{:S(2)}) collective-permute-start(s32[33]{0:T(128)S(1)} %pad_add_fusion.own_index), channel_id=1, source_target_pairs={{0,2},{2,0},{4,6},{6,4},{8,10},{10,8},{12,14},{14,12},{16,18},{18,... | collective-permute-start | bytes 404 | tf_op jit(solution)/shard_map/ppermute | solution.py:30
  16.5 7.6 %collective-permute-start.5 = (bf16[4,64,512]{2,1,0:T(8,128)(2,1)S(1)}, bf16[4,64,512]{2,1,0:T(8,128)(2,1)S(1)}, u32[]{:S(2)}, u32[]{:S(2)}) collective-permute-start(bf16[4,64,512]{2,1,0:T(8,128)(2,1)S(1)} %pad_maximum_fusion.2), channel_id=1, source_target_pairs={{0,4},{2,6},{4,0},{6,2},{8,12},{10,14},{12,8},{14,10},{16,20},{18,... | collective-permute-start | bytes 786440 | tf_op jit(solution)/shard_map/ppermute | solution.py:30
  17.0 22.8 %collective-permute-start.7 = (bf16[192,1024]{1,0:T(8,128)(2,1)S(1)}, bf16[192,1024]{1,0:T(8,128)(2,1)S(1)}, u32[]{:S(2)}, u32[]{:S(2)}) collective-permute-start(bf16[192,1024]{1,0:T(8,128)(2,1)S(1)} %get-tuple-element.54.rest_0_), channel_id=1, source_target_pairs={{1,16},{3,18},{5,20},{7,22},{9,24},{11,26},{13,28},{15,30},{16,1},... | collective-permute-start | bytes 1179656 | tf_op jit(solution)/shard_map/ppermute | solution.py:46
  20.5 22.5 %collective-permute-start.8 = (bf16[192,1024]{1,0:T(8,128)(2,1)S(1)}, bf16[192,1024]{1,0:T(8,128)(2,1)S(1)}, u32[]{:S(2)}, u32[]{:S(2)}) collective-permute-start(bf16[192,1024]{1,0:T(8,128)(2,1)S(1)} %collective-permute-done.2), channel_id=1, source_target_pairs={{0,16},{2,18},{4,20},{6,22},{8,24},{10,26},{12,28},{14,30},{17,1},... | collective-permute-start | bytes 1179656 | tf_op jit(solution)/shard_map/ppermute | solution.py:276
  25.4 4.8 %collective-permute-start.6 = (bf16[64,512]{1,0:T(8,128)(2,1)S(1)}, bf16[64,512]{1,0:T(8,128)(2,1)S(1)}, u32[]{:S(2)}, u32[]{:S(2)}) collective-permute-start(bf16[64,512]{1,0:T(8,128)(2,1)S(1)} %get-tuple-element.49), channel_id=1, source_target_pairs={{0,2},{2,0},{4,6},{6,4},{8,10},{10,8},{12,14},{14,12},{16,18},{18,... | collective-permute-start | bytes 196616 | tf_op jit(solution)/shard_map/ppermute | solution.py:30
  25.4 8.7 %collective-permute-start.9 = (bf16[64,1024]{1,0:T(8,128)(2,1)S(1)}, bf16[64,1024]{1,0:T(8,128)(2,1)S(1)}, u32[]{:S(2)}, u32[]{:S(2)}) collective-permute-start(bf16[64,1024]{1,0:T(8,128)(2,1)S(1)} %get-tuple-element.51.rest_3_), channel_id=1, source_target_pairs={{1,0},{3,2},{5,4},{7,6},{9,8},{11,10},{13,12},{15,14},{16,17},{18,... | collective-permute-start | bytes 393224 | tf_op jit(solution)/shard_map/ppermute | solution.py:263
  43.0 5.2 %collective-permute-start.10 = (bf16[64,512]{1,0:T(8,128)(2,1)S(1)}, bf16[64,512]{1,0:T(8,128)(2,1)S(1)}, u32[]{:S(2)}, u32[]{:S(2)}) collective-permute-start(bf16[64,512]{1,0:T(8,128)(2,1)S(1)} %get-tuple-element.57.v_t), channel_id=1, source_target_pairs={{0,16},{2,18},{4,20},{6,22},{8,24},{10,26},{12,28},{14,30},{16,0},... | collective-permute-start | bytes 196616 | tf_op jit(solution)/shard_map/ppermute | solution.py:30
  43.0 8.1 %collective-permute-start.11 = (bf16[64,512]{1,0:T(8,128)(2,1)S(1)}, bf16[64,512]{1,0:T(8,128)(2,1)S(1)}, u32[]{:S(2)}, u32[]{:S(2)}) collective-permute-start(bf16[64,512]{1,0:T(8,128)(2,1)S(1)} %get-tuple-element.58), channel_id=1, source_target_pairs={{1,16},{3,18},{5,20},{7,22},{9,24},{11,26},{13,28},{15,30},{16,1},... | collective-permute-start | bytes 196616 | tf_op jit(solution)/shard_map/ppermute | solution.py:46
  44.9 6.1 %collective-permute-start.12 = (bf16[64,512]{1,0:T(8,128)(2,1)S(1)}, bf16[64,512]{1,0:T(8,128)(2,1)S(1)}, u32[]{:S(2)}, u32[]{:S(2)}) collective-permute-start(bf16[64,512]{1,0:T(8,128)(2,1)S(1)} %get-tuple-element.58), channel_id=1, source_target_pairs={{1,0},{3,2},{5,4},{7,6},{9,8},{11,10},{13,12},{15,14},{16,17},{18,... | collective-permute-start | bytes 196616 | tf_op jit(solution)/shard_map/ppermute | solution.py:300
  51.1 5.0 %collective-permute-start.13 = (bf16[2,64,512]{2,1,0:T(8,128)(2,1)S(1)}, bf16[2,64,512]{2,1,0:T(8,128)(2,1)S(1)}, u32[]{:S(2)}, u32[]{:S(2)}) collective-permute-start(bf16[2,64,512]{2,1,0:T(8,128)(2,1)S(1)} %combine.1), channel_id=1, source_target_pairs={{0,8},{2,10},{4,12},{6,14},{8,0},{10,2},{12,4},{14,6},{16,24},{18,... | collective-permute-start | bytes 393224 | tf_op jit(solution)/shard_map/ppermute | solution.py:30
  56.1 10.5 %collective-permute-start.17 = (bf16[4,64,512]{2,1,0:T(8,128)(2,1)S(1)}, bf16[4,64,512]{2,1,0:T(8,128)(2,1)S(1)}, u32[]{:S(2)}, u32[]{:S(2)}) collective-permute-start(bf16[4,64,512]{2,1,0:T(8,128)(2,1)S(1)} %pad_maximum_fusion.3), channel_id=1, source_target_pairs={{0,4},{2,6},{4,0},{6,2},{8,12},{10,14},{12,8},{14,10},{16,20},{18,... | collective-permute-start | bytes 786440 | tf_op jit(solution)/shard_map/ppermute | solution.py:30
  57.7 12.8 %collective-permute-start.15 = (bf16[64,1024]{1,0:T(8,128)(2,1)S(1)}, bf16[64,1024]{1,0:T(8,128)(2,1)S(1)}, u32[]{:S(2)}, u32[]{:S(2)}) collective-permute-start(bf16[64,1024]{1,0:T(8,128)(2,1)S(1)} %get-tuple-element.60.rest_1_), channel_id=1, source_target_pairs={{1,16},{3,18},{5,20},{7,22},{9,24},{11,26},{13,28},{15,30},{16,1},... | collective-permute-start | bytes 393224 | tf_op jit(solution)/shard_map/ppermute | solution.py:46
  61.3 9.3 %collective-permute-start.16 = (bf16[64,1024]{1,0:T(8,128)(2,1)S(1)}, bf16[64,1024]{1,0:T(8,128)(2,1)S(1)}, u32[]{:S(2)}, u32[]{:S(2)}) collective-permute-start(bf16[64,1024]{1,0:T(8,128)(2,1)S(1)} %collective-permute-done.9), channel_id=1, source_target_pairs={{0,16},{2,18},{4,20},{6,22},{8,24},{10,26},{12,28},{14,30},{17,1},... | collective-permute-start | bytes 393224 | tf_op jit(solution)/shard_map/ppermute | solution.py:276
  62.6 8.0 %collective-permute-start.14 = (bf16[64,512]{1,0:T(8,128)(2,1)S(1)}, bf16[64,512]{1,0:T(8,128)(2,1)S(1)}, u32[]{:S(2)}, u32[]{:S(2)}) collective-permute-start(bf16[64,512]{1,0:T(8,128)(2,1)S(1)} %add_convert_fusion.1.agg_t), channel_id=1, source_target_pairs={{1,16},{3,18},{5,20},{7,22},{9,24},{11,26},{13,28},{15,30},{16,1},... | collective-permute-start | bytes 196616 | tf_op jit(solution)/shard_map/ppermute | solution.py:46
  70.5 1.3 %collective-permute-start.18 = (bf16[64,512]{1,0:T(8,128)(2,1)S(1)}, bf16[64,512]{1,0:T(8,128)(2,1)S(1)}, u32[]{:S(2)}, u32[]{:S(2)}) collective-permute-start(bf16[64,512]{1,0:T(8,128)(2,1)S(1)} %get-tuple-element.73), channel_id=1, source_target_pairs={{0,2},{2,0},{4,6},{6,4},{8,10},{10,8},{12,14},{14,12},{16,18},{18,... | collective-permute-start | bytes 196616 | tf_op jit(solution)/shard_map/ppermute | solution.py:30
  71.8 12.5 %collective-permute-start.19 = (bf16[64,512]{1,0:T(8,128)(2,1)S(1)}, bf16[64,512]{1,0:T(8,128)(2,1)S(1)}, u32[]{:S(2)}, u32[]{:S(2)}) collective-permute-start(bf16[64,512]{1,0:T(8,128)(2,1)S(1)} %add_convert_fusion.agg_t), channel_id=1, source_target_pairs={{1,16},{3,18},{5,20},{7,22},{9,24},{11,26},{13,28},{15,30},{16,1},... | collective-permute-start | bytes 196616 | tf_op jit(solution)/shard_map/ppermute | solution.py:46

commit v5 on v4

--- a/solution.py
+++ b/solution.py
@@ -9,8 +9,8 @@
 
 BLK = 128
 LAYERS = 2
-ROWS = 256
-EARLY = 12
+ROWS = 512
+LATE = 4
 PROJECT_FLOPS = 10 * 1153 * 10**6
 MIB = 2**20
 F32 = jnp.float32
@@ -172,7 +172,7 @@
     weights = weights_of(0, w_up, w_in, w_out, gain)
     agg = agg_t[...].astype(F32).T.astype(BF16)
     w_next = w_proj_t[1]
-    *parts, total, branch, v_t, u_t = rest
+    *parts, total, branch, v_t, u_t, late = rest
     state = jnp.concatenate([part[...] for part in parts], axis=0)
     edges = state.shape[0]
     for rows in chunks(edges):
@@ -185,6 +185,10 @@
     v = dot_nt(w_next, total[...].astype(BF16))
     u_t[...] = turned.astype(BF16)
     v_t[...] = jnp.where(own_mirror(), v + turned, v).astype(BF16)
+    rows, low = parts[1].shape[0], agg_t.shape[0] * edges // state.shape[1]
+    late[:rows, :] = parts[1][...]
+    for k in range(agg_t.shape[0] // low):
+        late[rows:, pl.ds(k * edges, edges)] = agg_t[pl.ds(k * low, low), :]
 
 
 def combine_body(v_t, u_mirror, out):
@@ -199,18 +203,23 @@
     out[1] = jnp.where(here, other + u_across[...].astype(F32), other).astype(BF16)
 
 
-def second_body(
-    w_up, w_in, w_out, gain, agg_t, agg_other, reverse, total, branch, *rest
-):
+def second_body(w_up, w_in, w_out, gain, agg_t, reverse, total, branch, *rest):
     edges = total.shape[0]
     weights = weights_of(0, w_up, w_in, w_out, gain)
     here = own_mirror()
     *parts, state, mirrored = rest
-    own, other = parts[: len(parts) // 2], parts[len(parts) // 2 :]
-    source = jnp.concatenate(
-        [jnp.where(here, x[...], y[...]) for x, y in zip(own, other)], axis=0
-    )
-    low = jnp.where(here, agg_t[...], agg_other[...])
+    own, other = parts[:3], parts[3:]
+    rows = own[1].shape[0]
+    source = jnp.where(
+        here,
+        jnp.concatenate([x[...] for x in own], axis=0),
+        jnp.concatenate([other[0][...], other[1][:rows, :], other[2][...], other[3][...]], axis=0),
+    )
+    fold = own[1].shape[1] // edges
+    agg_other = jnp.concatenate(
+        [other[1][rows:, pl.ds(k * edges, edges)] for k in range(fold)], axis=0
+    )
+    low = jnp.where(here, agg_t[...], agg_other)
     column = reverse_column(reverse)
     for rows in chunks(edges):
         pick = picking(column, rows, edges)
@@ -245,9 +254,10 @@
 
 
 def part_sizes(edges):
-    half = edges // 2
-    cut = max(16, half * EARLY // 16 // 16 * 16)
-    return [cut, half - cut, cut, half - cut]
+    unit = max(16, edges // 32)
+    late = LATE * unit
+    direct = (edges - 2 * late) // 2 - unit
+    return [direct, late, edges - late - direct]
 
 
 def second_route_x(values):
@@ -337,14 +347,15 @@
     own_coeffs = triplet_coeff[0, 0]
     index, coeffs = [own_index, hop(own_index, 1)], [own_coeffs, hop(own_coeffs, 1)]
     proj0, *parts = project(w_proj_t, state0, part_sizes(edges))
-    turned = [second_route_x(part) for part in parts[2:]]
+    turned = second_route_x(parts[2])
     pool = gather_down(proj0[None], 4)
-    index, coeffs, direct, turned[0], pool = lax.optimization_barrier(
-        (index, coeffs, parts[0], turned[0], pool)
-    )
-    early = [to_mirror(direct), second_route_z(turned[0], parts[2])]
+    index, coeffs, direct, turned, pool = lax.optimization_barrier(
+        (index, coeffs, parts[0], turned, pool)
+    )
+    cut = parts[2].shape[0] - parts[1].shape[0]
+    early = [to_mirror(direct), second_route_z(turned[:cut], parts[2][:cut])]
     agg0 = sum_over_cores(*triplet_partials(index, gather_down(pool, 2), coeffs))
-    total0, branch0, v_t, u_t = call(
+    total0, branch0, v_t, u_t, late_direct = call(
         first_body,
         "first",
         [
@@ -352,31 +363,30 @@
             like((edges, features), BF16),
             like((width, edges), BF16),
             like((width, edges), BF16),
+            like((parts[1].shape[0] + width * edges // features, features), BF16),
         ],
         [],
         weights + [w_proj_t, agg0, reverse] + parts,
     )
-    u_t, v_t, early, turned[1] = lax.optimization_barrier((u_t, v_t, early, turned[1]))
+    u_t, v_t, early = lax.optimization_barrier((u_t, v_t, early))
     pool1 = next_pool(v_t, u_t)
-    direct, turned[1], agg0_held, pool1 = lax.optimization_barrier(
-        (parts[1], turned[1], agg0, pool1)
-    )
-    agg0_other = to_mirror(agg0_held)
-    late = [to_mirror(direct), second_route_z(turned[1], parts[3])]
+    late_direct, turned, pool1 = lax.optimization_barrier((late_direct, turned, pool1))
+    late = [to_mirror(late_direct), second_route_z(turned[cut:], parts[2][cut:])]
     kept, sent = triplet_partials(index, gather_down(pool1, 2), coeffs)
-    agg0_other, late, sent = lax.optimization_barrier((agg0_other, late, sent))
+    late, sent = lax.optimization_barrier((late, sent))
     agg1 = sum_over_cores(kept, sent)
-    agg1_other = to_mirror(agg1)
     state1, mirrored1 = call(
         second_body,
         "second",
         [like((edges, features), BF16), like((edges, features), BF16)],
         [],
         weights
-        + [agg0, agg0_other, reverse, total0, branch0]
+        + [agg0, reverse, total0, branch0]
         + parts
         + [early[0], late[0], early[1], late[1]],
     )
+    agg1, state1, mirrored1 = lax.optimization_barrier((agg1, state1, mirrored1))
+    agg1_other = to_mirror(agg1)
     total1 = call(
         third_body,
         "third",

time: 89.2 us -> 87.8 us (0.984)
  starting transfers between devices: 34.7 us -> 27.3 us
  waiting for transfers between devices: 31.2 us -> 37.4 us
    ppermute x5 -> x4, waiting for transfers between devices: 11.2 us -> 15.5 us  [to_mirror(): return lax.ppermute(values, ('src', 'tgt'), mirror_pairs())]
    ppermute x2 -> x1, starting transfers between devices: 7.14 us -> 2.87 us  [second_route_x(): return lax.ppermute(values, ('src', 'tgt'), pairs)]
    ppermute x2, waiting for transfers between devices: 3.09 us -> 5.54 us  [second_route_z(): return lax.ppermute(turned, ('src', 'tgt'), pairs)]
    ppermute x2 -> x1, waiting for transfers between devices: 1.87 us -> 0.01 us  [second_route_x(): return lax.ppermute(values, ('src', 'tgt'), pairs)]
    ppermute x10, starting transfers between devices: 6.45 us -> 4.86 us  [hop(): return lax.ppermute(values, 'src', [(i, i ^ bit) for i in range(size)])]
    ppermute x5 -> x4, starting transfers between devices: 17.3 us -> 15.7 us  [to_mirror(): return lax.ppermute(values, ('src', 'tgt'), mirror_pairs())]
    ppermute x10, waiting for transfers between devices: 15 us -> 16.3 us  [hop(): return lax.ppermute(values, 'src', [(i, i ^ bit) for i in range(size)])]
  transfers between devices with their start and end apart: 20 -> 18, of which waited for: 11 -> 11; matrix products, arithmetic and copies ran while one was open for 0% -> 0% of each run, Pallas kernels for 17% -> 16%
where the time goes in v5:
time: 87.8 us; the launch traced here: 87.1 us
  waiting for transfers between devices  37.4 us (43%)
  starting transfers between devices  27.3 us (31%)
  Pallas kernels  18.8 us (21%)
  local copies, waits for them, and re-layouts  2.26 us (3%)
  between operations  1.02 us (1%)
    pallas_call x8, Pallas kernels, call(): pl.pallas_call(body, in_specs=[smem] * len(scalars) + [vmem] * len(arrays...  18.8 us
    ppermute x10, waiting for transfers between devices, hop(): return lax.ppermute(values, 'src', [(i, i ^ bit) for i in range(size)])  16.3 us
    ppermute x4, starting transfers between devices, to_mirror(): return lax.ppermute(values, ('src', 'tgt'), mirror_pairs())  15.7 us
    ppermute x4, waiting for transfers between devices, to_mirror(): return lax.ppermute(values, ('src', 'tgt'), mirror_pairs())  15.5 us
    ppermute x2, waiting for transfers between devices, second_route_z(): return lax.ppermute(turned, ('src', 'tgt'), pairs)  5.54 us
    ppermute x10, starting transfers between devices, hop(): return lax.ppermute(values, 'src', [(i, i ^ bit) for i in range(size)])  4.86 us
    ppermute x1, starting transfers between devices, second_route_x(): return lax.ppermute(values, ('src', 'tgt'), pairs)  2.87 us
    ppermute x2, starting transfers between devices, second_route_z(): return lax.ppermute(turned, ('src', 'tgt'), pairs)  2.58 us
  transfers between devices with their start and end apart: 18, of which 11 were waited for; matrix products, arithmetic and copies ran while one was open for 0% of the time, Pallas kernels for 16%

profile of v5, /device:TPU:6, one launch (start us, length us, event | category | flops | bytes accessed | tf_op | source)
XLA Modules:
  0.0 87.1 jit_solution(5481533846127572127)
XLA Ops:
  0.0 0.9 %copy-done.4 = bf16[2,1024,64]{1,2,0:T(8,128)(2,1)S(1)} copy-done((bf16[2,1024,64]{1,2,0:T(8,128)(2,1)S(1)}, bf16[2,1024,64]{1,2,0:T(8,128)(2,1)}, u32[]{:S(2)}) %copy-start.4) | copy-done | bytes 262168
  1.0 1.2 %copy-done.8 = bf16[1,1,512,1024]{3,2,1,0:T(8,128)(2,1)S(1)} copy-done((bf16[1,1,512,1024]{3,2,1,0:T(8,128)(2,1)S(1)}, bf16[1,1,512,1024]{3,2,1,0:T(8,128)(2,1)}, u32[]{:S(2)}) %copy-start.8) | copy-done | bytes 1048600
  2.2 0.4 project.1
  2.6 0.0 copy-start
  2.7 0.0 copy-start.2
  2.7 0.0 copy-start.6
  2.7 0.0 copy-start.7
  2.7 2.9 %collective-permute-start.2 = (bf16[272,1024]{1,0:T(8,128)(2,1)S(1)}, bf16[272,1024]{1,0:T(8,128)(2,1)S(1)}, u32[]{:S(2)}, u32[]{:S(2)}) collective-permute-start(bf16[272,1024]{1,0:T(8,128)(2,1)S(1)} %get-tuple-element.41.rest_2_), channel_id=1, source_target_pairs={{1,0},{3,2},{5,4},{7,6},{9,8},{11,10},{13,12},{15,14},{16,17},{18,... | collective-permute-start | bytes 1671176 | tf_op jit(solution)/shard_map/ppermute | solution.py:273
  5.6 0.1 collective-permute-start.1
  5.7 1.3 %collective-permute-start.3 = (bf16[1,64,512]{2,1,0:T(8,128)(2,1)S(1)}, bf16[1,64,512]{2,1,0:T(8,128)(2,1)S(1)}, u32[]{:S(2)}, u32[]{:S(2)}) collective-permute-start(bf16[1,64,512]{2,1,0:T(8,128)(2,1)S(1)} %bitcast.15), channel_id=1, source_target_pairs={{0,16},{2,18},{4,20},{6,22},{8,24},{10,26},{12,28},{14,30},{16,0},... | collective-permute-start | bytes 196616 | tf_op jit(solution)/shard_map/ppermute | solution.py:30
  7.0 5.5 %collective-permute-done.3 = bf16[1,64,512]{2,1,0:T(8,128)(2,1)S(1)} collective-permute-done((bf16[1,64,512]{2,1,0:T(8,128)(2,1)S(1)}, bf16[1,64,512]{2,1,0:T(8,128)(2,1)S(1)}, u32[]{:S(2)}, u32[]{:S(2)}) %collective-permute-start.3) | collective-permute-done | bytes 65568 | tf_op jit(solution)/shard_map/ppermute | solution.py:30
  12.5 0.3 collective-permute-start.4
  13.5 0.1 pad_add_fusion.own_index
  13.6 0.0 collective-permute-start
  13.6 3.9 %collective-permute-done.4 = bf16[2,64,512]{2,1,0:T(8,128)(2,1)S(1)} collective-permute-done((bf16[2,64,512]{2,1,0:T(8,128)(2,1)S(1)}, bf16[2,64,512]{2,1,0:T(8,128)(2,1)S(1)}, u32[]{:S(2)}, u32[]{:S(2)}) %collective-permute-start.4) | collective-permute-done | bytes 131104 | tf_op jit(solution)/shard_map/ppermute | solution.py:30
  17.6 0.0 collective-permute-done.other_index
  17.6 0.0 collective-permute-done.2
  17.6 0.1 collective-permute-start.5
  17.7 1.3 %collective-permute-start.8 = (bf16[208,1024]{1,0:T(8,128)(2,1)S(1)}, bf16[208,1024]{1,0:T(8,128)(2,1)S(1)}, u32[]{:S(2)}, u32[]{:S(2)}) collective-permute-start(bf16[208,1024]{1,0:T(8,128)(2,1)S(1)} %slice.6), channel_id=1, source_target_pairs={{0,16},{2,18},{4,20},{6,22},{8,24},{10,26},{12,28},{14,30},{17,1},... | collective-permute-start | bytes 1277960 | tf_op jit(solution)/shard_map/ppermute | solution.py:286
  19.0 6.0 %collective-permute-start.7 = (bf16[176,1024]{1,0:T(8,128)(2,1)S(1)}, bf16[176,1024]{1,0:T(8,128)(2,1)S(1)}, u32[]{:S(2)}, u32[]{:S(2)}) collective-permute-start(bf16[176,1024]{1,0:T(8,128)(2,1)S(1)} %get-tuple-element.55.rest_0_), channel_id=1, source_target_pairs={{1,16},{3,18},{5,20},{7,22},{9,24},{11,26},{13,28},{15,30},{16,1},... | collective-permute-start | bytes 1081352 | tf_op jit(solution)/shard_map/ppermute | solution.py:46
  25.0 0.0 collective-permute-done.5
  25.1 1.3 %triplets.2 = (f32[64,512]{1,0:T(8,128)S(1)}, bf16[64,512]{1,0:T(8,128)(2,1)S(1)}) custom-call(s32[33]{0:T(128)S(1)} %pad_add_fusion.own_index, s32[33]{0:T(128)S(1)} %collective-permute-done.other_index, bf16[8,64,512]{2,1,0:T(8,128)(2,1)S(1)} %pad_maximum_fusion.pool, bf16[16,128,128]{2,1,0:T(8,128)(2,1)S(1)} %bitcast.11, ...), custom_call_target="tpu_custom_call" | custom-call | tf_op jit(solution)/shard_map/triplets/pallas_call | solution.py:52
  26.3 0.1 collective-permute-start.6
  26.4 1.2 %collective-permute-done.6 = bf16[64,512]{1,0:T(8,128)(2,1)S(1)} collective-permute-done((bf16[64,512]{1,0:T(8,128)(2,1)S(1)}, bf16[64,512]{1,0:T(8,128)(2,1)S(1)}, u32[]{:S(2)}, u32[]{:S(2)}) %collective-permute-start.6) | collective-permute-done | bytes 65568 | tf_op jit(solution)/shard_map/ppermute | solution.py:30
  27.7 3.9 %first.1 = (f32[512,1024]{1,0:T(8,128)S(1)}, bf16[512,1024]{1,0:T(8,128)(2,1)S(1)}, bf16[64,512]{1,0:T(8,128)(2,1)S(1)}, bf16[64,512]{1,0:T(8,128)(2,1)S(1)}, bf16[96,1024]{1,0:T(8,128)(2,1)S(1)}) custom-call(bf16[2,64,1024]{2,1,0:T(8,128)(2,1)S(1)} %copy-done.2, bf16[2,1024,1024]{2,1,0:T(8,128)(2,1)S(1)} %copy-done, bf16[2,1024,1024]{2,1,0:T(8,128)(2,1)S(1)} %copy-done.1, ...), custom_call_target="tpu_custom_call" | custom-call | tf_op jit(solution)/shard_map/first/pallas_call | solution.py:52
  31.6 9.4 %collective-permute-done.7.rest_3_ = bf16[176,1024]{1,0:T(8,128)(2,1)S(1)} collective-permute-done((bf16[176,1024]{1,0:T(8,128)(2,1)S(1)}, bf16[176,1024]{1,0:T(8,128)(2,1)S(1)}, u32[]{:S(2)}, u32[]{:S(2)}) %collective-permute-start.7) | collective-permute-done | bytes 360480 | tf_op jit(solution)/shard_map/ppermute | solution.py:46
  41.0 0.4 collective-permute-done.8.rest_5_
  41.4 1.9 %collective-permute-start.10 = (bf16[64,512]{1,0:T(8,128)(2,1)S(1)}, bf16[64,512]{1,0:T(8,128)(2,1)S(1)}, u32[]{:S(2)}, u32[]{:S(2)}) collective-permute-start(bf16[64,512]{1,0:T(8,128)(2,1)S(1)} %get-tuple-element.57), channel_id=1, source_target_pairs={{1,16},{3,18},{5,20},{7,22},{9,24},{11,26},{13,28},{15,30},{16,1},... | collective-permute-start | bytes 196616 | tf_op jit(solution)/shard_map/ppermute | solution.py:46
  43.3 1.3 %collective-permute-start.11 = (bf16[64,512]{1,0:T(8,128)(2,1)S(1)}, bf16[64,512]{1,0:T(8,128)(2,1)S(1)}, u32[]{:S(2)}, u32[]{:S(2)}) collective-permute-start(bf16[64,512]{1,0:T(8,128)(2,1)S(1)} %get-tuple-element.57), channel_id=1, source_target_pairs={{1,0},{3,2},{5,4},{7,6},{9,8},{11,10},{13,12},{15,14},{16,17},{18,... | collective-permute-start | bytes 196616 | tf_op jit(solution)/shard_map/ppermute | solution.py:310
  44.6 2.0 %collective-permute-done.9.v_other = bf16[64,512]{1,0:T(8,128)(2,1)S(1)} collective-permute-done((bf16[64,512]{1,0:T(8,128)(2,1)S(1)}, bf16[64,512]{1,0:T(8,128)(2,1)S(1)}, u32[]{:S(2)}, u32[]{:S(2)}) %collective-permute-start.9) | collective-permute-done | bytes 65568 | tf_op jit(solution)/shard_map/ppermute | solution.py:30
  46.6 4.7 %collective-permute-done.10.u_mirror = bf16[64,512]{1,0:T(8,128)(2,1)S(1)} collective-permute-done((bf16[64,512]{1,0:T(8,128)(2,1)S(1)}, bf16[64,512]{1,0:T(8,128)(2,1)S(1)}, u32[]{:S(2)}, u32[]{:S(2)}) %collective-permute-start.10) | collective-permute-done | bytes 65568 | tf_op jit(solution)/shard_map/ppermute | solution.py:46
  51.3 0.1 combine.1
  51.4 1.4 %collective-permute-start.12 = (bf16[2,64,512]{2,1,0:T(8,128)(2,1)S(1)}, bf16[2,64,512]{2,1,0:T(8,128)(2,1)S(1)}, u32[]{:S(2)}, u32[]{:S(2)}) collective-permute-start(bf16[2,64,512]{2,1,0:T(8,128)(2,1)S(1)} %combine.1), channel_id=1, source_target_pairs={{0,8},{2,10},{4,12},{6,14},{8,0},{10,2},{12,4},{14,6},{16,24},{18,... | collective-permute-start | bytes 393224 | tf_op jit(solution)/shard_map/ppermute | solution.py:30
  52.7 3.7 %collective-permute-done.12 = bf16[2,64,512]{2,1,0:T(8,128)(2,1)S(1)} collective-permute-done((bf16[2,64,512]{2,1,0:T(8,128)(2,1)S(1)}, bf16[2,64,512]{2,1,0:T(8,128)(2,1)S(1)}, u32[]{:S(2)}, u32[]{:S(2)}) %collective-permute-start.12) | collective-permute-done | bytes 131104 | tf_op jit(solution)/shard_map/ppermute | solution.py:30
  56.4 1.6 %collective-permute-start.13 = (bf16[4,64,512]{2,1,0:T(8,128)(2,1)S(1)}, bf16[4,64,512]{2,1,0:T(8,128)(2,1)S(1)}, u32[]{:S(2)}, u32[]{:S(2)}) collective-permute-start(bf16[4,64,512]{2,1,0:T(8,128)(2,1)S(1)} %pad_maximum_fusion.3), channel_id=1, source_target_pairs={{0,4},{2,6},{4,0},{6,2},{8,12},{10,14},{12,8},{14,10},{16,20},{18,... | collective-permute-start | bytes 786440 | tf_op jit(solution)/shard_map/ppermute | solution.py:30
  58.0 4.0 %collective-permute-start.14 = (bf16[96,1024]{1,0:T(8,128)(2,1)S(1)}, bf16[96,1024]{1,0:T(8,128)(2,1)S(1)}, u32[]{:S(2)}, u32[]{:S(2)}) collective-permute-start(bf16[96,1024]{1,0:T(8,128)(2,1)S(1)} %get-tuple-element.60), channel_id=1, source_target_pairs={{1,16},{3,18},{5,20},{7,22},{9,24},{11,26},{13,28},{15,30},{16,1},... | collective-permute-start | bytes 589832 | tf_op jit(solution)/shard_map/ppermute | solution.py:46
  62.1 1.3 %collective-permute-start.15 = (bf16[64,1024]{1,0:T(8,128)(2,1)S(1)}, bf16[64,1024]{1,0:T(8,128)(2,1)S(1)}, u32[]{:S(2)}, u32[]{:S(2)}) collective-permute-start(bf16[64,1024]{1,0:T(8,128)(2,1)S(1)} %slice.7), channel_id=1, source_target_pairs={{0,16},{2,18},{4,20},{6,22},{8,24},{10,26},{12,28},{14,30},{17,1},... | collective-permute-start | bytes 393224 | tf_op jit(solution)/shard_map/ppermute | solution.py:286
  63.4 0.0 collective-permute-done.13
  63.5 1.3 %triplets.3 = (f32[64,512]{1,0:T(8,128)S(1)}, bf16[64,512]{1,0:T(8,128)(2,1)S(1)}) custom-call(s32[33]{0:T(128)S(1)} %pad_add_fusion.own_index, s32[33]{0:T(128)S(1)} %collective-permute-done.other_index, bf16[8,64,512]{2,1,0:T(8,128)(2,1)S(1)} %pad_maximum_fusion.1.pool, bf16[16,128,128]{2,1,0:T(8,128)(2,1)S(1)} %bitcast.12, ...), custom_call_target="tpu_custom_call" | custom-call | tf_op jit(solution)/shard_map/triplets/pallas_call | solution.py:52
  64.7 5.1 %collective-permute-done.15.rest_6_ = bf16[64,1024]{1,0:T(8,128)(2,1)S(1)} collective-permute-done((bf16[64,1024]{1,0:T(8,128)(2,1)S(1)}, bf16[64,1024]{1,0:T(8,128)(2,1)S(1)}, u32[]{:S(2)}, u32[]{:S(2)}) %collective-permute-start.15) | collective-permute-done | bytes 131104 | tf_op jit(solution)/shard_map/ppermute | solution.py:286
  69.8 0.1 collective-permute-done.14.rest_4_
  70.0 0.0 collective-permute-start.16
  70.0 4.5 %second.1 = (bf16[512,1024]{1,0:T(8,128)(2,1)S(1)}, bf16[512,1024]{1,0:T(8,128)(2,1)S(1)}) custom-call(bf16[2,64,1024]{2,1,0:T(8,128)(2,1)S(1)} %copy-done.2, bf16[2,1024,1024]{2,1,0:T(8,128)(2,1)S(1)} %copy-done, bf16[2,1024,1024]{2,1,0:T(8,128)(2,1)S(1)} %copy-done.1, f32[2,1024]{1,0:T(2,128)S(1)} %copy-done.6, ...), custom_call_target="tpu_custom_call" | custom-call | tf_op jit(solution)/shard_map/second/pallas_call | solution.py:52
  74.5 0.0 collective-permute-done.16
  74.6 3.7 %collective-permute-start.17 = (bf16[64,512]{1,0:T(8,128)(2,1)S(1)}, bf16[64,512]{1,0:T(8,128)(2,1)S(1)}, u32[]{:S(2)}, u32[]{:S(2)}) collective-permute-start(bf16[64,512]{1,0:T(8,128)(2,1)S(1)} %add_convert_fusion.agg_t), channel_id=1, source_target_pairs={{1,16},{3,18},{5,20},{7,22},{9,24},{11,26},{13,28},{15,30},{16,1},... | collective-permute-start | bytes 196616 | tf_op jit(solution)/shard_map/ppermute | solution.py:46
  78.3 3.1 %third.1.total = f32[512,1024]{1,0:T(8,128)S(1)} custom-call(bf16[2,64,1024]{2,1,0:T(8,128)(2,1)S(1)} %copy-done.2, bf16[2,1024,1024]{2,1,0:T(8,128)(2,1)S(1)} %copy-done, bf16[2,1024,1024]{2,1,0:T(8,128)(2,1)S(1)} %copy-done.1, f32[2,1024]{1,0:T(2,128)S(1)} %copy-done.6, bf16[512,1024]{1,0:T(8,128)(2,1)S(1)} %get-tuple-element.74.state, ...), custom_call_target="tpu_custom_call" | custom-call | tf_op jit(solution)/shard_map/third/pallas_call | solution.py:52
  81.4 1.3 %collective-permute-done.17.agg_other = bf16[64,512]{1,0:T(8,128)(2,1)S(1)} collective-permute-done((bf16[64,512]{1,0:T(8,128)(2,1)S(1)}, bf16[64,512]{1,0:T(8,128)(2,1)S(1)}, u32[]{:S(2)}, u32[]{:S(2)}) %collective-permute-start.17) | collective-permute-done | bytes 65568 | tf_op jit(solution)/shard_map/ppermute | solution.py:46
  82.8 4.3 %last.1 = bf16[512,1024]{1,0:T(8,128)(2,1)} custom-call(bf16[2,64,1024]{2,1,0:T(8,128)(2,1)S(1)} %copy-done.2, bf16[2,1024,1024]{2,1,0:T(8,128)(2,1)S(1)} %copy-done, bf16[2,1024,1024]{2,1,0:T(8,128)(2,1)S(1)} %copy-done.1, f32[2,1024]{1,0:T(2,128)S(1)} %copy-done.6, bf16[512,1024]{1,0:T(8,128)(2,1)S(1)} %get-tuple-element.72.mirrored, ...), custom_call_target="tpu_custom_call" | custom-call | tf_op jit(solution)/shard_map/last/pallas_call | solution.py:52
  (28 shorter events, 0.3 us)
Async XLA Ops:
  0.0 0.9 %copy-start.4 = (bf16[2,1024,64]{1,2,0:T(8,128)(2,1)S(1)}, bf16[2,1024,64]{1,2,0:T(8,128)(2,1)}, u32[]{:S(2)}) copy-start(bf16[2,1024,64]{1,2,0:T(8,128)(2,1)} %param.17) | copy-start | bytes 786436
  1.0 1.2 %copy-start.8 = (bf16[1,1,512,1024]{3,2,1,0:T(8,128)(2,1)S(1)}, bf16[1,1,512,1024]{3,2,1,0:T(8,128)(2,1)}, u32[]{:S(2)}) copy-start(bf16[1,1,512,1024]{3,2,1,0:T(8,128)(2,1)} %param.11) | copy-start | bytes 3145732
  2.2 3.4 %copy-start.3 = (bf16[1,1,16,128,128]{4,3,2,1,0:T(8,128)(2,1)S(1)}, bf16[1,1,16,128,128]{4,3,2,1,0:T(8,128)(2,1)}, u32[]{:S(2)}) copy-start(bf16[1,1,16,128,128]{4,3,2,1,0:T(8,128)(2,1)} %param.12) | copy-start | bytes 1572868
  2.2 11.3 %copy-start.9 = (s32[1,1,16]{2,1,0:T(1,128)S(1)}, s32[1,1,16]{2,1,0:T(1,128)}, u32[]{:S(2)}) copy-start(s32[1,1,16]{2,1,0:T(1,128)} %param.14) | copy-start | bytes 196
  2.2 11.3 %copy-start.10 = (s32[1,1,16]{2,1,0:T(1,128)S(1)}, s32[1,1,16]{2,1,0:T(1,128)}, u32[]{:S(2)}) copy-start(s32[1,1,16]{2,1,0:T(1,128)} %param.13) | copy-start | bytes 196
  2.2 25.5 %copy-start.1 = (bf16[2,1024,1024]{2,1,0:T(8,128)(2,1)S(1)}, bf16[2,1024,1024]{2,1,0:T(8,128)(2,1)}, u32[]{:S(2)}) copy-start(bf16[2,1024,1024]{2,1,0:T(8,128)(2,1)} %w_out.7) | copy-start | bytes 12582916
  2.2 25.5 %copy-start.5 = (bf16[2,1024,64]{1,2,0:T(8,128)(2,1)S(1)}, bf16[2,1024,64]{1,2,0:T(8,128)(2,1)}, u32[]{:S(2)}) copy-start(bf16[2,1024,64]{1,2,0:T(8,128)(2,1)} %param.17) | copy-start | bytes 786436
  2.6 25.1 %copy-start = (bf16[2,1024,1024]{2,1,0:T(8,128)(2,1)S(1)}, bf16[2,1024,1024]{2,1,0:T(8,128)(2,1)}, u32[]{:S(2)}) copy-start(bf16[2,1024,1024]{2,1,0:T(8,128)(2,1)} %w_in.7) | copy-start | bytes 12582916
  2.7 25.1 %copy-start.2 = (bf16[2,64,1024]{2,1,0:T(8,128)(2,1)S(1)}, bf16[2,64,1024]{2,1,0:T(8,128)(2,1)}, u32[]{:S(2)}) copy-start(bf16[2,64,1024]{2,1,0:T(8,128)(2,1)} %w_up.7) | copy-start | bytes 786436
  2.7 25.1 %copy-start.6 = (f32[2,1024]{1,0:T(2,128)S(1)}, f32[2,1024]{1,0:T(2,128)}, u32[]{:S(2)}) copy-start(f32[2,1024]{1,0:T(2,128)} %gain.7) | copy-start | bytes 24580
  2.7 25.1 %copy-start.7 = (s32[1,1,512]{2,1,0:T(1,128)S(1)}, s32[1,1,512]{2,1,0:T(1,128)}, u32[]{:S(2)}) copy-start(s32[1,1,512]{2,1,0:T(1,128)} %param.16) | copy-start | bytes 6148
  2.7 14.9 %collective-permute-start.2 = (bf16[272,1024]{1,0:T(8,128)(2,1)S(1)}, bf16[272,1024]{1,0:T(8,128)(2,1)S(1)}, u32[]{:S(2)}, u32[]{:S(2)}) collective-permute-start(bf16[272,1024]{1,0:T(8,128)(2,1)S(1)} %get-tuple-element.41.rest_2_), channel_id=1, source_target_pairs={{1,0},{3,2},{5,4},{7,6},{9,8},{11,10},{13,12},{15,14},{16,17},{18,... | collective-permute-start | bytes 1671176 | tf_op jit(solution)/shard_map/ppermute | solution.py:273
  5.6 12.0 %collective-permute-start.1 = (bf16[16,128,128]{2,1,0:T(8,128)(2,1)S(1)}, bf16[16,128,128]{2,1,0:T(8,128)(2,1)S(1)}, u32[]{:S(2)}, u32[]{:S(2)}) collective-permute-start(bf16[16,128,128]{2,1,0:T(8,128)(2,1)S(1)} %bitcast.10), channel_id=1, source_target_pairs={{0,2},{2,0},{4,6},{6,4},{8,10},{10,8},{12,14},{14,12},{16,18},{18,... | collective-permute-start | bytes 1572872 | tf_op jit(solution)/shard_map/ppermute | solution.py:30
  5.7 6.8 %collective-permute-start.3 = (bf16[1,64,512]{2,1,0:T(8,128)(2,1)S(1)}, bf16[1,64,512]{2,1,0:T(8,128)(2,1)S(1)}, u32[]{:S(2)}, u32[]{:S(2)}) collective-permute-start(bf16[1,64,512]{2,1,0:T(8,128)(2,1)S(1)} %bitcast.15), channel_id=1, source_target_pairs={{0,16},{2,18},{4,20},{6,22},{8,24},{10,26},{12,28},{14,30},{16,0},... | collective-permute-start | bytes 196616 | tf_op jit(solution)/shard_map/ppermute | solution.py:30
  12.5 5.0 %collective-permute-start.4 = (bf16[2,64,512]{2,1,0:T(8,128)(2,1)S(1)}, bf16[2,64,512]{2,1,0:T(8,128)(2,1)S(1)}, u32[]{:S(2)}, u32[]{:S(2)}) collective-permute-start(bf16[2,64,512]{2,1,0:T(8,128)(2,1)S(1)} %pad_maximum_fusion.4), channel_id=1, source_target_pairs={{0,8},{2,10},{4,12},{6,14},{8,0},{10,2},{12,4},{14,6},{16,24},{18,... | collective-permute-start | bytes 393224 | tf_op jit(solution)/shard_map/ppermute | solution.py:30
  13.6 4.0 %collective-permute-start = (s32[33]{0:T(128)S(1)}, s32[33]{0:T(128)S(1)}, u32[]{:S(2)}, u32[]{:S(2)}) collective-permute-start(s32[33]{0:T(128)S(1)} %pad_add_fusion.own_index), channel_id=1, source_target_pairs={{0,2},{2,0},{4,6},{6,4},{8,10},{10,8},{12,14},{14,12},{16,18},{18,... | collective-permute-start | bytes 404 | tf_op jit(solution)/shard_map/ppermute | solution.py:30
  17.6 7.4 %collective-permute-start.5 = (bf16[4,64,512]{2,1,0:T(8,128)(2,1)S(1)}, bf16[4,64,512]{2,1,0:T(8,128)(2,1)S(1)}, u32[]{:S(2)}, u32[]{:S(2)}) collective-permute-start(bf16[4,64,512]{2,1,0:T(8,128)(2,1)S(1)} %pad_maximum_fusion.2), channel_id=1, source_target_pairs={{0,4},{2,6},{4,0},{6,2},{8,12},{10,14},{12,8},{14,10},{16,20},{18,... | collective-permute-start | bytes 786440 | tf_op jit(solution)/shard_map/ppermute | solution.py:30
  17.7 23.7 %collective-permute-start.8 = (bf16[208,1024]{1,0:T(8,128)(2,1)S(1)}, bf16[208,1024]{1,0:T(8,128)(2,1)S(1)}, u32[]{:S(2)}, u32[]{:S(2)}) collective-permute-start(bf16[208,1024]{1,0:T(8,128)(2,1)S(1)} %slice.6), channel_id=1, source_target_pairs={{0,16},{2,18},{4,20},{6,22},{8,24},{10,26},{12,28},{14,30},{17,1},... | collective-permute-start | bytes 1277960 | tf_op jit(solution)/shard_map/ppermute | solution.py:286
  19.0 22.0 %collective-permute-start.7 = (bf16[176,1024]{1,0:T(8,128)(2,1)S(1)}, bf16[176,1024]{1,0:T(8,128)(2,1)S(1)}, u32[]{:S(2)}, u32[]{:S(2)}) collective-permute-start(bf16[176,1024]{1,0:T(8,128)(2,1)S(1)} %get-tuple-element.55.rest_0_), channel_id=1, source_target_pairs={{1,16},{3,18},{5,20},{7,22},{9,24},{11,26},{13,28},{15,30},{16,1},... | collective-permute-start | bytes 1081352 | tf_op jit(solution)/shard_map/ppermute | solution.py:46
  26.3 1.3 %collective-permute-start.6 = (bf16[64,512]{1,0:T(8,128)(2,1)S(1)}, bf16[64,512]{1,0:T(8,128)(2,1)S(1)}, u32[]{:S(2)}, u32[]{:S(2)}) collective-permute-start(bf16[64,512]{1,0:T(8,128)(2,1)S(1)} %get-tuple-element.49), channel_id=1, source_target_pairs={{0,2},{2,0},{4,6},{6,4},{8,10},{10,8},{12,14},{14,12},{16,18},{18,... | collective-permute-start | bytes 196616 | tf_op jit(solution)/shard_map/ppermute | solution.py:30
  41.4 5.2 %collective-permute-start.9 = (bf16[64,512]{1,0:T(8,128)(2,1)S(1)}, bf16[64,512]{1,0:T(8,128)(2,1)S(1)}, u32[]{:S(2)}, u32[]{:S(2)}) collective-permute-start(bf16[64,512]{1,0:T(8,128)(2,1)S(1)} %get-tuple-element.56.v_t), channel_id=1, source_target_pairs={{0,16},{2,18},{4,20},{6,22},{8,24},{10,26},{12,28},{14,30},{16,0},... | collective-permute-start | bytes 196616 | tf_op jit(solution)/shard_map/ppermute | solution.py:30
  41.4 9.9 %collective-permute-start.10 = (bf16[64,512]{1,0:T(8,128)(2,1)S(1)}, bf16[64,512]{1,0:T(8,128)(2,1)S(1)}, u32[]{:S(2)}, u32[]{:S(2)}) collective-permute-start(bf16[64,512]{1,0:T(8,128)(2,1)S(1)} %get-tuple-element.57), channel_id=1, source_target_pairs={{1,16},{3,18},{5,20},{7,22},{9,24},{11,26},{13,28},{15,30},{16,1},... | collective-permute-start | bytes 196616 | tf_op jit(solution)/shard_map/ppermute | solution.py:46
  43.3 8.0 %collective-permute-start.11 = (bf16[64,512]{1,0:T(8,128)(2,1)S(1)}, bf16[64,512]{1,0:T(8,128)(2,1)S(1)}, u32[]{:S(2)}, u32[]{:S(2)}) collective-permute-start(bf16[64,512]{1,0:T(8,128)(2,1)S(1)} %get-tuple-element.57), channel_id=1, source_target_pairs={{1,0},{3,2},{5,4},{7,6},{9,8},{11,10},{13,12},{15,14},{16,17},{18,... | collective-permute-start | bytes 196616 | tf_op jit(solution)/shard_map/ppermute | solution.py:310
  51.4 5.0 %collective-permute-start.12 = (bf16[2,64,512]{2,1,0:T(8,128)(2,1)S(1)}, bf16[2,64,512]{2,1,0:T(8,128)(2,1)S(1)}, u32[]{:S(2)}, u32[]{:S(2)}) collective-permute-start(bf16[2,64,512]{2,1,0:T(8,128)(2,1)S(1)} %combine.1), channel_id=1, source_target_pairs={{0,8},{2,10},{4,12},{6,14},{8,0},{10,2},{12,4},{14,6},{16,24},{18,... | collective-permute-start | bytes 393224 | tf_op jit(solution)/shard_map/ppermute | solution.py:30
  56.4 7.0 %collective-permute-start.13 = (bf16[4,64,512]{2,1,0:T(8,128)(2,1)S(1)}, bf16[4,64,512]{2,1,0:T(8,128)(2,1)S(1)}, u32[]{:S(2)}, u32[]{:S(2)}) collective-permute-start(bf16[4,64,512]{2,1,0:T(8,128)(2,1)S(1)} %pad_maximum_fusion.3), channel_id=1, source_target_pairs={{0,4},{2,6},{4,0},{6,2},{8,12},{10,14},{12,8},{14,10},{16,20},{18,... | collective-permute-start | bytes 786440 | tf_op jit(solution)/shard_map/ppermute | solution.py:30
  58.0 12.0 %collective-permute-start.14 = (bf16[96,1024]{1,0:T(8,128)(2,1)S(1)}, bf16[96,1024]{1,0:T(8,128)(2,1)S(1)}, u32[]{:S(2)}, u32[]{:S(2)}) collective-permute-start(bf16[96,1024]{1,0:T(8,128)(2,1)S(1)} %get-tuple-element.60), channel_id=1, source_target_pairs={{1,16},{3,18},{5,20},{7,22},{9,24},{11,26},{13,28},{15,30},{16,1},... | collective-permute-start | bytes 589832 | tf_op jit(solution)/shard_map/ppermute | solution.py:46
  62.1 7.8 %collective-permute-start.15 = (bf16[64,1024]{1,0:T(8,128)(2,1)S(1)}, bf16[64,1024]{1,0:T(8,128)(2,1)S(1)}, u32[]{:S(2)}, u32[]{:S(2)}) collective-permute-start(bf16[64,1024]{1,0:T(8,128)(2,1)S(1)} %slice.7), channel_id=1, source_target_pairs={{0,16},{2,18},{4,20},{6,22},{8,24},{10,26},{12,28},{14,30},{17,1},... | collective-permute-start | bytes 393224 | tf_op jit(solution)/shard_map/ppermute | solution.py:286
  70.0 4.6 %collective-permute-start.16 = (bf16[64,512]{1,0:T(8,128)(2,1)S(1)}, bf16[64,512]{1,0:T(8,128)(2,1)S(1)}, u32[]{:S(2)}, u32[]{:S(2)}) collective-permute-start(bf16[64,512]{1,0:T(8,128)(2,1)S(1)} %get-tuple-element.63), channel_id=1, source_target_pairs={{0,2},{2,0},{4,6},{6,4},{8,10},{10,8},{12,14},{14,12},{16,18},{18,... | collective-permute-start | bytes 196616 | tf_op jit(solution)/shard_map/ppermute | solution.py:30
  74.6 8.2 %collective-permute-start.17 = (bf16[64,512]{1,0:T(8,128)(2,1)S(1)}, bf16[64,512]{1,0:T(8,128)(2,1)S(1)}, u32[]{:S(2)}, u32[]{:S(2)}) collective-permute-start(bf16[64,512]{1,0:T(8,128)(2,1)S(1)} %add_convert_fusion.agg_t), channel_id=1, source_target_pairs={{1,16},{3,18},{5,20},{7,22},{9,24},{11,26},{13,28},{15,30},{16,1},... | collective-permute-start | bytes 196616 | tf_op jit(solution)/shard_map/ppermute | solution.py:46

commit v6 on v4

--- a/solution.py
+++ b/solution.py
@@ -9,9 +9,10 @@
 
 BLK = 128
 LAYERS = 2
-ROWS = 256
-EARLY = 12
+ROWS = 512
+PARTS = (4, 4)
 PROJECT_FLOPS = 10 * 1153 * 10**6
+SECOND_FLOPS = 5 * 1153 * 10**6
 MIB = 2**20
 F32 = jnp.float32
 BF16 = jnp.bfloat16
@@ -74,25 +75,34 @@
     return jax.ShapeDtypeStruct(shape, dtype)
 
 
+def by_core(on_first, on_second):
+    return jnp.where(lax.axis_index("src") % 2 == 0, on_first, on_second)
+
+
 def project_body(w_proj_t, state, out, *parts):
     out[...] = dot_nt(w_proj_t[0], state[...]).astype(BF16)
-    start = 0
-    for part in parts:
-        part[...] = state[pl.ds(start, part.shape[0]), :]
-        start += part.shape[0]
-
-
-def project(w_proj_t, state, sizes):
-    width, features = w_proj_t.shape[1:]
-    return call(
+    half, start, count = state.shape[0] // 2, 0, len(parts) // 2
+    for keep, swap in zip(parts[:count], parts[count:]):
+        rows = keep.shape[0]
+        low, high = state[pl.ds(start, rows), :], state[pl.ds(half + start, rows), :]
+        keep[...] = by_core(low, high)
+        swap[...] = by_core(high, low)
+        start += rows
+
+
+def project(w_proj_t, state):
+    width, (edges, features) = w_proj_t.shape[1], state.shape
+    sizes = [edges // 2 * part // sum(PARTS) for part in PARTS]
+    outs = call(
         project_body,
         "project",
-        [like((width, state.shape[0]), BF16)] + [like((n, features), BF16) for n in sizes],
+        [like((width, edges), BF16)] + [like((n, features), BF16) for n in sizes * 2],
         [],
         [w_proj_t, state],
         limit=8,
         flops=PROJECT_FLOPS,
     )
+    return outs[0], outs[1 : 1 + len(sizes)], outs[1 + len(sizes) :]
 
 
 def add_blocks(index, slots, blocks, pool, add):
@@ -168,15 +178,15 @@
     return (column[rows.start : rows.start + rows.size] == lanes).astype(BF16)
 
 
-def first_body(w_up, w_in, w_out, gain, w_proj_t, agg_t, reverse, *rest):
+def first_body(
+    w_up, w_in, w_out, gain, w_proj_t, agg_t, reverse, state, total, branch, v_t, u_t
+):
     weights = weights_of(0, w_up, w_in, w_out, gain)
     agg = agg_t[...].astype(F32).T.astype(BF16)
     w_next = w_proj_t[1]
-    *parts, total, branch, v_t, u_t = rest
-    state = jnp.concatenate([part[...] for part in parts], axis=0)
     edges = state.shape[0]
     for rows in chunks(edges):
-        summed, out = branch_of(state[rows.start : rows.start + rows.size], agg[rows.start : rows.start + rows.size], *weights)
+        summed, out = branch_of(state[rows, :], agg[rows.start : rows.start + rows.size], *weights)
         branch[rows, :] = out
         total[rows, :] = summed + out.astype(F32)
     u = dot_nt(w_next, branch[...]).astype(BF16)
@@ -200,16 +210,20 @@
 
 
 def second_body(
-    w_up, w_in, w_out, gain, agg_t, agg_other, reverse, total, branch, *rest
+    w_up, w_in, w_out, gain, agg_t, agg_other, reverse, total, branch, own, *rest
 ):
     edges = total.shape[0]
     weights = weights_of(0, w_up, w_in, w_out, gain)
     here = own_mirror()
-    *parts, state, mirrored = rest
-    own, other = parts[: len(parts) // 2], parts[len(parts) // 2 :]
-    source = jnp.concatenate(
-        [jnp.where(here, x[...], y[...]) for x, y in zip(own, other)], axis=0
-    )
+    *other, state, mirrored = rest
+    if len(other) == 1:
+        received = other[0][...]
+    else:
+        count = len(other) // 2
+        passed = jnp.concatenate([y[...] for y in other[count:]], axis=0)
+        routed = jnp.concatenate([x[: y.shape[0], :] for x, y in zip(other, other[count:])], axis=0)
+        received = jnp.concatenate([by_core(routed, passed), by_core(passed, routed)], axis=0)
+    source = jnp.where(here, own[...], received)
     low = jnp.where(here, agg_t[...], agg_other[...])
     column = reverse_column(reverse)
     for rows in chunks(edges):
@@ -244,36 +258,32 @@
     return jnp.concatenate([held, hop(held, bit)], axis=0)
 
 
-def part_sizes(edges):
-    half = edges // 2
-    cut = max(16, half * EARLY // 16 // 16 * 16)
-    return [cut, half - cut, cut, half - cut]
-
-
-def second_route_x(values):
-    groups, size = lax.axis_size("tgt"), lax.axis_size("src")
-    if groups != 2:
-        return values
-    copies = size // groups
-    pairs = [
-        ((a * copies + r) * 2 + 1 - a, (a * copies + r) * 2 + a)
-        for a in range(2)
-        for r in range(copies)
-    ]
-    return lax.ppermute(values, ("src", "tgt"), pairs)
-
-
-def second_route_z(turned, values):
-    groups, size = lax.axis_size("tgt"), lax.axis_size("src")
-    if groups != 2:
-        return to_mirror(values)
-    copies = size // groups
-    pairs = [
-        ((a * copies + r) * 2 + a, ((1 - a) * copies + r) * 2 + a)
-        for a in range(2)
-        for r in range(copies)
-    ]
-    return lax.ppermute(turned, ("src", "tgt"), pairs)
+def stage_routes(keep, swap):
+    message = jnp.concatenate([keep, hop(swap, 1)], axis=0)
+    copies = lax.axis_size("src") // 2
+    pairs = []
+    for a in range(2):
+        for r in range(copies):
+            row = (a * copies + r) * 2
+            pairs += [(row + 1 - a, row + a)] if r % 2 else [(row, row), (row + 1, row + 1)]
+    return lax.ppermute(message, ("src", "tgt"), pairs)
+
+
+def send_routes(staged):
+    copies = lax.axis_size("src") // 2
+    pairs = []
+    for a in range(2):
+        for r in range(copies):
+            across = (1 - a) * copies + r
+            if r % 2:
+                pairs.append(((a * copies + r) * 2 + a, across * 2 + a))
+            else:
+                pairs.append(((a * copies + r) * 2 + 1 - a, across * 2 + a))
+    return lax.ppermute(staged, ("src", "tgt"), pairs)
+
+
+def pass_on(routed):
+    return hop(routed[routed.shape[0] // 2 :], 1)
 
 
 def gather_down(held, last):
@@ -288,8 +298,7 @@
     size, groups = lax.axis_size("src"), lax.axis_size("tgt")
     u_mirror = to_mirror(u_t)
     if groups != 2:
-        held = call(combine_body, "combine", [like((1,) + v_t.shape, BF16)], [], [v_t, u_mirror])[0]
-        return gather_down(held, 4)
+        return call(combine_body, "combine", [like((1,) + v_t.shape, BF16)], [], [v_t, u_mirror])[0]
     v_other = hop(v_t, size // 2)
     copies = size // 2
     pairs = [
@@ -298,7 +307,7 @@
         for r in range(copies)
     ]
     u_across = lax.ppermute(u_t, ("src", "tgt"), pairs)
-    held = call(
+    return call(
         combine_pair_body,
         "combine",
         [like((2,) + v_t.shape, BF16)],
@@ -306,7 +315,6 @@
         [v_t, v_other, u_mirror, u_across],
         limit=4,
     )[0]
-    return gather_down(held, 4)
 
 
 def sum_over_cores(kept, sent):
@@ -336,13 +344,16 @@
     own_index = jnp.concatenate([block_target[0, 0], block_source[0, 0], block_count[0]])
     own_coeffs = triplet_coeff[0, 0]
     index, coeffs = [own_index, hop(own_index, 1)], [own_coeffs, hop(own_coeffs, 1)]
-    proj0, *parts = project(w_proj_t, state0, part_sizes(edges))
-    turned = [second_route_x(part) for part in parts[2:]]
+    paired = lax.axis_size("tgt") == 2
+    paired = lax.axis_size("tgt") == 2
+    proj0, keep, swap = project(w_proj_t, state0)
+    if paired:
+        staged = [stage_routes(x, y) for x, y in zip(keep, swap)]
+    else:
+        staged = [state0]
     pool = gather_down(proj0[None], 4)
-    index, coeffs, direct, turned[0], pool = lax.optimization_barrier(
-        (index, coeffs, parts[0], turned[0], pool)
-    )
-    early = [to_mirror(direct), second_route_z(turned[0], parts[2])]
+    index, coeffs, pool = lax.optimization_barrier((index, coeffs, pool))
+    routed = [send_routes(x) if paired else to_mirror(x) for x in staged]
     agg0 = sum_over_cores(*triplet_partials(index, gather_down(pool, 2), coeffs))
     total0, branch0, v_t, u_t = call(
         first_body,
@@ -354,29 +365,30 @@
             like((width, edges), BF16),
         ],
         [],
-        weights + [w_proj_t, agg0, reverse] + parts,
+        weights + [w_proj_t, agg0, reverse, state0],
     )
-    u_t, v_t, early, turned[1] = lax.optimization_barrier((u_t, v_t, early, turned[1]))
-    pool1 = next_pool(v_t, u_t)
-    direct, turned[1], agg0_held, pool1 = lax.optimization_barrier(
-        (parts[1], turned[1], agg0, pool1)
-    )
-    agg0_other = to_mirror(agg0_held)
-    late = [to_mirror(direct), second_route_z(turned[1], parts[3])]
-    kept, sent = triplet_partials(index, gather_down(pool1, 2), coeffs)
-    agg0_other, late, sent = lax.optimization_barrier((agg0_other, late, sent))
-    agg1 = sum_over_cores(kept, sent)
-    agg1_other = to_mirror(agg1)
+    passed = [pass_on(routed[0])] if paired else []
+    u_t, v_t, routed, passed = lax.optimization_barrier((u_t, v_t, routed, passed))
+    held1 = next_pool(v_t, u_t)
+    routed, agg0_sent, held1 = lax.optimization_barrier((routed, agg0, held1))
+    received = routed + passed + [pass_on(x) for x in routed[1:] if paired]
+    agg0_other = to_mirror(agg0_sent)
+    pool1 = gather_down(held1, 4)
+    near1 = gather_down(pool1, 2)
     state1, mirrored1 = call(
         second_body,
         "second",
         [like((edges, features), BF16), like((edges, features), BF16)],
         [],
         weights
-        + [agg0, agg0_other, reverse, total0, branch0]
-        + parts
-        + [early[0], late[0], early[1], late[1]],
+        + [agg0, agg0_other, reverse, total0, branch0, state0]
+        + received,
+        flops=SECOND_FLOPS,
     )
+    near1, state1, mirrored1 = lax.optimization_barrier((near1, state1, mirrored1))
+    kept, sent = triplet_partials(index, near1, coeffs)
+    agg1 = sum_over_cores(kept, sent)
+    agg1_other = to_mirror(agg1)
     total1 = call(
         third_body,
         "third",

time: 89.2 us -> 85.1 us (0.954)
  starting transfers between devices: 34.7 us -> 29.4 us
  waiting for transfers between devices: 31.2 us -> 32.8 us
    ppermute x4, waiting for transfers between devices: 4.97 us -> 12.6 us  [the longest x2 12.6 us: send_routes(): return lax.ppermute(staged, ('src', 'tgt'), pairs)]
    ppermute x5 -> x3, starting transfers between devices: 17.3 us -> 10.8 us  [to_mirror(): return lax.ppermute(values, ('src', 'tgt'), mirror_pairs())]
    ppermute x10 -> x14, waiting for transfers between devices: 15 us -> 11.7 us  [hop(): return lax.ppermute(values, 'src', [(i, i ^ bit) for i in range(size)])]
    ppermute x5 -> x3, waiting for transfers between devices: 11.2 us -> 8.48 us  [to_mirror(): return lax.ppermute(values, ('src', 'tgt'), mirror_pairs())]
    ppermute x4, starting transfers between devices: 9.72 us -> 10.7 us  [the longest x2 9.16 us: send_routes(): return lax.ppermute(staged, ('src', 'tgt'), pairs)]
    ppermute x10 -> x14, starting transfers between devices: 6.45 us -> 6.67 us  [hop(): return lax.ppermute(values, 'src', [(i, i ^ bit) for i in range(size)])]
    unnamed x22 -> x24, local copies, waits for them, and re-layouts: 2.21 us -> 2.22 us
  transfers between devices with their start and end apart: 20 -> 22, of which waited for: 11 -> 11; matrix products, arithmetic and copies ran while one was open for 0% -> 0% of each run, Pallas kernels for 17% -> 15%
where the time goes in v6:
time: 85.1 us; the launch traced here: 84.7 us
  waiting for transfers between devices  32.8 us (39%)
  starting transfers between devices  29.4 us (35%)
  Pallas kernels  18.9 us (22%)
  local copies, waits for them, and re-layouts  2.26 us (3%)
  between operations  1.03 us (1%)
    pallas_call x8, Pallas kernels, call(): pl.pallas_call(body, in_specs=[smem] * len(scalars) + [vmem] * len(arrays...  18.9 us
    ppermute x2, waiting for transfers between devices, send_routes(): return lax.ppermute(staged, ('src', 'tgt'), pairs)  12.6 us
    ppermute x14, waiting for transfers between devices, hop(): return lax.ppermute(values, 'src', [(i, i ^ bit) for i in range(size)])  11.7 us
    ppermute x3, starting transfers between devices, to_mirror(): return lax.ppermute(values, ('src', 'tgt'), mirror_pairs())  10.8 us
    ppermute x2, starting transfers between devices, send_routes(): return lax.ppermute(staged, ('src', 'tgt'), pairs)  9.16 us
    ppermute x3, waiting for transfers between devices, to_mirror(): return lax.ppermute(values, ('src', 'tgt'), mirror_pairs())  8.48 us
    ppermute x14, starting transfers between devices, hop(): return lax.ppermute(values, 'src', [(i, i ^ bit) for i in range(size)])  6.67 us
    unnamed x24, local copies, waits for them, and re-layouts  2.22 us
  transfers between devices with their start and end apart: 22, of which 11 were waited for; matrix products, arithmetic and copies ran while one was open for 0% of the time, Pallas kernels for 15%

profile of v6, /device:TPU:6, one launch (start us, length us, event | category | flops | bytes accessed | tf_op | source)
XLA Modules:
  0.0 84.7 jit_solution(13690886848411712123)
XLA Ops:
  0.0 1.2 %copy-done.4 = bf16[1,1,512,1024]{3,2,1,0:T(8,128)(2,1)S(1)} copy-done((bf16[1,1,512,1024]{3,2,1,0:T(8,128)(2,1)S(1)}, bf16[1,1,512,1024]{3,2,1,0:T(8,128)(2,1)}, u32[]{:S(2)}) %copy-start.4) | copy-done | bytes 1048600
  1.2 0.9 %copy-done.6 = bf16[2,1024,64]{1,2,0:T(8,128)(2,1)S(1)} copy-done((bf16[2,1024,64]{1,2,0:T(8,128)(2,1)S(1)}, bf16[2,1024,64]{1,2,0:T(8,128)(2,1)}, u32[]{:S(2)}) %copy-start.6) | copy-done | bytes 262168
  2.2 0.4 project.1
  2.6 0.0 copy-start.2
  2.7 0.0 copy-start.5
  2.7 0.0 copy-start.7
  2.7 0.0 copy-start.8
  2.7 0.1 collective-permute-start.6
  2.8 0.5 collective-permute-start.9
  3.3 1.0 %collective-permute-done.6 = bf16[128,1024]{1,0:T(8,128)(2,1)S(1)} collective-permute-done((bf16[128,1024]{1,0:T(8,128)(2,1)S(1)}, bf16[128,1024]{1,0:T(8,128)(2,1)S(1)}, u32[]{:S(2)}, u32[]{:S(2)}) %collective-permute-start.6) | collective-permute-done | bytes 262176 | tf_op jit(solution)/shard_map/ppermute | solution.py:31
  4.3 0.8 collective-permute-start.7
  5.2 1.7 %collective-permute-start.1 = (bf16[16,128,128]{2,1,0:T(8,128)(2,1)S(1)}, bf16[16,128,128]{2,1,0:T(8,128)(2,1)S(1)}, u32[]{:S(2)}, u32[]{:S(2)}) collective-permute-start(bf16[16,128,128]{2,1,0:T(8,128)(2,1)S(1)} %bitcast.10), channel_id=1, source_target_pairs={{0,2},{2,0},{4,6},{6,4},{8,10},{10,8},{12,14},{14,12},{16,18},{18,... | collective-permute-start | bytes 1572872 | tf_op jit(solution)/shard_map/ppermute | solution.py:31
  6.9 1.7 %collective-permute-start.2 = (bf16[1,64,512]{2,1,0:T(8,128)(2,1)S(1)}, bf16[1,64,512]{2,1,0:T(8,128)(2,1)S(1)}, u32[]{:S(2)}, u32[]{:S(2)}) collective-permute-start(bf16[1,64,512]{2,1,0:T(8,128)(2,1)S(1)} %bitcast.18), channel_id=1, source_target_pairs={{0,16},{2,18},{4,20},{6,22},{8,24},{10,26},{12,28},{14,30},{16,0},... | collective-permute-start | bytes 196616 | tf_op jit(solution)/shard_map/ppermute | solution.py:31
  8.6 0.7 collective-permute-start.10
  9.3 4.1 %collective-permute-done.2 = bf16[1,64,512]{2,1,0:T(8,128)(2,1)S(1)} collective-permute-done((bf16[1,64,512]{2,1,0:T(8,128)(2,1)S(1)}, bf16[1,64,512]{2,1,0:T(8,128)(2,1)S(1)}, u32[]{:S(2)}, u32[]{:S(2)}) %collective-permute-start.2) | collective-permute-done | bytes 65568 | tf_op jit(solution)/shard_map/ppermute | solution.py:31
  13.5 0.2 collective-permute-start.3
  14.4 0.1 pad_add_fusion.own_index
  14.5 0.2 collective-permute-start
  14.6 6.4 %collective-permute-start.8 = (bf16[256,1024]{1,0:T(8,128)(2,1)S(1)}, bf16[256,1024]{1,0:T(8,128)(2,1)S(1)}, u32[]{:S(2)}, u32[]{:S(2)}) collective-permute-start(bf16[256,1024]{1,0:T(8,128)(2,1)S(1)} %collective-permute-done.7), channel_id=1, source_target_pairs={{1,16},{2,18},{5,20},{6,22},{9,24},{10,26},{13,28},{14,30},{16,1},... | collective-permute-start | bytes 1572872 | tf_op jit(solution)/shard_map/ppermute | solution.py:282
  21.1 0.6 collective-permute-start.4
  21.7 2.8 %collective-permute-start.11 = (bf16[256,1024]{1,0:T(8,128)(2,1)S(1)}, bf16[256,1024]{1,0:T(8,128)(2,1)S(1)}, u32[]{:S(2)}, u32[]{:S(2)}) collective-permute-start(bf16[256,1024]{1,0:T(8,128)(2,1)S(1)} %collective-permute-done.10), channel_id=1, source_target_pairs={{1,16},{2,18},{5,20},{6,22},{9,24},{10,26},{13,28},{14,30},{16,1},... | collective-permute-start | bytes 1572872 | tf_op jit(solution)/shard_map/ppermute | solution.py:282
  24.4 3.1 %collective-permute-done.4 = bf16[4,64,512]{2,1,0:T(8,128)(2,1)S(1)} collective-permute-done((bf16[4,64,512]{2,1,0:T(8,128)(2,1)S(1)}, bf16[4,64,512]{2,1,0:T(8,128)(2,1)S(1)}, u32[]{:S(2)}, u32[]{:S(2)}) %collective-permute-start.4) | collective-permute-done | bytes 262176 | tf_op jit(solution)/shard_map/ppermute | solution.py:31
  27.6 1.3 %triplets.2 = (f32[64,512]{1,0:T(8,128)S(1)}, bf16[64,512]{1,0:T(8,128)(2,1)S(1)}) custom-call(s32[33]{0:T(128)S(1)} %pad_add_fusion.own_index, s32[33]{0:T(128)S(1)} %collective-permute-done.other_index, bf16[8,64,512]{2,1,0:T(8,128)(2,1)S(1)} %pad_maximum_fusion.pool, bf16[16,128,128]{2,1,0:T(8,128)(2,1)S(1)} %bitcast.11, ...), custom_call_target="tpu_custom_call" | custom-call | tf_op jit(solution)/shard_map/triplets/pallas_call | solution.py:53
  28.9 0.1 collective-permute-start.5
  28.9 10.5 %collective-permute-done.8.rest_0_ = bf16[256,1024]{1,0:T(8,128)(2,1)S(1)} collective-permute-done((bf16[256,1024]{1,0:T(8,128)(2,1)S(1)}, bf16[256,1024]{1,0:T(8,128)(2,1)S(1)}, u32[]{:S(2)}, u32[]{:S(2)}) %collective-permute-start.8) | collective-permute-done | bytes 524320 | tf_op jit(solution)/shard_map/ppermute | solution.py:282
  39.4 0.1 collective-permute-start.12
  39.6 3.8 %first.1 = (f32[512,1024]{1,0:T(8,128)S(1)}, bf16[512,1024]{1,0:T(8,128)(2,1)S(1)}, bf16[64,512]{1,0:T(8,128)(2,1)S(1)}, bf16[64,512]{1,0:T(8,128)(2,1)S(1)}) custom-call(bf16[2,64,1024]{2,1,0:T(8,128)(2,1)S(1)} %copy-done.2, bf16[2,1024,1024]{2,1,0:T(8,128)(2,1)S(1)} %copy-done, bf16[2,1024,1024]{2,1,0:T(8,128)(2,1)S(1)} %copy-done.1, ...), custom_call_target="tpu_custom_call" | custom-call | tf_op jit(solution)/shard_map/first/pallas_call | solution.py:53
  43.5 2.1 %collective-permute-done.11.rest_1_ = bf16[256,1024]{1,0:T(8,128)(2,1)S(1)} collective-permute-done((bf16[256,1024]{1,0:T(8,128)(2,1)S(1)}, bf16[256,1024]{1,0:T(8,128)(2,1)S(1)}, u32[]{:S(2)}, u32[]{:S(2)}) %collective-permute-start.11) | collective-permute-done | bytes 524320 | tf_op jit(solution)/shard_map/ppermute | solution.py:282
  45.5 1.9 %collective-permute-start.14 = (bf16[64,512]{1,0:T(8,128)(2,1)S(1)}, bf16[64,512]{1,0:T(8,128)(2,1)S(1)}, u32[]{:S(2)}, u32[]{:S(2)}) collective-permute-start(bf16[64,512]{1,0:T(8,128)(2,1)S(1)} %get-tuple-element.54), channel_id=1, source_target_pairs={{1,16},{3,18},{5,20},{7,22},{9,24},{11,26},{13,28},{15,30},{16,1},... | collective-permute-start | bytes 196616 | tf_op jit(solution)/shard_map/ppermute | solution.py:47
  47.5 1.3 %collective-permute-start.15 = (bf16[64,512]{1,0:T(8,128)(2,1)S(1)}, bf16[64,512]{1,0:T(8,128)(2,1)S(1)}, u32[]{:S(2)}, u32[]{:S(2)}) collective-permute-start(bf16[64,512]{1,0:T(8,128)(2,1)S(1)} %get-tuple-element.54), channel_id=1, source_target_pairs={{1,0},{3,2},{5,4},{7,6},{9,8},{11,10},{13,12},{15,14},{16,17},{18,... | collective-permute-start | bytes 196616 | tf_op jit(solution)/shard_map/ppermute | solution.py:309
  48.8 1.9 %collective-permute-done.13.v_other = bf16[64,512]{1,0:T(8,128)(2,1)S(1)} collective-permute-done((bf16[64,512]{1,0:T(8,128)(2,1)S(1)}, bf16[64,512]{1,0:T(8,128)(2,1)S(1)}, u32[]{:S(2)}, u32[]{:S(2)}) %collective-permute-start.13) | collective-permute-done | bytes 65568 | tf_op jit(solution)/shard_map/ppermute | solution.py:31
  50.7 2.9 %collective-permute-done.14.u_mirror = bf16[64,512]{1,0:T(8,128)(2,1)S(1)} collective-permute-done((bf16[64,512]{1,0:T(8,128)(2,1)S(1)}, bf16[64,512]{1,0:T(8,128)(2,1)S(1)}, u32[]{:S(2)}, u32[]{:S(2)}) %collective-permute-start.14) | collective-permute-done | bytes 65568 | tf_op jit(solution)/shard_map/ppermute | solution.py:47
  53.6 0.1 combine.1
  53.7 0.1 collective-permute-start.19
  53.8 0.9 %collective-permute-start.16 = (bf16[2,64,512]{2,1,0:T(8,128)(2,1)S(1)}, bf16[2,64,512]{2,1,0:T(8,128)(2,1)S(1)}, u32[]{:S(2)}, u32[]{:S(2)}) collective-permute-start(bf16[2,64,512]{2,1,0:T(8,128)(2,1)S(1)} %combine.1), channel_id=1, source_target_pairs={{0,8},{2,10},{4,12},{6,14},{8,0},{10,2},{12,4},{14,6},{16,24},{18,... | collective-permute-start | bytes 393224 | tf_op jit(solution)/shard_map/ppermute | solution.py:31
  54.7 4.8 %collective-permute-start.18 = (bf16[64,512]{1,0:T(8,128)(2,1)S(1)}, bf16[64,512]{1,0:T(8,128)(2,1)S(1)}, u32[]{:S(2)}, u32[]{:S(2)}) collective-permute-start(bf16[64,512]{1,0:T(8,128)(2,1)S(1)} %add_convert_fusion.1.agg_t), channel_id=1, source_target_pairs={{1,16},{3,18},{5,20},{7,22},{9,24},{11,26},{13,28},{15,30},{16,1},... | collective-permute-start | bytes 196616 | tf_op jit(solution)/shard_map/ppermute | solution.py:47
  59.4 0.3 collective-permute-done.16
  59.7 0.6 collective-permute-start.17
  60.3 3.6 %collective-permute-done.18.agg_other = bf16[64,512]{1,0:T(8,128)(2,1)S(1)} collective-permute-done((bf16[64,512]{1,0:T(8,128)(2,1)S(1)}, bf16[64,512]{1,0:T(8,128)(2,1)S(1)}, u32[]{:S(2)}, u32[]{:S(2)}) %collective-permute-start.18) | collective-permute-done | bytes 65568 | tf_op jit(solution)/shard_map/ppermute | solution.py:47
  63.9 4.6 %second.1 = (bf16[512,1024]{1,0:T(8,128)(2,1)S(1)}, bf16[512,1024]{1,0:T(8,128)(2,1)S(1)}) custom-call(bf16[2,64,1024]{2,1,0:T(8,128)(2,1)S(1)} %copy-done.2, bf16[2,1024,1024]{2,1,0:T(8,128)(2,1)S(1)} %copy-done, bf16[2,1024,1024]{2,1,0:T(8,128)(2,1)S(1)} %copy-done.1, f32[2,1024]{1,0:T(2,128)S(1)} %copy-done.8, ...), custom_call_target="tpu_custom_call" | custom-call | flops 5765000192 | tf_op jit(solution)/shard_map/second/pallas_call | solution.py:53
  68.5 0.1 pad_maximum_fusion.3.pool
  68.6 1.3 %triplets.3 = (f32[64,512]{1,0:T(8,128)S(1)}, bf16[64,512]{1,0:T(8,128)(2,1)S(1)}) custom-call(s32[33]{0:T(128)S(1)} %pad_add_fusion.own_index, s32[33]{0:T(128)S(1)} %collective-permute-done.other_index, bf16[8,64,512]{2,1,0:T(8,128)(2,1)S(1)} %pad_maximum_fusion.3.pool, bf16[16,128,128]{2,1,0:T(8,128)(2,1)S(1)} %bitcast.12, ...), custom_call_target="tpu_custom_call" | custom-call | tf_op jit(solution)/shard_map/triplets/pallas_call | solution.py:53
  69.9 0.1 collective-permute-start.20
  70.0 1.2 %collective-permute-done.20 = bf16[64,512]{1,0:T(8,128)(2,1)S(1)} collective-permute-done((bf16[64,512]{1,0:T(8,128)(2,1)S(1)}, bf16[64,512]{1,0:T(8,128)(2,1)S(1)}, u32[]{:S(2)}, u32[]{:S(2)}) %collective-permute-start.20) | collective-permute-done | bytes 65568 | tf_op jit(solution)/shard_map/ppermute | solution.py:31
  71.2 4.1 %collective-permute-start.21 = (bf16[64,512]{1,0:T(8,128)(2,1)S(1)}, bf16[64,512]{1,0:T(8,128)(2,1)S(1)}, u32[]{:S(2)}, u32[]{:S(2)}) collective-permute-start(bf16[64,512]{1,0:T(8,128)(2,1)S(1)} %add_convert_fusion.agg_t), channel_id=1, source_target_pairs={{1,16},{3,18},{5,20},{7,22},{9,24},{11,26},{13,28},{15,30},{16,1},... | collective-permute-start | bytes 196616 | tf_op jit(solution)/shard_map/ppermute | solution.py:47
  75.3 3.1 %third.1.total = f32[512,1024]{1,0:T(8,128)S(1)} custom-call(bf16[2,64,1024]{2,1,0:T(8,128)(2,1)S(1)} %copy-done.2, bf16[2,1024,1024]{2,1,0:T(8,128)(2,1)S(1)} %copy-done, bf16[2,1024,1024]{2,1,0:T(8,128)(2,1)S(1)} %copy-done.1, f32[2,1024]{1,0:T(2,128)S(1)} %copy-done.8, bf16[512,1024]{1,0:T(8,128)(2,1)S(1)} %get-tuple-element.68.state, ...), custom_call_target="tpu_custom_call" | custom-call | tf_op jit(solution)/shard_map/third/pallas_call | solution.py:53
  78.5 1.9 %collective-permute-done.21.agg_other = bf16[64,512]{1,0:T(8,128)(2,1)S(1)} collective-permute-done((bf16[64,512]{1,0:T(8,128)(2,1)S(1)}, bf16[64,512]{1,0:T(8,128)(2,1)S(1)}, u32[]{:S(2)}, u32[]{:S(2)}) %collective-permute-start.21) | collective-permute-done | bytes 65568 | tf_op jit(solution)/shard_map/ppermute | solution.py:47
  80.4 4.3 %last.1 = bf16[512,1024]{1,0:T(8,128)(2,1)} custom-call(bf16[2,64,1024]{2,1,0:T(8,128)(2,1)S(1)} %copy-done.2, bf16[2,1024,1024]{2,1,0:T(8,128)(2,1)S(1)} %copy-done, bf16[2,1024,1024]{2,1,0:T(8,128)(2,1)S(1)} %copy-done.1, f32[2,1024]{1,0:T(2,128)S(1)} %copy-done.8, bf16[512,1024]{1,0:T(8,128)(2,1)S(1)} %get-tuple-element.64.mirrored, ...), custom_call_target="tpu_custom_call" | custom-call | tf_op jit(solution)/shard_map/last/pallas_call | solution.py:53
  (40 shorter events, 0.3 us)
Async XLA Ops:
  0.0 1.2 %copy-start.4 = (bf16[1,1,512,1024]{3,2,1,0:T(8,128)(2,1)S(1)}, bf16[1,1,512,1024]{3,2,1,0:T(8,128)(2,1)}, u32[]{:S(2)}) copy-start(bf16[1,1,512,1024]{3,2,1,0:T(8,128)(2,1)} %param.11) | copy-start | bytes 3145732
  1.2 0.9 %copy-start.6 = (bf16[2,1024,64]{1,2,0:T(8,128)(2,1)S(1)}, bf16[2,1024,64]{1,2,0:T(8,128)(2,1)}, u32[]{:S(2)}) copy-start(bf16[2,1024,64]{1,2,0:T(8,128)(2,1)} %param.17) | copy-start | bytes 786436
  2.2 3.0 %copy-start.3 = (bf16[1,1,16,128,128]{4,3,2,1,0:T(8,128)(2,1)S(1)}, bf16[1,1,16,128,128]{4,3,2,1,0:T(8,128)(2,1)}, u32[]{:S(2)}) copy-start(bf16[1,1,16,128,128]{4,3,2,1,0:T(8,128)(2,1)} %param.12) | copy-start | bytes 1572868
  2.2 12.2 %copy-start.10 = (s32[1,1,16]{2,1,0:T(1,128)S(1)}, s32[1,1,16]{2,1,0:T(1,128)}, u32[]{:S(2)}) copy-start(s32[1,1,16]{2,1,0:T(1,128)} %param.14) | copy-start | bytes 196
  2.2 12.2 %copy-start.11 = (s32[1,1,16]{2,1,0:T(1,128)S(1)}, s32[1,1,16]{2,1,0:T(1,128)}, u32[]{:S(2)}) copy-start(s32[1,1,16]{2,1,0:T(1,128)} %param.13) | copy-start | bytes 196
  2.2 37.4 %copy-start.1 = (bf16[2,1024,1024]{2,1,0:T(8,128)(2,1)S(1)}, bf16[2,1024,1024]{2,1,0:T(8,128)(2,1)}, u32[]{:S(2)}) copy-start(bf16[2,1024,1024]{2,1,0:T(8,128)(2,1)} %w_out.7) | copy-start | bytes 12582916
  2.6 36.9 %copy-start = (bf16[2,1024,1024]{2,1,0:T(8,128)(2,1)S(1)}, bf16[2,1024,1024]{2,1,0:T(8,128)(2,1)}, u32[]{:S(2)}) copy-start(bf16[2,1024,1024]{2,1,0:T(8,128)(2,1)} %w_in.7) | copy-start | bytes 12582916
  2.6 36.9 %copy-start.2 = (bf16[2,64,1024]{2,1,0:T(8,128)(2,1)S(1)}, bf16[2,64,1024]{2,1,0:T(8,128)(2,1)}, u32[]{:S(2)}) copy-start(bf16[2,64,1024]{2,1,0:T(8,128)(2,1)} %w_up.7) | copy-start | bytes 786436
  2.7 36.9 %copy-start.5 = (bf16[1,1,512,1024]{3,2,1,0:T(8,128)(2,1)S(1)}, bf16[1,1,512,1024]{3,2,1,0:T(8,128)(2,1)}, u32[]{:S(2)}) copy-start(bf16[1,1,512,1024]{3,2,1,0:T(8,128)(2,1)} %param.11) | copy-start | bytes 3145732
  2.7 36.9 %copy-start.7 = (bf16[2,1024,64]{1,2,0:T(8,128)(2,1)S(1)}, bf16[2,1024,64]{1,2,0:T(8,128)(2,1)}, u32[]{:S(2)}) copy-start(bf16[2,1024,64]{1,2,0:T(8,128)(2,1)} %param.17) | copy-start | bytes 786436
  2.7 36.9 %copy-start.8 = (f32[2,1024]{1,0:T(2,128)S(1)}, f32[2,1024]{1,0:T(2,128)}, u32[]{:S(2)}) copy-start(f32[2,1024]{1,0:T(2,128)} %gain.7) | copy-start | bytes 24580
  2.7 36.9 %copy-start.9 = (s32[1,1,512]{2,1,0:T(1,128)S(1)}, s32[1,1,512]{2,1,0:T(1,128)}, u32[]{:S(2)}) copy-start(s32[1,1,512]{2,1,0:T(1,128)} %param.16) | copy-start | bytes 6148
  2.7 1.6 %collective-permute-start.6 = (bf16[128,1024]{1,0:T(8,128)(2,1)S(1)}, bf16[128,1024]{1,0:T(8,128)(2,1)S(1)}, u32[]{:S(2)}, u32[]{:S(2)}) collective-permute-start(bf16[128,1024]{1,0:T(8,128)(2,1)S(1)} %get-tuple-element.48), channel_id=1, source_target_pairs={{0,2},{2,0},{4,6},{6,4},{8,10},{10,8},{12,14},{14,12},{16,18},{18,... | collective-permute-start | bytes 786440 | tf_op jit(solution)/shard_map/ppermute | solution.py:31
  2.8 5.8 %collective-permute-start.9 = (bf16[128,1024]{1,0:T(8,128)(2,1)S(1)}, bf16[128,1024]{1,0:T(8,128)(2,1)S(1)}, u32[]{:S(2)}, u32[]{:S(2)}) collective-permute-start(bf16[128,1024]{1,0:T(8,128)(2,1)S(1)} %get-tuple-element.50), channel_id=1, source_target_pairs={{0,2},{2,0},{4,6},{6,4},{8,10},{10,8},{12,14},{14,12},{16,18},{18,... | collective-permute-start | bytes 786440 | tf_op jit(solution)/shard_map/ppermute | solution.py:31
  4.3 10.3 %collective-permute-start.7 = (bf16[256,1024]{1,0:T(8,128)(2,1)S(1)}, bf16[256,1024]{1,0:T(8,128)(2,1)S(1)}, u32[]{:S(2)}, u32[]{:S(2)}) collective-permute-start(bf16[256,1024]{1,0:T(8,128)(2,1)S(1)} %pad_maximum_fusion.1), channel_id=1, source_target_pairs={{0,0},{1,1},{3,2},{4,4},{5,5},{7,6},{8,8},{9,9},{11,10},{12,12},{1... | collective-permute-start | bytes 1572872 | tf_op jit(solution)/shard_map/ppermute | solution.py:269
  5.2 15.9 %collective-permute-start.1 = (bf16[16,128,128]{2,1,0:T(8,128)(2,1)S(1)}, bf16[16,128,128]{2,1,0:T(8,128)(2,1)S(1)}, u32[]{:S(2)}, u32[]{:S(2)}) collective-permute-start(bf16[16,128,128]{2,1,0:T(8,128)(2,1)S(1)} %bitcast.10), channel_id=1, source_target_pairs={{0,2},{2,0},{4,6},{6,4},{8,10},{10,8},{12,14},{14,12},{16,18},{18,... | collective-permute-start | bytes 1572872 | tf_op jit(solution)/shard_map/ppermute | solution.py:31
  6.9 6.6 %collective-permute-start.2 = (bf16[1,64,512]{2,1,0:T(8,128)(2,1)S(1)}, bf16[1,64,512]{2,1,0:T(8,128)(2,1)S(1)}, u32[]{:S(2)}, u32[]{:S(2)}) collective-permute-start(bf16[1,64,512]{2,1,0:T(8,128)(2,1)S(1)} %bitcast.18), channel_id=1, source_target_pairs={{0,16},{2,18},{4,20},{6,22},{8,24},{10,26},{12,28},{14,30},{16,0},... | collective-permute-start | bytes 196616 | tf_op jit(solution)/shard_map/ppermute | solution.py:31
  8.6 13.0 %collective-permute-start.10 = (bf16[256,1024]{1,0:T(8,128)(2,1)S(1)}, bf16[256,1024]{1,0:T(8,128)(2,1)S(1)}, u32[]{:S(2)}, u32[]{:S(2)}) collective-permute-start(bf16[256,1024]{1,0:T(8,128)(2,1)S(1)} %pad_maximum_fusion.2), channel_id=1, source_target_pairs={{0,0},{1,1},{3,2},{4,4},{5,5},{7,6},{8,8},{9,9},{11,10},{12,12},{1... | collective-permute-start | bytes 1572872 | tf_op jit(solution)/shard_map/ppermute | solution.py:269
  13.5 7.6 %collective-permute-start.3 = (bf16[2,64,512]{2,1,0:T(8,128)(2,1)S(1)}, bf16[2,64,512]{2,1,0:T(8,128)(2,1)S(1)}, u32[]{:S(2)}, u32[]{:S(2)}) collective-permute-start(bf16[2,64,512]{2,1,0:T(8,128)(2,1)S(1)} %pad_maximum_fusion.6), channel_id=1, source_target_pairs={{0,8},{2,10},{4,12},{6,14},{8,0},{10,2},{12,4},{14,6},{16,24},{18,... | collective-permute-start | bytes 393224 | tf_op jit(solution)/shard_map/ppermute | solution.py:31
  14.5 6.6 %collective-permute-start = (s32[33]{0:T(128)S(1)}, s32[33]{0:T(128)S(1)}, u32[]{:S(2)}, u32[]{:S(2)}) collective-permute-start(s32[33]{0:T(128)S(1)} %pad_add_fusion.own_index), channel_id=1, source_target_pairs={{0,2},{2,0},{4,6},{6,4},{8,10},{10,8},{12,14},{14,12},{16,18},{18,... | collective-permute-start | bytes 404 | tf_op jit(solution)/shard_map/ppermute | solution.py:31
  14.6 24.8 %collective-permute-start.8 = (bf16[256,1024]{1,0:T(8,128)(2,1)S(1)}, bf16[256,1024]{1,0:T(8,128)(2,1)S(1)}, u32[]{:S(2)}, u32[]{:S(2)}) collective-permute-start(bf16[256,1024]{1,0:T(8,128)(2,1)S(1)} %collective-permute-done.7), channel_id=1, source_target_pairs={{1,16},{2,18},{5,20},{6,22},{9,24},{10,26},{13,28},{14,30},{16,1},... | collective-permute-start | bytes 1572872 | tf_op jit(solution)/shard_map/ppermute | solution.py:282
  21.1 6.4 %collective-permute-start.4 = (bf16[4,64,512]{2,1,0:T(8,128)(2,1)S(1)}, bf16[4,64,512]{2,1,0:T(8,128)(2,1)S(1)}, u32[]{:S(2)}, u32[]{:S(2)}) collective-permute-start(bf16[4,64,512]{2,1,0:T(8,128)(2,1)S(1)} %pad_maximum_fusion.4), channel_id=1, source_target_pairs={{0,4},{2,6},{4,0},{6,2},{8,12},{10,14},{12,8},{14,10},{16,20},{18,... | collective-permute-start | bytes 786440 | tf_op jit(solution)/shard_map/ppermute | solution.py:31
  21.7 23.9 %collective-permute-start.11 = (bf16[256,1024]{1,0:T(8,128)(2,1)S(1)}, bf16[256,1024]{1,0:T(8,128)(2,1)S(1)}, u32[]{:S(2)}, u32[]{:S(2)}) collective-permute-start(bf16[256,1024]{1,0:T(8,128)(2,1)S(1)} %collective-permute-done.10), channel_id=1, source_target_pairs={{1,16},{2,18},{5,20},{6,22},{9,24},{10,26},{13,28},{14,30},{16,1},... | collective-permute-start | bytes 1572872 | tf_op jit(solution)/shard_map/ppermute | solution.py:282
  28.9 10.7 %collective-permute-start.5 = (bf16[64,512]{1,0:T(8,128)(2,1)S(1)}, bf16[64,512]{1,0:T(8,128)(2,1)S(1)}, u32[]{:S(2)}, u32[]{:S(2)}) collective-permute-start(bf16[64,512]{1,0:T(8,128)(2,1)S(1)} %get-tuple-element.44), channel_id=1, source_target_pairs={{0,2},{2,0},{4,6},{6,4},{8,10},{10,8},{12,14},{14,12},{16,18},{18,... | collective-permute-start | bytes 196616 | tf_op jit(solution)/shard_map/ppermute | solution.py:31
  39.4 6.1 %collective-permute-start.12 = (bf16[128,1024]{1,0:T(8,128)(2,1)S(1)}, bf16[128,1024]{1,0:T(8,128)(2,1)S(1)}, u32[]{:S(2)}, u32[]{:S(2)}) collective-permute-start(bf16[128,1024]{1,0:T(8,128)(2,1)S(1)} %slice.8), channel_id=1, source_target_pairs={{0,2},{2,0},{4,6},{6,4},{8,10},{10,8},{12,14},{14,12},{16,18},{18,... | collective-permute-start | bytes 786440 | tf_op jit(solution)/shard_map/ppermute | solution.py:31
  45.5 5.2 %collective-permute-start.13 = (bf16[64,512]{1,0:T(8,128)(2,1)S(1)}, bf16[64,512]{1,0:T(8,128)(2,1)S(1)}, u32[]{:S(2)}, u32[]{:S(2)}) collective-permute-start(bf16[64,512]{1,0:T(8,128)(2,1)S(1)} %get-tuple-element.53.v_t), channel_id=1, source_target_pairs={{0,16},{2,18},{4,20},{6,22},{8,24},{10,26},{12,28},{14,30},{16,0},... | collective-permute-start | bytes 196616 | tf_op jit(solution)/shard_map/ppermute | solution.py:31
  45.5 8.1 %collective-permute-start.14 = (bf16[64,512]{1,0:T(8,128)(2,1)S(1)}, bf16[64,512]{1,0:T(8,128)(2,1)S(1)}, u32[]{:S(2)}, u32[]{:S(2)}) collective-permute-start(bf16[64,512]{1,0:T(8,128)(2,1)S(1)} %get-tuple-element.54), channel_id=1, source_target_pairs={{1,16},{3,18},{5,20},{7,22},{9,24},{11,26},{13,28},{15,30},{16,1},... | collective-permute-start | bytes 196616 | tf_op jit(solution)/shard_map/ppermute | solution.py:47
  47.5 6.2 %collective-permute-start.15 = (bf16[64,512]{1,0:T(8,128)(2,1)S(1)}, bf16[64,512]{1,0:T(8,128)(2,1)S(1)}, u32[]{:S(2)}, u32[]{:S(2)}) collective-permute-start(bf16[64,512]{1,0:T(8,128)(2,1)S(1)} %get-tuple-element.54), channel_id=1, source_target_pairs={{1,0},{3,2},{5,4},{7,6},{9,8},{11,10},{13,12},{15,14},{16,17},{18,... | collective-permute-start | bytes 196616 | tf_op jit(solution)/shard_map/ppermute | solution.py:309
  53.7 10.2 %collective-permute-start.19 = (bf16[128,1024]{1,0:T(8,128)(2,1)S(1)}, bf16[128,1024]{1,0:T(8,128)(2,1)S(1)}, u32[]{:S(2)}, u32[]{:S(2)}) collective-permute-start(bf16[128,1024]{1,0:T(8,128)(2,1)S(1)} %slice.7), channel_id=1, source_target_pairs={{0,2},{2,0},{4,6},{6,4},{8,10},{10,8},{12,14},{14,12},{16,18},{18,... | collective-permute-start | bytes 786440 | tf_op jit(solution)/shard_map/ppermute | solution.py:31
  53.8 5.9 %collective-permute-start.16 = (bf16[2,64,512]{2,1,0:T(8,128)(2,1)S(1)}, bf16[2,64,512]{2,1,0:T(8,128)(2,1)S(1)}, u32[]{:S(2)}, u32[]{:S(2)}) collective-permute-start(bf16[2,64,512]{2,1,0:T(8,128)(2,1)S(1)} %combine.1), channel_id=1, source_target_pairs={{0,8},{2,10},{4,12},{6,14},{8,0},{10,2},{12,4},{14,6},{16,24},{18,... | collective-permute-start | bytes 393224 | tf_op jit(solution)/shard_map/ppermute | solution.py:31
  54.7 9.2 %collective-permute-start.18 = (bf16[64,512]{1,0:T(8,128)(2,1)S(1)}, bf16[64,512]{1,0:T(8,128)(2,1)S(1)}, u32[]{:S(2)}, u32[]{:S(2)}) collective-permute-start(bf16[64,512]{1,0:T(8,128)(2,1)S(1)} %add_convert_fusion.1.agg_t), channel_id=1, source_target_pairs={{1,16},{3,18},{5,20},{7,22},{9,24},{11,26},{13,28},{15,30},{16,1},... | collective-permute-start | bytes 196616 | tf_op jit(solution)/shard_map/ppermute | solution.py:47
  59.7 8.8 %collective-permute-start.17 = (bf16[4,64,512]{2,1,0:T(8,128)(2,1)S(1)}, bf16[4,64,512]{2,1,0:T(8,128)(2,1)S(1)}, u32[]{:S(2)}, u32[]{:S(2)}) collective-permute-start(bf16[4,64,512]{2,1,0:T(8,128)(2,1)S(1)} %pad_maximum_fusion.5), channel_id=1, source_target_pairs={{0,4},{2,6},{4,0},{6,2},{8,12},{10,14},{12,8},{14,10},{16,20},{18,... | collective-permute-start | bytes 786440 | tf_op jit(solution)/shard_map/ppermute | solution.py:31
  69.9 1.3 %collective-permute-start.20 = (bf16[64,512]{1,0:T(8,128)(2,1)S(1)}, bf16[64,512]{1,0:T(8,128)(2,1)S(1)}, u32[]{:S(2)}, u32[]{:S(2)}) collective-permute-start(bf16[64,512]{1,0:T(8,128)(2,1)S(1)} %get-tuple-element.67), channel_id=1, source_target_pairs={{0,2},{2,0},{4,6},{6,4},{8,10},{10,8},{12,14},{14,12},{16,18},{18,... | collective-permute-start | bytes 196616 | tf_op jit(solution)/shard_map/ppermute | solution.py:31
  71.2 9.2 %collective-permute-start.21 = (bf16[64,512]{1,0:T(8,128)(2,1)S(1)}, bf16[64,512]{1,0:T(8,128)(2,1)S(1)}, u32[]{:S(2)}, u32[]{:S(2)}) collective-permute-start(bf16[64,512]{1,0:T(8,128)(2,1)S(1)} %add_convert_fusion.agg_t), channel_id=1, source_target_pairs={{1,16},{3,18},{5,20},{7,22},{9,24},{11,26},{13,28},{15,30},{16,1},... | collective-permute-start | bytes 196616 | tf_op jit(solution)/shard_map/ppermute | solution.py:47

commit v7 on v6

--- a/solution.py
+++ b/solution.py
@@ -11,6 +11,7 @@
 LAYERS = 2
 ROWS = 512
 PARTS = (4, 4)
+AHEAD = 8
 PROJECT_FLOPS = 10 * 1153 * 10**6
 SECOND_FLOPS = 5 * 1153 * 10**6
 MIB = 2**20
@@ -79,9 +80,11 @@
     return jnp.where(lax.axis_index("src") % 2 == 0, on_first, on_second)
 
 
-def project_body(w_proj_t, state, out, *parts):
+def project_body(w_proj_t, state, out, ahead, *parts):
     out[...] = dot_nt(w_proj_t[0], state[...]).astype(BF16)
-    half, start, count = state.shape[0] // 2, 0, len(parts) // 2
+    start, count = ahead.shape[0], len(parts) // 2
+    half = (state.shape[0] - start) // 2
+    ahead[...] = state[:start, :]
     for keep, swap in zip(parts[:count], parts[count:]):
         rows = keep.shape[0]
         low, high = state[pl.ds(start, rows), :], state[pl.ds(half + start, rows), :]
@@ -92,17 +95,19 @@
 
 def project(w_proj_t, state):
     width, (edges, features) = w_proj_t.shape[1], state.shape
-    sizes = [edges // 2 * part // sum(PARTS) for part in PARTS]
+    ahead = edges // AHEAD
+    sizes = [(edges - ahead) // 2 * part // sum(PARTS) for part in PARTS]
     outs = call(
         project_body,
         "project",
-        [like((width, edges), BF16)] + [like((n, features), BF16) for n in sizes * 2],
+        [like((width, edges), BF16)]
+        + [like((n, features), BF16) for n in [ahead] + sizes * 2],
         [],
         [w_proj_t, state],
         limit=8,
         flops=PROJECT_FLOPS,
     )
-    return outs[0], outs[1 : 1 + len(sizes)], outs[1 + len(sizes) :]
+    return outs[0], outs[1], outs[2 : 2 + len(sizes)], outs[2 + len(sizes) :]
 
 
 def add_blocks(index, slots, blocks, pool, add):
@@ -219,10 +224,18 @@
     if len(other) == 1:
         received = other[0][...]
     else:
+        first, first_passed, *other = other
         count = len(other) // 2
         passed = jnp.concatenate([y[...] for y in other[count:]], axis=0)
         routed = jnp.concatenate([x[: y.shape[0], :] for x, y in zip(other, other[count:])], axis=0)
-        received = jnp.concatenate([by_core(routed, passed), by_core(passed, routed)], axis=0)
+        received = jnp.concatenate(
+            [
+                by_core(first[: first_passed.shape[0], :], first_passed[...]),
+                by_core(routed, passed),
+                by_core(passed, routed),
+            ],
+            axis=0,
+        )
     source = jnp.where(here, own[...], received)
     low = jnp.where(here, agg_t[...], agg_other[...])
     column = reverse_column(reverse)
@@ -280,6 +293,16 @@
             else:
                 pairs.append(((a * copies + r) * 2 + 1 - a, across * 2 + a))
     return lax.ppermute(staged, ("src", "tgt"), pairs)
+
+
+def send_ahead(rows):
+    copies = lax.axis_size("src") // 2
+    pairs = [
+        ((a * copies + r) * 2 + 1 - a, ((1 - a) * copies + r) * 2 + a)
+        for a in range(2)
+        for r in range(0, copies, 2)
+    ]
+    return lax.ppermute(jnp.concatenate([rows, hop(rows, 1)], axis=0), ("src", "tgt"), pairs)
 
 
 def pass_on(routed):
@@ -345,14 +368,15 @@
     own_coeffs = triplet_coeff[0, 0]
     index, coeffs = [own_index, hop(own_index, 1)], [own_coeffs, hop(own_coeffs, 1)]
     paired = lax.axis_size("tgt") == 2
-    paired = lax.axis_size("tgt") == 2
-    proj0, keep, swap = project(w_proj_t, state0)
+    proj0, ahead, keep, swap = project(w_proj_t, state0)
     if paired:
         staged = [stage_routes(x, y) for x, y in zip(keep, swap)]
     else:
         staged = [state0]
     pool = gather_down(proj0[None], 4)
-    index, coeffs, pool = lax.optimization_barrier((index, coeffs, pool))
+    first = [send_ahead(ahead)] if paired else []
+    index, coeffs, first, pool = lax.optimization_barrier((index, coeffs, first, pool))
+    first += [pass_on(x) for x in first]
     routed = [send_routes(x) if paired else to_mirror(x) for x in staged]
     agg0 = sum_over_cores(*triplet_partials(index, gather_down(pool, 2), coeffs))
     total0, branch0, v_t, u_t = call(
@@ -371,7 +395,7 @@
     u_t, v_t, routed, passed = lax.optimization_barrier((u_t, v_t, routed, passed))
     held1 = next_pool(v_t, u_t)
     routed, agg0_sent, held1 = lax.optimization_barrier((routed, agg0, held1))
-    received = routed + passed + [pass_on(x) for x in routed[1:] if paired]
+    received = first + routed + passed + [pass_on(x) for x in routed[1:] if paired]
     agg0_other = to_mirror(agg0_sent)
     pool1 = gather_down(held1, 4)
     near1 = gather_down(pool1, 2)

time: 85.1 us -> 82.2 us (0.966)
  waiting for transfers between devices: 32.8 us -> 28.5 us
  starting transfers between devices: 29.4 us -> 30.7 us
    ppermute x0 -> x1, starting transfers between devices: none -> 5.24 us  [send_ahead(): lax.ppermute(jnp.concatenate([rows, hop(rows, 1)], axis=0), ('src', 'tgt'...]
    ppermute x2, waiting for transfers between devices: 12.6 us -> 8.39 us  [send_routes(): return lax.ppermute(staged, ('src', 'tgt'), pairs)]
    ppermute x2, starting transfers between devices: 9.16 us -> 5.41 us  [send_routes(): return lax.ppermute(staged, ('src', 'tgt'), pairs)]
    ppermute x0 -> x1, waiting for transfers between devices: none -> 3.15 us  [send_ahead(): lax.ppermute(jnp.concatenate([rows, hop(rows, 1)], axis=0), ('src', 'tgt'...]
    ppermute x14 -> x16, waiting for transfers between devices: 11.7 us -> 9.29 us  [hop(): return lax.ppermute(values, 'src', [(i, i ^ bit) for i in range(size)])]
    ppermute x14 -> x16, starting transfers between devices: 6.67 us -> 6.17 us  [hop(): return lax.ppermute(values, 'src', [(i, i ^ bit) for i in range(size)])]
  transfers between devices with their start and end apart: 22 -> 25, of which waited for: 11 -> 10; matrix products, arithmetic and copies ran while one was open for 0% -> 0% of each run, Pallas kernels for 15% -> 16%
where the time goes in v7:
time: 82.2 us; the launch traced here: 82 us
  starting transfers between devices  30.7 us (37%)
  waiting for transfers between devices  28.5 us (35%)
  Pallas kernels  19 us (23%)
  local copies, waits for them, and re-layouts  2.27 us (3%)
  between operations  1.07 us (1%)
    pallas_call x8, Pallas kernels, call(): pl.pallas_call(body, in_specs=[smem] * len(scalars) + [vmem] * len(arrays...  19 us
    ppermute x3, starting transfers between devices, to_mirror(): return lax.ppermute(values, ('src', 'tgt'), mirror_pairs())  11.2 us
    ppermute x16, waiting for transfers between devices, hop(): return lax.ppermute(values, 'src', [(i, i ^ bit) for i in range(size)])  9.29 us
    ppermute x2, waiting for transfers between devices, send_routes(): return lax.ppermute(staged, ('src', 'tgt'), pairs)  8.39 us
    ppermute x3, waiting for transfers between devices, to_mirror(): return lax.ppermute(values, ('src', 'tgt'), mirror_pairs())  7.7 us
    ppermute x16, starting transfers between devices, hop(): return lax.ppermute(values, 'src', [(i, i ^ bit) for i in range(size)])  6.17 us
    ppermute x2, starting transfers between devices, send_routes(): return lax.ppermute(staged, ('src', 'tgt'), pairs)  5.41 us
    ppermute x1, starting transfers between devices, send_ahead(): lax.ppermute(jnp.concatenate([rows, hop(rows, 1)], axis=0), ('src', 'tgt'...  5.24 us
  transfers between devices with their start and end apart: 25, of which 10 were waited for; matrix products, arithmetic and copies ran while one was open for 0% of the time, Pallas kernels for 16%

profile of v7, /device:TPU:6, one launch (start us, length us, event | category | flops | bytes accessed | tf_op | source)
XLA Modules:
  0.0 82.0 jit_solution(12329478750138806316)
XLA Ops:
  0.0 1.2 %copy-done.4 = bf16[1,1,512,1024]{3,2,1,0:T(8,128)(2,1)S(1)} copy-done((bf16[1,1,512,1024]{3,2,1,0:T(8,128)(2,1)S(1)}, bf16[1,1,512,1024]{3,2,1,0:T(8,128)(2,1)}, u32[]{:S(2)}) %copy-start.4) | copy-done | bytes 1048600
  1.2 0.9 %copy-done.6 = bf16[2,1024,64]{1,2,0:T(8,128)(2,1)S(1)} copy-done((bf16[2,1024,64]{1,2,0:T(8,128)(2,1)S(1)}, bf16[2,1024,64]{1,2,0:T(8,128)(2,1)}, u32[]{:S(2)}) %copy-start.6) | copy-done | bytes 262168
  2.2 0.4 project.1
  2.6 0.0 copy-start.2
  2.7 0.0 copy-start.5
  2.7 0.1 collective-permute-start.8
  2.8 2.7 %collective-permute-start.4 = (bf16[1,64,512]{2,1,0:T(8,128)(2,1)S(1)}, bf16[1,64,512]{2,1,0:T(8,128)(2,1)S(1)}, u32[]{:S(2)}, u32[]{:S(2)}) collective-permute-start(bf16[1,64,512]{2,1,0:T(8,128)(2,1)S(1)} %bitcast.18), channel_id=1, source_target_pairs={{0,16},{2,18},{4,20},{6,22},{8,24},{10,26},{12,28},{14,30},{16,0},... | collective-permute-start | bytes 196616 | tf_op jit(solution)/shard_map/ppermute | solution.py:32
  5.4 0.2 collective-permute-start.2
  5.6 0.3 collective-permute-start.1
  5.9 0.2 collective-permute-start.11
  6.2 0.7 collective-permute-start.9
  6.9 2.7 %collective-permute-done.4 = bf16[1,64,512]{2,1,0:T(8,128)(2,1)S(1)} collective-permute-done((bf16[1,64,512]{2,1,0:T(8,128)(2,1)S(1)}, bf16[1,64,512]{2,1,0:T(8,128)(2,1)S(1)}, u32[]{:S(2)}, u32[]{:S(2)}) %collective-permute-start.4) | collective-permute-done | bytes 65568 | tf_op jit(solution)/shard_map/ppermute | solution.py:32
  9.6 0.8 collective-permute-start.5
  10.4 5.2 %collective-permute-start.3 = (bf16[128,1024]{1,0:T(8,128)(2,1)S(1)}, bf16[128,1024]{1,0:T(8,128)(2,1)S(1)}, u32[]{:S(2)}, u32[]{:S(2)}) collective-permute-start(bf16[128,1024]{1,0:T(8,128)(2,1)S(1)} %pad_maximum_fusion.4), channel_id=1, source_target_pairs={{1,16},{5,20},{9,24},{13,28},{16,1},{20,5},{24,9},{28,13}} | collective-permute-start | bytes 786440 | tf_op jit(solution)/shard_map/ppermute | solution.py:305
  15.7 0.7 collective-permute-start.12
  17.1 0.1 pad_add_fusion.own_index
  17.1 0.0 collective-permute-start
  17.2 2.9 %collective-permute-start.10 = (bf16[224,1024]{1,0:T(8,128)(2,1)S(1)}, bf16[224,1024]{1,0:T(8,128)(2,1)S(1)}, u32[]{:S(2)}, u32[]{:S(2)}) collective-permute-start(bf16[224,1024]{1,0:T(8,128)(2,1)S(1)} %collective-permute-done.9), channel_id=1, source_target_pairs={{1,16},{2,18},{5,20},{6,22},{9,24},{10,26},{13,28},{14,30},{16,1},... | collective-permute-start | bytes 1376264 | tf_op jit(solution)/shard_map/ppermute | solution.py:295
  20.1 3.1 %collective-permute-done.3.rest_0_ = bf16[128,1024]{1,0:T(8,128)(2,1)S(1)} collective-permute-done((bf16[128,1024]{1,0:T(8,128)(2,1)S(1)}, bf16[128,1024]{1,0:T(8,128)(2,1)S(1)}, u32[]{:S(2)}, u32[]{:S(2)}) %collective-permute-start.3) | collective-permute-done | bytes 262176 | tf_op jit(solution)/shard_map/ppermute | solution.py:305
  23.3 0.5 collective-permute-start.6
  23.8 2.5 %collective-permute-start.13 = (bf16[224,1024]{1,0:T(8,128)(2,1)S(1)}, bf16[224,1024]{1,0:T(8,128)(2,1)S(1)}, u32[]{:S(2)}, u32[]{:S(2)}) collective-permute-start(bf16[224,1024]{1,0:T(8,128)(2,1)S(1)} %collective-permute-done.12), channel_id=1, source_target_pairs={{1,16},{2,18},{5,20},{6,22},{9,24},{10,26},{13,28},{14,30},{16,1},... | collective-permute-start | bytes 1376264 | tf_op jit(solution)/shard_map/ppermute | solution.py:295
  26.3 3.3 %collective-permute-done.6 = bf16[4,64,512]{2,1,0:T(8,128)(2,1)S(1)} collective-permute-done((bf16[4,64,512]{2,1,0:T(8,128)(2,1)S(1)}, bf16[4,64,512]{2,1,0:T(8,128)(2,1)S(1)}, u32[]{:S(2)}, u32[]{:S(2)}) %collective-permute-start.6) | collective-permute-done | bytes 262176 | tf_op jit(solution)/shard_map/ppermute | solution.py:32
  29.7 1.3 %triplets.2 = (f32[64,512]{1,0:T(8,128)S(1)}, bf16[64,512]{1,0:T(8,128)(2,1)S(1)}) custom-call(s32[33]{0:T(128)S(1)} %pad_add_fusion.own_index, s32[33]{0:T(128)S(1)} %collective-permute-done.other_index, bf16[8,64,512]{2,1,0:T(8,128)(2,1)S(1)} %pad_maximum_fusion.pool, bf16[16,128,128]{2,1,0:T(8,128)(2,1)S(1)} %bitcast.11, ...), custom_call_target="tpu_custom_call" | custom-call | tf_op jit(solution)/shard_map/triplets/pallas_call | solution.py:54
  31.0 0.1 collective-permute-start.7
  31.1 7.5 %collective-permute-done.10.rest_2_ = bf16[224,1024]{1,0:T(8,128)(2,1)S(1)} collective-permute-done((bf16[224,1024]{1,0:T(8,128)(2,1)S(1)}, bf16[224,1024]{1,0:T(8,128)(2,1)S(1)}, u32[]{:S(2)}, u32[]{:S(2)}) %collective-permute-start.10) | collective-permute-done | bytes 458784 | tf_op jit(solution)/shard_map/ppermute | solution.py:295
  38.7 0.1 collective-permute-start.14
  38.8 3.8 %first.1 = (f32[512,1024]{1,0:T(8,128)S(1)}, bf16[512,1024]{1,0:T(8,128)(2,1)S(1)}, bf16[64,512]{1,0:T(8,128)(2,1)S(1)}, bf16[64,512]{1,0:T(8,128)(2,1)S(1)}) custom-call(bf16[2,64,1024]{2,1,0:T(8,128)(2,1)S(1)} %copy-done.2, bf16[2,1024,1024]{2,1,0:T(8,128)(2,1)S(1)} %copy-done, bf16[2,1024,1024]{2,1,0:T(8,128)(2,1)S(1)} %copy-done.1, ...), custom_call_target="tpu_custom_call" | custom-call | tf_op jit(solution)/shard_map/first/pallas_call | solution.py:54
  42.7 0.9 %collective-permute-done.13.rest_3_ = bf16[224,1024]{1,0:T(8,128)(2,1)S(1)} collective-permute-done((bf16[224,1024]{1,0:T(8,128)(2,1)S(1)}, bf16[224,1024]{1,0:T(8,128)(2,1)S(1)}, u32[]{:S(2)}, u32[]{:S(2)}) %collective-permute-start.13) | collective-permute-done | bytes 458784 | tf_op jit(solution)/shard_map/ppermute | solution.py:295
  43.6 1.9 %collective-permute-start.16 = (bf16[64,512]{1,0:T(8,128)(2,1)S(1)}, bf16[64,512]{1,0:T(8,128)(2,1)S(1)}, u32[]{:S(2)}, u32[]{:S(2)}) collective-permute-start(bf16[64,512]{1,0:T(8,128)(2,1)S(1)} %get-tuple-element.57), channel_id=1, source_target_pairs={{1,16},{3,18},{5,20},{7,22},{9,24},{11,26},{13,28},{15,30},{16,1},... | collective-permute-start | bytes 196616 | tf_op jit(solution)/shard_map/ppermute | solution.py:48
  45.5 1.3 %collective-permute-start.17 = (bf16[64,512]{1,0:T(8,128)(2,1)S(1)}, bf16[64,512]{1,0:T(8,128)(2,1)S(1)}, u32[]{:S(2)}, u32[]{:S(2)}) collective-permute-start(bf16[64,512]{1,0:T(8,128)(2,1)S(1)} %get-tuple-element.57), channel_id=1, source_target_pairs={{1,0},{3,2},{5,4},{7,6},{9,8},{11,10},{13,12},{15,14},{16,17},{18,... | collective-permute-start | bytes 196616 | tf_op jit(solution)/shard_map/ppermute | solution.py:332
  46.8 1.9 %collective-permute-done.15.v_other = bf16[64,512]{1,0:T(8,128)(2,1)S(1)} collective-permute-done((bf16[64,512]{1,0:T(8,128)(2,1)S(1)}, bf16[64,512]{1,0:T(8,128)(2,1)S(1)}, u32[]{:S(2)}, u32[]{:S(2)}) %collective-permute-start.15) | collective-permute-done | bytes 65568 | tf_op jit(solution)/shard_map/ppermute | solution.py:32
  48.7 2.8 %collective-permute-done.16.u_mirror = bf16[64,512]{1,0:T(8,128)(2,1)S(1)} collective-permute-done((bf16[64,512]{1,0:T(8,128)(2,1)S(1)}, bf16[64,512]{1,0:T(8,128)(2,1)S(1)}, u32[]{:S(2)}, u32[]{:S(2)}) %collective-permute-start.16) | collective-permute-done | bytes 65568 | tf_op jit(solution)/shard_map/ppermute | solution.py:48
  51.5 0.1 combine.1
  51.6 0.1 collective-permute-start.18
  51.7 0.1 collective-permute-start.22
  51.8 0.6 collective-permute-start.21
  52.3 4.8 %collective-permute-start.20 = (bf16[64,512]{1,0:T(8,128)(2,1)S(1)}, bf16[64,512]{1,0:T(8,128)(2,1)S(1)}, u32[]{:S(2)}, u32[]{:S(2)}) collective-permute-start(bf16[64,512]{1,0:T(8,128)(2,1)S(1)} %add_convert_fusion.1.agg_t), channel_id=1, source_target_pairs={{1,16},{3,18},{5,20},{7,22},{9,24},{11,26},{13,28},{15,30},{16,1},... | collective-permute-start | bytes 196616 | tf_op jit(solution)/shard_map/ppermute | solution.py:48
  57.1 0.6 collective-permute-start.19
  57.7 3.3 %collective-permute-done.20.agg_other = bf16[64,512]{1,0:T(8,128)(2,1)S(1)} collective-permute-done((bf16[64,512]{1,0:T(8,128)(2,1)S(1)}, bf16[64,512]{1,0:T(8,128)(2,1)S(1)}, u32[]{:S(2)}, u32[]{:S(2)}) %collective-permute-start.20) | collective-permute-done | bytes 65568 | tf_op jit(solution)/shard_map/ppermute | solution.py:48
  61.0 4.6 %second.1 = (bf16[512,1024]{1,0:T(8,128)(2,1)S(1)}, bf16[512,1024]{1,0:T(8,128)(2,1)S(1)}) custom-call(bf16[2,64,1024]{2,1,0:T(8,128)(2,1)S(1)} %copy-done.2, bf16[2,1024,1024]{2,1,0:T(8,128)(2,1)S(1)} %copy-done, bf16[2,1024,1024]{2,1,0:T(8,128)(2,1)S(1)} %copy-done.1, f32[2,1024]{1,0:T(2,128)S(1)} %copy-done.8, ...), custom_call_target="tpu_custom_call" | custom-call | flops 5765000192 | tf_op jit(solution)/shard_map/second/pallas_call | solution.py:54
  65.6 0.1 pad_maximum_fusion.1.pool
  65.6 1.3 %triplets.3 = (f32[64,512]{1,0:T(8,128)S(1)}, bf16[64,512]{1,0:T(8,128)(2,1)S(1)}) custom-call(s32[33]{0:T(128)S(1)} %pad_add_fusion.own_index, s32[33]{0:T(128)S(1)} %collective-permute-done.other_index, bf16[8,64,512]{2,1,0:T(8,128)(2,1)S(1)} %pad_maximum_fusion.1.pool, bf16[16,128,128]{2,1,0:T(8,128)(2,1)S(1)} %bitcast.12, ...), custom_call_target="tpu_custom_call" | custom-call | tf_op jit(solution)/shard_map/triplets/pallas_call | solution.py:54
  67.0 0.1 collective-permute-start.23
  67.1 1.2 %collective-permute-done.23 = bf16[64,512]{1,0:T(8,128)(2,1)S(1)} collective-permute-done((bf16[64,512]{1,0:T(8,128)(2,1)S(1)}, bf16[64,512]{1,0:T(8,128)(2,1)S(1)}, u32[]{:S(2)}, u32[]{:S(2)}) %collective-permute-start.23) | collective-permute-done | bytes 65568 | tf_op jit(solution)/shard_map/ppermute | solution.py:32
  68.3 4.6 %collective-permute-start.24 = (bf16[64,512]{1,0:T(8,128)(2,1)S(1)}, bf16[64,512]{1,0:T(8,128)(2,1)S(1)}, u32[]{:S(2)}, u32[]{:S(2)}) collective-permute-start(bf16[64,512]{1,0:T(8,128)(2,1)S(1)} %add_convert_fusion.agg_t), channel_id=1, source_target_pairs={{1,16},{3,18},{5,20},{7,22},{9,24},{11,26},{13,28},{15,30},{16,1},... | collective-permute-start | bytes 196616 | tf_op jit(solution)/shard_map/ppermute | solution.py:48
  72.9 3.1 %third.1.total = f32[512,1024]{1,0:T(8,128)S(1)} custom-call(bf16[2,64,1024]{2,1,0:T(8,128)(2,1)S(1)} %copy-done.2, bf16[2,1024,1024]{2,1,0:T(8,128)(2,1)S(1)} %copy-done, bf16[2,1024,1024]{2,1,0:T(8,128)(2,1)S(1)} %copy-done.1, f32[2,1024]{1,0:T(2,128)S(1)} %copy-done.8, bf16[512,1024]{1,0:T(8,128)(2,1)S(1)} %get-tuple-element.72.state, ...), custom_call_target="tpu_custom_call" | custom-call | tf_op jit(solution)/shard_map/third/pallas_call | solution.py:54
  76.0 1.7 %collective-permute-done.24.agg_other = bf16[64,512]{1,0:T(8,128)(2,1)S(1)} collective-permute-done((bf16[64,512]{1,0:T(8,128)(2,1)S(1)}, bf16[64,512]{1,0:T(8,128)(2,1)S(1)}, u32[]{:S(2)}, u32[]{:S(2)}) %collective-permute-start.24) | collective-permute-done | bytes 65568 | tf_op jit(solution)/shard_map/ppermute | solution.py:48
  77.7 4.3 %last.1 = bf16[512,1024]{1,0:T(8,128)(2,1)} custom-call(bf16[2,64,1024]{2,1,0:T(8,128)(2,1)S(1)} %copy-done.2, bf16[2,1024,1024]{2,1,0:T(8,128)(2,1)S(1)} %copy-done, bf16[2,1024,1024]{2,1,0:T(8,128)(2,1)S(1)} %copy-done.1, f32[2,1024]{1,0:T(2,128)S(1)} %copy-done.8, bf16[512,1024]{1,0:T(8,128)(2,1)S(1)} %get-tuple-element.68.mirrored, ...), custom_call_target="tpu_custom_call" | custom-call | tf_op jit(solution)/shard_map/last/pallas_call | solution.py:54
  (48 shorter events, 0.4 us)
Async XLA Ops:
  0.0 1.2 %copy-start.4 = (bf16[1,1,512,1024]{3,2,1,0:T(8,128)(2,1)S(1)}, bf16[1,1,512,1024]{3,2,1,0:T(8,128)(2,1)}, u32[]{:S(2)}) copy-start(bf16[1,1,512,1024]{3,2,1,0:T(8,128)(2,1)} %param.11) | copy-start | bytes 3145732
  1.2 0.9 %copy-start.6 = (bf16[2,1024,64]{1,2,0:T(8,128)(2,1)S(1)}, bf16[2,1024,64]{1,2,0:T(8,128)(2,1)}, u32[]{:S(2)}) copy-start(bf16[2,1024,64]{1,2,0:T(8,128)(2,1)} %param.17) | copy-start | bytes 786436
  2.2 3.4 %copy-start.3 = (bf16[1,1,16,128,128]{4,3,2,1,0:T(8,128)(2,1)S(1)}, bf16[1,1,16,128,128]{4,3,2,1,0:T(8,128)(2,1)}, u32[]{:S(2)}) copy-start(bf16[1,1,16,128,128]{4,3,2,1,0:T(8,128)(2,1)} %param.12) | copy-start | bytes 1572868
  2.2 14.9 %copy-start.10 = (s32[1,1,16]{2,1,0:T(1,128)S(1)}, s32[1,1,16]{2,1,0:T(1,128)}, u32[]{:S(2)}) copy-start(s32[1,1,16]{2,1,0:T(1,128)} %param.14) | copy-start | bytes 196
  2.2 14.9 %copy-start.11 = (s32[1,1,16]{2,1,0:T(1,128)S(1)}, s32[1,1,16]{2,1,0:T(1,128)}, u32[]{:S(2)}) copy-start(s32[1,1,16]{2,1,0:T(1,128)} %param.13) | copy-start | bytes 196
  2.2 36.6 %copy-start.1 = (bf16[2,1024,1024]{2,1,0:T(8,128)(2,1)S(1)}, bf16[2,1024,1024]{2,1,0:T(8,128)(2,1)}, u32[]{:S(2)}) copy-start(bf16[2,1024,1024]{2,1,0:T(8,128)(2,1)} %w_out.7) | copy-start | bytes 12582916
  2.6 36.2 %copy-start = (bf16[2,1024,1024]{2,1,0:T(8,128)(2,1)S(1)}, bf16[2,1024,1024]{2,1,0:T(8,128)(2,1)}, u32[]{:S(2)}) copy-start(bf16[2,1024,1024]{2,1,0:T(8,128)(2,1)} %w_in.7) | copy-start | bytes 12582916
  2.6 36.2 %copy-start.2 = (bf16[2,64,1024]{2,1,0:T(8,128)(2,1)S(1)}, bf16[2,64,1024]{2,1,0:T(8,128)(2,1)}, u32[]{:S(2)}) copy-start(bf16[2,64,1024]{2,1,0:T(8,128)(2,1)} %w_up.7) | copy-start | bytes 786436
  2.7 36.1 %copy-start.5 = (bf16[1,1,512,1024]{3,2,1,0:T(8,128)(2,1)S(1)}, bf16[1,1,512,1024]{3,2,1,0:T(8,128)(2,1)}, u32[]{:S(2)}) copy-start(bf16[1,1,512,1024]{3,2,1,0:T(8,128)(2,1)} %param.11) | copy-start | bytes 3145732
  2.7 36.1 %copy-start.7 = (bf16[2,1024,64]{1,2,0:T(8,128)(2,1)S(1)}, bf16[2,1024,64]{1,2,0:T(8,128)(2,1)}, u32[]{:S(2)}) copy-start(bf16[2,1024,64]{1,2,0:T(8,128)(2,1)} %param.17) | copy-start | bytes 786436
  2.7 36.1 %copy-start.8 = (f32[2,1024]{1,0:T(2,128)S(1)}, f32[2,1024]{1,0:T(2,128)}, u32[]{:S(2)}) copy-start(f32[2,1024]{1,0:T(2,128)} %gain.7) | copy-start | bytes 24580
  2.7 36.1 %copy-start.9 = (s32[1,1,512]{2,1,0:T(1,128)S(1)}, s32[1,1,512]{2,1,0:T(1,128)}, u32[]{:S(2)}) copy-start(s32[1,1,512]{2,1,0:T(1,128)} %param.16) | copy-start | bytes 6148
  2.7 3.4 %collective-permute-start.8 = (bf16[112,1024]{1,0:T(8,128)(2,1)S(1)}, bf16[112,1024]{1,0:T(8,128)(2,1)S(1)}, u32[]{:S(2)}, u32[]{:S(2)}) collective-permute-start(bf16[112,1024]{1,0:T(8,128)(2,1)S(1)} %get-tuple-element.51), channel_id=1, source_target_pairs={{0,2},{2,0},{4,6},{6,4},{8,10},{10,8},{12,14},{14,12},{16,18},{18,... | collective-permute-start | bytes 688136 | tf_op jit(solution)/shard_map/ppermute | solution.py:32
  2.8 6.8 %collective-permute-start.4 = (bf16[1,64,512]{2,1,0:T(8,128)(2,1)S(1)}, bf16[1,64,512]{2,1,0:T(8,128)(2,1)S(1)}, u32[]{:S(2)}, u32[]{:S(2)}) collective-permute-start(bf16[1,64,512]{2,1,0:T(8,128)(2,1)S(1)} %bitcast.18), channel_id=1, source_target_pairs={{0,16},{2,18},{4,20},{6,22},{8,24},{10,26},{12,28},{14,30},{16,0},... | collective-permute-start | bytes 196616 | tf_op jit(solution)/shard_map/ppermute | solution.py:32
  5.4 4.9 %collective-permute-start.2 = (bf16[64,1024]{1,0:T(8,128)(2,1)S(1)}, bf16[64,1024]{1,0:T(8,128)(2,1)S(1)}, u32[]{:S(2)}, u32[]{:S(2)}) collective-permute-start(bf16[64,1024]{1,0:T(8,128)(2,1)S(1)} %get-tuple-element.39), channel_id=1, source_target_pairs={{0,2},{2,0},{4,6},{6,4},{8,10},{10,8},{12,14},{14,12},{16,18},{18,... | collective-permute-start | bytes 393224 | tf_op jit(solution)/shard_map/ppermute | solution.py:32
  5.6 17.7 %collective-permute-start.1 = (bf16[16,128,128]{2,1,0:T(8,128)(2,1)S(1)}, bf16[16,128,128]{2,1,0:T(8,128)(2,1)S(1)}, u32[]{:S(2)}, u32[]{:S(2)}) collective-permute-start(bf16[16,128,128]{2,1,0:T(8,128)(2,1)S(1)} %bitcast.10), channel_id=1, source_target_pairs={{0,2},{2,0},{4,6},{6,4},{8,10},{10,8},{12,14},{14,12},{16,18},{18,... | collective-permute-start | bytes 1572872 | tf_op jit(solution)/shard_map/ppermute | solution.py:32
  5.9 9.7 %collective-permute-start.11 = (bf16[112,1024]{1,0:T(8,128)(2,1)S(1)}, bf16[112,1024]{1,0:T(8,128)(2,1)S(1)}, u32[]{:S(2)}, u32[]{:S(2)}) collective-permute-start(bf16[112,1024]{1,0:T(8,128)(2,1)S(1)} %get-tuple-element.53), channel_id=1, source_target_pairs={{0,2},{2,0},{4,6},{6,4},{8,10},{10,8},{12,14},{14,12},{16,18},{18,... | collective-permute-start | bytes 688136 | tf_op jit(solution)/shard_map/ppermute | solution.py:32
  6.2 11.0 %collective-permute-start.9 = (bf16[224,1024]{1,0:T(8,128)(2,1)S(1)}, bf16[224,1024]{1,0:T(8,128)(2,1)S(1)}, u32[]{:S(2)}, u32[]{:S(2)}) collective-permute-start(bf16[224,1024]{1,0:T(8,128)(2,1)S(1)} %pad_maximum_fusion.2), channel_id=1, source_target_pairs={{0,0},{1,1},{3,2},{4,4},{5,5},{7,6},{8,8},{9,9},{11,10},{12,12},{1... | collective-permute-start | bytes 1376264 | tf_op jit(solution)/shard_map/ppermute | solution.py:282
  9.6 7.5 %collective-permute-start.5 = (bf16[2,64,512]{2,1,0:T(8,128)(2,1)S(1)}, bf16[2,64,512]{2,1,0:T(8,128)(2,1)S(1)}, u32[]{:S(2)}, u32[]{:S(2)}) collective-permute-start(bf16[2,64,512]{2,1,0:T(8,128)(2,1)S(1)} %pad_maximum_fusion.7), channel_id=1, source_target_pairs={{0,8},{2,10},{4,12},{6,14},{8,0},{10,2},{12,4},{14,6},{16,24},{18,... | collective-permute-start | bytes 393224 | tf_op jit(solution)/shard_map/ppermute | solution.py:32
  10.4 12.9 %collective-permute-start.3 = (bf16[128,1024]{1,0:T(8,128)(2,1)S(1)}, bf16[128,1024]{1,0:T(8,128)(2,1)S(1)}, u32[]{:S(2)}, u32[]{:S(2)}) collective-permute-start(bf16[128,1024]{1,0:T(8,128)(2,1)S(1)} %pad_maximum_fusion.4), channel_id=1, source_target_pairs={{1,16},{5,20},{9,24},{13,28},{16,1},{20,5},{24,9},{28,13}} | collective-permute-start | bytes 786440 | tf_op jit(solution)/shard_map/ppermute | solution.py:305
  15.7 8.1 %collective-permute-start.12 = (bf16[224,1024]{1,0:T(8,128)(2,1)S(1)}, bf16[224,1024]{1,0:T(8,128)(2,1)S(1)}, u32[]{:S(2)}, u32[]{:S(2)}) collective-permute-start(bf16[224,1024]{1,0:T(8,128)(2,1)S(1)} %pad_maximum_fusion.3), channel_id=1, source_target_pairs={{0,0},{1,1},{3,2},{4,4},{5,5},{7,6},{8,8},{9,9},{11,10},{12,12},{1... | collective-permute-start | bytes 1376264 | tf_op jit(solution)/shard_map/ppermute | solution.py:282
  17.1 3.0 %collective-permute-start = (s32[33]{0:T(128)S(1)}, s32[33]{0:T(128)S(1)}, u32[]{:S(2)}, u32[]{:S(2)}) collective-permute-start(s32[33]{0:T(128)S(1)} %pad_add_fusion.own_index), channel_id=1, source_target_pairs={{0,2},{2,0},{4,6},{6,4},{8,10},{10,8},{12,14},{14,12},{16,18},{18,... | collective-permute-start | bytes 404 | tf_op jit(solution)/shard_map/ppermute | solution.py:32
  17.2 21.5 %collective-permute-start.10 = (bf16[224,1024]{1,0:T(8,128)(2,1)S(1)}, bf16[224,1024]{1,0:T(8,128)(2,1)S(1)}, u32[]{:S(2)}, u32[]{:S(2)}) collective-permute-start(bf16[224,1024]{1,0:T(8,128)(2,1)S(1)} %collective-permute-done.9), channel_id=1, source_target_pairs={{1,16},{2,18},{5,20},{6,22},{9,24},{10,26},{13,28},{14,30},{16,1},... | collective-permute-start | bytes 1376264 | tf_op jit(solution)/shard_map/ppermute | solution.py:295
  23.3 6.4 %collective-permute-start.6 = (bf16[4,64,512]{2,1,0:T(8,128)(2,1)S(1)}, bf16[4,64,512]{2,1,0:T(8,128)(2,1)S(1)}, u32[]{:S(2)}, u32[]{:S(2)}) collective-permute-start(bf16[4,64,512]{2,1,0:T(8,128)(2,1)S(1)} %pad_maximum_fusion.5), channel_id=1, source_target_pairs={{0,4},{2,6},{4,0},{6,2},{8,12},{10,14},{12,8},{14,10},{16,20},{18,... | collective-permute-start | bytes 786440 | tf_op jit(solution)/shard_map/ppermute | solution.py:32
  23.8 19.8 %collective-permute-start.13 = (bf16[224,1024]{1,0:T(8,128)(2,1)S(1)}, bf16[224,1024]{1,0:T(8,128)(2,1)S(1)}, u32[]{:S(2)}, u32[]{:S(2)}) collective-permute-start(bf16[224,1024]{1,0:T(8,128)(2,1)S(1)} %collective-permute-done.12), channel_id=1, source_target_pairs={{1,16},{2,18},{5,20},{6,22},{9,24},{10,26},{13,28},{14,30},{16,1},... | collective-permute-start | bytes 1376264 | tf_op jit(solution)/shard_map/ppermute | solution.py:295
  31.0 7.7 %collective-permute-start.7 = (bf16[64,512]{1,0:T(8,128)(2,1)S(1)}, bf16[64,512]{1,0:T(8,128)(2,1)S(1)}, u32[]{:S(2)}, u32[]{:S(2)}) collective-permute-start(bf16[64,512]{1,0:T(8,128)(2,1)S(1)} %get-tuple-element.47), channel_id=1, source_target_pairs={{0,2},{2,0},{4,6},{6,4},{8,10},{10,8},{12,14},{14,12},{16,18},{18,... | collective-permute-start | bytes 196616 | tf_op jit(solution)/shard_map/ppermute | solution.py:32
  38.7 4.9 %collective-permute-start.14 = (bf16[112,1024]{1,0:T(8,128)(2,1)S(1)}, bf16[112,1024]{1,0:T(8,128)(2,1)S(1)}, u32[]{:S(2)}, u32[]{:S(2)}) collective-permute-start(bf16[112,1024]{1,0:T(8,128)(2,1)S(1)} %slice.12), channel_id=1, source_target_pairs={{0,2},{2,0},{4,6},{6,4},{8,10},{10,8},{12,14},{14,12},{16,18},{18,... | collective-permute-start | bytes 688136 | tf_op jit(solution)/shard_map/ppermute | solution.py:32
  43.6 5.2 %collective-permute-start.15 = (bf16[64,512]{1,0:T(8,128)(2,1)S(1)}, bf16[64,512]{1,0:T(8,128)(2,1)S(1)}, u32[]{:S(2)}, u32[]{:S(2)}) collective-permute-start(bf16[64,512]{1,0:T(8,128)(2,1)S(1)} %get-tuple-element.56.v_t), channel_id=1, source_target_pairs={{0,16},{2,18},{4,20},{6,22},{8,24},{10,26},{12,28},{14,30},{16,0},... | collective-permute-start | bytes 196616 | tf_op jit(solution)/shard_map/ppermute | solution.py:32
  43.6 7.9 %collective-permute-start.16 = (bf16[64,512]{1,0:T(8,128)(2,1)S(1)}, bf16[64,512]{1,0:T(8,128)(2,1)S(1)}, u32[]{:S(2)}, u32[]{:S(2)}) collective-permute-start(bf16[64,512]{1,0:T(8,128)(2,1)S(1)} %get-tuple-element.57), channel_id=1, source_target_pairs={{1,16},{3,18},{5,20},{7,22},{9,24},{11,26},{13,28},{15,30},{16,1},... | collective-permute-start | bytes 196616 | tf_op jit(solution)/shard_map/ppermute | solution.py:48
  45.5 6.0 %collective-permute-start.17 = (bf16[64,512]{1,0:T(8,128)(2,1)S(1)}, bf16[64,512]{1,0:T(8,128)(2,1)S(1)}, u32[]{:S(2)}, u32[]{:S(2)}) collective-permute-start(bf16[64,512]{1,0:T(8,128)(2,1)S(1)} %get-tuple-element.57), channel_id=1, source_target_pairs={{1,0},{3,2},{5,4},{7,6},{9,8},{11,10},{13,12},{15,14},{16,17},{18,... | collective-permute-start | bytes 196616 | tf_op jit(solution)/shard_map/ppermute | solution.py:332
  51.6 5.5 %collective-permute-start.18 = (bf16[2,64,512]{2,1,0:T(8,128)(2,1)S(1)}, bf16[2,64,512]{2,1,0:T(8,128)(2,1)S(1)}, u32[]{:S(2)}, u32[]{:S(2)}) collective-permute-start(bf16[2,64,512]{2,1,0:T(8,128)(2,1)S(1)} %combine.1), channel_id=1, source_target_pairs={{0,8},{2,10},{4,12},{6,14},{8,0},{10,2},{12,4},{14,6},{16,24},{18,... | collective-permute-start | bytes 393224 | tf_op jit(solution)/shard_map/ppermute | solution.py:32
  51.7 9.3 %collective-permute-start.22 = (bf16[112,1024]{1,0:T(8,128)(2,1)S(1)}, bf16[112,1024]{1,0:T(8,128)(2,1)S(1)}, u32[]{:S(2)}, u32[]{:S(2)}) collective-permute-start(bf16[112,1024]{1,0:T(8,128)(2,1)S(1)} %slice.11), channel_id=1, source_target_pairs={{0,2},{2,0},{4,6},{6,4},{8,10},{10,8},{12,14},{14,12},{16,18},{18,... | collective-permute-start | bytes 688136 | tf_op jit(solution)/shard_map/ppermute | solution.py:32
  51.8 5.9 %collective-permute-start.21 = (bf16[64,1024]{1,0:T(8,128)(2,1)S(1)}, bf16[64,1024]{1,0:T(8,128)(2,1)S(1)}, u32[]{:S(2)}, u32[]{:S(2)}) collective-permute-start(bf16[64,1024]{1,0:T(8,128)(2,1)S(1)} %slice.10), channel_id=1, source_target_pairs={{0,2},{2,0},{4,6},{6,4},{8,10},{10,8},{12,14},{14,12},{16,18},{18,... | collective-permute-start | bytes 393224 | tf_op jit(solution)/shard_map/ppermute | solution.py:32
  52.3 8.6 %collective-permute-start.20 = (bf16[64,512]{1,0:T(8,128)(2,1)S(1)}, bf16[64,512]{1,0:T(8,128)(2,1)S(1)}, u32[]{:S(2)}, u32[]{:S(2)}) collective-permute-start(bf16[64,512]{1,0:T(8,128)(2,1)S(1)} %add_convert_fusion.1.agg_t), channel_id=1, source_target_pairs={{1,16},{3,18},{5,20},{7,22},{9,24},{11,26},{13,28},{15,30},{16,1},... | collective-permute-start | bytes 196616 | tf_op jit(solution)/shard_map/ppermute | solution.py:48
  57.1 8.4 %collective-permute-start.19 = (bf16[4,64,512]{2,1,0:T(8,128)(2,1)S(1)}, bf16[4,64,512]{2,1,0:T(8,128)(2,1)S(1)}, u32[]{:S(2)}, u32[]{:S(2)}) collective-permute-start(bf16[4,64,512]{2,1,0:T(8,128)(2,1)S(1)} %pad_maximum_fusion.6), channel_id=1, source_target_pairs={{0,4},{2,6},{4,0},{6,2},{8,12},{10,14},{12,8},{14,10},{16,20},{18,... | collective-permute-start | bytes 786440 | tf_op jit(solution)/shard_map/ppermute | solution.py:32
  67.0 1.3 %collective-permute-start.23 = (bf16[64,512]{1,0:T(8,128)(2,1)S(1)}, bf16[64,512]{1,0:T(8,128)(2,1)S(1)}, u32[]{:S(2)}, u32[]{:S(2)}) collective-permute-start(bf16[64,512]{1,0:T(8,128)(2,1)S(1)} %get-tuple-element.71), channel_id=1, source_target_pairs={{0,2},{2,0},{4,6},{6,4},{8,10},{10,8},{12,14},{14,12},{16,18},{18,... | collective-permute-start | bytes 196616 | tf_op jit(solution)/shard_map/ppermute | solution.py:32
  68.3 9.4 %collective-permute-start.24 = (bf16[64,512]{1,0:T(8,128)(2,1)S(1)}, bf16[64,512]{1,0:T(8,128)(2,1)S(1)}, u32[]{:S(2)}, u32[]{:S(2)}) collective-permute-start(bf16[64,512]{1,0:T(8,128)(2,1)S(1)} %add_convert_fusion.agg_t), channel_id=1, source_target_pairs={{1,16},{3,18},{5,20},{7,22},{9,24},{11,26},{13,28},{15,30},{16,1},... | collective-permute-start | bytes 196616 | tf_op jit(solution)/shard_map/ppermute | solution.py:48

commit v8 on v7

--- a/solution.py
+++ b/solution.py
@@ -366,7 +366,6 @@
 
     own_index = jnp.concatenate([block_target[0, 0], block_source[0, 0], block_count[0]])
     own_coeffs = triplet_coeff[0, 0]
-    index, coeffs = [own_index, hop(own_index, 1)], [own_coeffs, hop(own_coeffs, 1)]
     paired = lax.axis_size("tgt") == 2
     proj0, ahead, keep, swap = project(w_proj_t, state0)
     if paired:
@@ -375,7 +374,10 @@
         staged = [state0]
     pool = gather_down(proj0[None], 4)
     first = [send_ahead(ahead)] if paired else []
-    index, coeffs, first, pool = lax.optimization_barrier((index, coeffs, first, pool))
+    own_index, own_coeffs, first, pool = lax.optimization_barrier(
+        (own_index, own_coeffs, first, pool)
+    )
+    index, coeffs = [own_index, hop(own_index, 1)], [own_coeffs, hop(own_coeffs, 1)]
     first += [pass_on(x) for x in first]
     routed = [send_routes(x) if paired else to_mirror(x) for x in staged]
     agg0 = sum_over_cores(*triplet_partials(index, gather_down(pool, 2), coeffs))

time: 82.2 us -> 87.9 us (1.069)
  waiting for transfers between devices: 28.5 us -> 32.6 us
  starting transfers between devices: 30.7 us -> 32.5 us
    ppermute x1, waiting for transfers between devices: 3.15 us -> 5.97 us  [send_ahead(): lax.ppermute(jnp.concatenate([rows, hop(rows, 1)], axis=0), ('src', 'tgt'...]
    ppermute x2, starting transfers between devices: 5.41 us -> 7.63 us  [send_routes(): return lax.ppermute(staged, ('src', 'tgt'), pairs)]
    ppermute x2, waiting for transfers between devices: 8.39 us -> 10.4 us  [send_routes(): return lax.ppermute(staged, ('src', 'tgt'), pairs)]
    ppermute x16, waiting for transfers between devices: 9.29 us -> 7.68 us  [hop(): return lax.ppermute(values, 'src', [(i, i ^ bit) for i in range(size)])]
  transfers between devices with their start and end apart: 25 -> 25, of which waited for: 10 -> 10; matrix products, arithmetic and copies ran while one was open for 0% -> 0% of each run, Pallas kernels for 16% -> 15%
where the time goes in v8:
time: 87.9 us; the launch traced here: 87.6 us
  waiting for transfers between devices  32.6 us (37%)
  starting transfers between devices  32.5 us (37%)
  Pallas kernels  18.8 us (21%)
  local copies, waits for them, and re-layouts  2.27 us (3%)
  between operations  1.07 us (1%)
    pallas_call x8, Pallas kernels, call(): pl.pallas_call(body, in_specs=[smem] * len(scalars) + [vmem] * len(arrays...  18.8 us
    ppermute x3, starting transfers between devices, to_mirror(): return lax.ppermute(values, ('src', 'tgt'), mirror_pairs())  11.1 us
    ppermute x2, waiting for transfers between devices, send_routes(): return lax.ppermute(staged, ('src', 'tgt'), pairs)  10.4 us
    ppermute x3, waiting for transfers between devices, to_mirror(): return lax.ppermute(values, ('src', 'tgt'), mirror_pairs())  8.58 us
    ppermute x16, waiting for transfers between devices, hop(): return lax.ppermute(values, 'src', [(i, i ^ bit) for i in range(size)])  7.68 us
    ppermute x2, starting transfers between devices, send_routes(): return lax.ppermute(staged, ('src', 'tgt'), pairs)  7.63 us
    ppermute x1, waiting for transfers between devices, send_ahead(): lax.ppermute(jnp.concatenate([rows, hop(rows, 1)], axis=0), ('src', 'tgt'...  5.97 us
    ppermute x16, starting transfers between devices, hop(): return lax.ppermute(values, 'src', [(i, i ^ bit) for i in range(size)])  5.83 us
  transfers between devices with their start and end apart: 25, of which 10 were waited for; matrix products, arithmetic and copies ran while one was open for 0% of the time, Pallas kernels for 15%

profile of v8, /device:TPU:6, one launch (start us, length us, event | category | flops | bytes accessed | tf_op | source)
XLA Modules:
  0.0 87.6 jit_solution(10885116933920523082)
XLA Ops:
  0.0 1.2 %copy-done.4 = bf16[1,1,512,1024]{3,2,1,0:T(8,128)(2,1)S(1)} copy-done((bf16[1,1,512,1024]{3,2,1,0:T(8,128)(2,1)S(1)}, bf16[1,1,512,1024]{3,2,1,0:T(8,128)(2,1)}, u32[]{:S(2)}) %copy-start.4) | copy-done | bytes 1048600
  1.2 0.9 %copy-done.6 = bf16[2,1024,64]{1,2,0:T(8,128)(2,1)S(1)} copy-done((bf16[2,1024,64]{1,2,0:T(8,128)(2,1)S(1)}, bf16[2,1024,64]{1,2,0:T(8,128)(2,1)}, u32[]{:S(2)}) %copy-start.6) | copy-done | bytes 262168
  2.2 0.4 project.1
  2.6 0.0 copy-start.2
  2.7 0.0 copy-start.5
  2.7 0.0 copy-start.7
  2.7 0.0 copy-start.8
  2.7 0.0 copy-start.9
  2.7 2.7 %collective-permute-start.2 = (bf16[1,64,512]{2,1,0:T(8,128)(2,1)S(1)}, bf16[1,64,512]{2,1,0:T(8,128)(2,1)S(1)}, u32[]{:S(2)}, u32[]{:S(2)}) collective-permute-start(bf16[1,64,512]{2,1,0:T(8,128)(2,1)S(1)} %bitcast.18), channel_id=1, source_target_pairs={{0,16},{2,18},{4,20},{6,22},{8,24},{10,26},{12,28},{14,30},{16,0},... | collective-permute-start | bytes 196616 | tf_op jit(solution)/shard_map/ppermute | solution.py:32
  5.4 0.5 collective-permute-start.8
  6.5 2.7 %collective-permute-done.2 = bf16[1,64,512]{2,1,0:T(8,128)(2,1)S(1)} collective-permute-done((bf16[1,64,512]{2,1,0:T(8,128)(2,1)S(1)}, bf16[1,64,512]{2,1,0:T(8,128)(2,1)S(1)}, u32[]{:S(2)}, u32[]{:S(2)}) %collective-permute-start.2) | collective-permute-done | bytes 65568 | tf_op jit(solution)/shard_map/ppermute | solution.py:32
  9.2 0.4 collective-permute-start.3
  9.7 5.3 %collective-permute-start.1 = (bf16[128,1024]{1,0:T(8,128)(2,1)S(1)}, bf16[128,1024]{1,0:T(8,128)(2,1)S(1)}, u32[]{:S(2)}, u32[]{:S(2)}) collective-permute-start(bf16[128,1024]{1,0:T(8,128)(2,1)S(1)} %pad_maximum_fusion.4), channel_id=1, source_target_pairs={{1,16},{5,20},{9,24},{13,28},{16,1},{20,5},{24,9},{28,13}} | collective-permute-start | bytes 786440 | tf_op jit(solution)/shard_map/ppermute | solution.py:305
  15.0 0.7 collective-permute-start.9
  15.7 0.1 pad_add_fusion.own_index
  15.8 0.7 collective-permute-start.12
  16.6 6.0 %collective-permute-done.1.rest_0_ = bf16[128,1024]{1,0:T(8,128)(2,1)S(1)} collective-permute-done((bf16[128,1024]{1,0:T(8,128)(2,1)S(1)}, bf16[128,1024]{1,0:T(8,128)(2,1)S(1)}, u32[]{:S(2)}, u32[]{:S(2)}) %collective-permute-start.1) | collective-permute-done | bytes 262176 | tf_op jit(solution)/shard_map/ppermute | solution.py:305
  22.6 2.6 %collective-permute-start.10 = (bf16[224,1024]{1,0:T(8,128)(2,1)S(1)}, bf16[224,1024]{1,0:T(8,128)(2,1)S(1)}, u32[]{:S(2)}, u32[]{:S(2)}) collective-permute-start(bf16[224,1024]{1,0:T(8,128)(2,1)S(1)} %collective-permute-done.9), channel_id=1, source_target_pairs={{1,16},{2,18},{5,20},{6,22},{9,24},{10,26},{13,28},{14,30},{16,1},... | collective-permute-start | bytes 1376264 | tf_op jit(solution)/shard_map/ppermute | solution.py:295
  25.1 0.6 collective-permute-start.5
  25.7 5.1 %collective-permute-start.13 = (bf16[224,1024]{1,0:T(8,128)(2,1)S(1)}, bf16[224,1024]{1,0:T(8,128)(2,1)S(1)}, u32[]{:S(2)}, u32[]{:S(2)}) collective-permute-start(bf16[224,1024]{1,0:T(8,128)(2,1)S(1)} %collective-permute-done.12), channel_id=1, source_target_pairs={{1,16},{2,18},{5,20},{6,22},{9,24},{10,26},{13,28},{14,30},{16,1},... | collective-permute-start | bytes 1376264 | tf_op jit(solution)/shard_map/ppermute | solution.py:295
  30.8 0.1 collective-permute-start.4
  30.9 1.8 %collective-permute-done.5 = bf16[4,64,512]{2,1,0:T(8,128)(2,1)S(1)} collective-permute-done((bf16[4,64,512]{2,1,0:T(8,128)(2,1)S(1)}, bf16[4,64,512]{2,1,0:T(8,128)(2,1)S(1)}, u32[]{:S(2)}, u32[]{:S(2)}) %collective-permute-start.5) | collective-permute-done | bytes 262176 | tf_op jit(solution)/shard_map/ppermute | solution.py:32
  32.7 1.3 %triplets.2 = (f32[64,512]{1,0:T(8,128)S(1)}, bf16[64,512]{1,0:T(8,128)(2,1)S(1)}) custom-call(s32[33]{0:T(128)S(1)} %pad_add_fusion.own_index, s32[33]{0:T(128)S(1)} %collective-permute-done.4.other_index, bf16[8,64,512]{2,1,0:T(8,128)(2,1)S(1)} %pad_maximum_fusion.pool, bf16[16,128,128]{2,1,0:T(8,128)(2,1)S(1)} %bitcast.11, ...), custom_call_target="tpu_custom_call" | custom-call | tf_op jit(solution)/shard_map/triplets/pallas_call | solution.py:54
  34.0 0.1 collective-permute-start.7
  34.1 9.5 %collective-permute-done.10.rest_2_ = bf16[224,1024]{1,0:T(8,128)(2,1)S(1)} collective-permute-done((bf16[224,1024]{1,0:T(8,128)(2,1)S(1)}, bf16[224,1024]{1,0:T(8,128)(2,1)S(1)}, u32[]{:S(2)}, u32[]{:S(2)}) %collective-permute-start.10) | collective-permute-done | bytes 458784 | tf_op jit(solution)/shard_map/ppermute | solution.py:295
  43.6 0.1 collective-permute-start.14
  43.8 3.8 %first.1 = (f32[512,1024]{1,0:T(8,128)S(1)}, bf16[512,1024]{1,0:T(8,128)(2,1)S(1)}, bf16[64,512]{1,0:T(8,128)(2,1)S(1)}, bf16[64,512]{1,0:T(8,128)(2,1)S(1)}) custom-call(bf16[2,64,1024]{2,1,0:T(8,128)(2,1)S(1)} %copy-done.2, bf16[2,1024,1024]{2,1,0:T(8,128)(2,1)S(1)} %copy-done, bf16[2,1024,1024]{2,1,0:T(8,128)(2,1)S(1)} %copy-done.1, ...), custom_call_target="tpu_custom_call" | custom-call | tf_op jit(solution)/shard_map/first/pallas_call | solution.py:54
  47.6 0.9 collective-permute-done.13.rest_3_
  48.5 1.9 %collective-permute-start.16 = (bf16[64,512]{1,0:T(8,128)(2,1)S(1)}, bf16[64,512]{1,0:T(8,128)(2,1)S(1)}, u32[]{:S(2)}, u32[]{:S(2)}) collective-permute-start(bf16[64,512]{1,0:T(8,128)(2,1)S(1)} %get-tuple-element.53), channel_id=1, source_target_pairs={{1,16},{3,18},{5,20},{7,22},{9,24},{11,26},{13,28},{15,30},{16,1},... | collective-permute-start | bytes 196616 | tf_op jit(solution)/shard_map/ppermute | solution.py:48
  50.4 1.3 %collective-permute-start.17 = (bf16[64,512]{1,0:T(8,128)(2,1)S(1)}, bf16[64,512]{1,0:T(8,128)(2,1)S(1)}, u32[]{:S(2)}, u32[]{:S(2)}) collective-permute-start(bf16[64,512]{1,0:T(8,128)(2,1)S(1)} %get-tuple-element.53), channel_id=1, source_target_pairs={{1,0},{3,2},{5,4},{7,6},{9,8},{11,10},{13,12},{15,14},{16,17},{18,... | collective-permute-start | bytes 196616 | tf_op jit(solution)/shard_map/ppermute | solution.py:332
  51.7 1.9 %collective-permute-done.15.v_other = bf16[64,512]{1,0:T(8,128)(2,1)S(1)} collective-permute-done((bf16[64,512]{1,0:T(8,128)(2,1)S(1)}, bf16[64,512]{1,0:T(8,128)(2,1)S(1)}, u32[]{:S(2)}, u32[]{:S(2)}) %collective-permute-start.15) | collective-permute-done | bytes 65568 | tf_op jit(solution)/shard_map/ppermute | solution.py:32
  53.7 2.9 %collective-permute-done.16.u_mirror = bf16[64,512]{1,0:T(8,128)(2,1)S(1)} collective-permute-done((bf16[64,512]{1,0:T(8,128)(2,1)S(1)}, bf16[64,512]{1,0:T(8,128)(2,1)S(1)}, u32[]{:S(2)}, u32[]{:S(2)}) %collective-permute-start.16) | collective-permute-done | bytes 65568 | tf_op jit(solution)/shard_map/ppermute | solution.py:48
  56.6 0.1 combine.1
  56.6 0.2 collective-permute-start.18
  56.8 0.1 collective-permute-start.22
  56.9 0.6 collective-permute-start.21
  57.5 4.8 %collective-permute-start.20 = (bf16[64,512]{1,0:T(8,128)(2,1)S(1)}, bf16[64,512]{1,0:T(8,128)(2,1)S(1)}, u32[]{:S(2)}, u32[]{:S(2)}) collective-permute-start(bf16[64,512]{1,0:T(8,128)(2,1)S(1)} %add_convert_fusion.1.agg_t), channel_id=1, source_target_pairs={{1,16},{3,18},{5,20},{7,22},{9,24},{11,26},{13,28},{15,30},{16,1},... | collective-permute-start | bytes 196616 | tf_op jit(solution)/shard_map/ppermute | solution.py:48
  62.3 0.6 collective-permute-start.19
  62.9 4.0 %collective-permute-done.20.agg_other = bf16[64,512]{1,0:T(8,128)(2,1)S(1)} collective-permute-done((bf16[64,512]{1,0:T(8,128)(2,1)S(1)}, bf16[64,512]{1,0:T(8,128)(2,1)S(1)}, u32[]{:S(2)}, u32[]{:S(2)}) %collective-permute-start.20) | collective-permute-done | bytes 65568 | tf_op jit(solution)/shard_map/ppermute | solution.py:48
  66.8 4.6 %second.1 = (bf16[512,1024]{1,0:T(8,128)(2,1)S(1)}, bf16[512,1024]{1,0:T(8,128)(2,1)S(1)}) custom-call(bf16[2,64,1024]{2,1,0:T(8,128)(2,1)S(1)} %copy-done.2, bf16[2,1024,1024]{2,1,0:T(8,128)(2,1)S(1)} %copy-done, bf16[2,1024,1024]{2,1,0:T(8,128)(2,1)S(1)} %copy-done.1, f32[2,1024]{1,0:T(2,128)S(1)} %copy-done.8, ...), custom_call_target="tpu_custom_call" | custom-call | flops 5765000192 | tf_op jit(solution)/shard_map/second/pallas_call | solution.py:54
  71.4 0.1 pad_maximum_fusion.1.pool
  71.5 1.3 %triplets.3 = (f32[64,512]{1,0:T(8,128)S(1)}, bf16[64,512]{1,0:T(8,128)(2,1)S(1)}) custom-call(s32[33]{0:T(128)S(1)} %pad_add_fusion.own_index, s32[33]{0:T(128)S(1)} %collective-permute-done.4.other_index, bf16[8,64,512]{2,1,0:T(8,128)(2,1)S(1)} %pad_maximum_fusion.1.pool, bf16[16,128,128]{2,1,0:T(8,128)(2,1)S(1)} %bitcast.12, ...), custom_call_target="tpu_custom_call" | custom-call | tf_op jit(solution)/shard_map/triplets/pallas_call | solution.py:54
  72.8 0.1 collective-permute-start.23
  72.8 1.2 %collective-permute-done.23 = bf16[64,512]{1,0:T(8,128)(2,1)S(1)} collective-permute-done((bf16[64,512]{1,0:T(8,128)(2,1)S(1)}, bf16[64,512]{1,0:T(8,128)(2,1)S(1)}, u32[]{:S(2)}, u32[]{:S(2)}) %collective-permute-start.23) | collective-permute-done | bytes 65568 | tf_op jit(solution)/shard_map/ppermute | solution.py:32
  74.1 4.4 %collective-permute-start.24 = (bf16[64,512]{1,0:T(8,128)(2,1)S(1)}, bf16[64,512]{1,0:T(8,128)(2,1)S(1)}, u32[]{:S(2)}, u32[]{:S(2)}) collective-permute-start(bf16[64,512]{1,0:T(8,128)(2,1)S(1)} %add_convert_fusion.agg_t), channel_id=1, source_target_pairs={{1,16},{3,18},{5,20},{7,22},{9,24},{11,26},{13,28},{15,30},{16,1},... | collective-permute-start | bytes 196616 | tf_op jit(solution)/shard_map/ppermute | solution.py:48
  78.5 3.1 %third.1.total = f32[512,1024]{1,0:T(8,128)S(1)} custom-call(bf16[2,64,1024]{2,1,0:T(8,128)(2,1)S(1)} %copy-done.2, bf16[2,1024,1024]{2,1,0:T(8,128)(2,1)S(1)} %copy-done, bf16[2,1024,1024]{2,1,0:T(8,128)(2,1)S(1)} %copy-done.1, f32[2,1024]{1,0:T(2,128)S(1)} %copy-done.8, bf16[512,1024]{1,0:T(8,128)(2,1)S(1)} %get-tuple-element.68.state, ...), custom_call_target="tpu_custom_call" | custom-call | tf_op jit(solution)/shard_map/third/pallas_call | solution.py:54
  81.6 1.7 %collective-permute-done.24.agg_other = bf16[64,512]{1,0:T(8,128)(2,1)S(1)} collective-permute-done((bf16[64,512]{1,0:T(8,128)(2,1)S(1)}, bf16[64,512]{1,0:T(8,128)(2,1)S(1)}, u32[]{:S(2)}, u32[]{:S(2)}) %collective-permute-start.24) | collective-permute-done | bytes 65568 | tf_op jit(solution)/shard_map/ppermute | solution.py:48
  83.3 4.3 %last.1 = bf16[512,1024]{1,0:T(8,128)(2,1)} custom-call(bf16[2,64,1024]{2,1,0:T(8,128)(2,1)S(1)} %copy-done.2, bf16[2,1024,1024]{2,1,0:T(8,128)(2,1)S(1)} %copy-done, bf16[2,1024,1024]{2,1,0:T(8,128)(2,1)S(1)} %copy-done.1, f32[2,1024]{1,0:T(2,128)S(1)} %copy-done.8, bf16[512,1024]{1,0:T(8,128)(2,1)S(1)} %get-tuple-element.64.mirrored, ...), custom_call_target="tpu_custom_call" | custom-call | tf_op jit(solution)/shard_map/last/pallas_call | solution.py:54
  (48 shorter events, 0.4 us)
Async XLA Ops:
  0.0 1.2 %copy-start.4 = (bf16[1,1,512,1024]{3,2,1,0:T(8,128)(2,1)S(1)}, bf16[1,1,512,1024]{3,2,1,0:T(8,128)(2,1)}, u32[]{:S(2)}) copy-start(bf16[1,1,512,1024]{3,2,1,0:T(8,128)(2,1)} %param.11) | copy-start | bytes 3145732
  1.2 0.9 %copy-start.6 = (bf16[2,1024,64]{1,2,0:T(8,128)(2,1)S(1)}, bf16[2,1024,64]{1,2,0:T(8,128)(2,1)}, u32[]{:S(2)}) copy-start(bf16[2,1024,64]{1,2,0:T(8,128)(2,1)} %param.17) | copy-start | bytes 786436
  2.2 13.5 %copy-start.10 = (s32[1,1,16]{2,1,0:T(1,128)S(1)}, s32[1,1,16]{2,1,0:T(1,128)}, u32[]{:S(2)}) copy-start(s32[1,1,16]{2,1,0:T(1,128)} %param.14) | copy-start | bytes 196
  2.2 13.5 %copy-start.11 = (s32[1,1,16]{2,1,0:T(1,128)S(1)}, s32[1,1,16]{2,1,0:T(1,128)}, u32[]{:S(2)}) copy-start(s32[1,1,16]{2,1,0:T(1,128)} %param.13) | copy-start | bytes 196
  2.2 20.4 %copy-start.3 = (bf16[1,1,16,128,128]{4,3,2,1,0:T(8,128)(2,1)S(1)}, bf16[1,1,16,128,128]{4,3,2,1,0:T(8,128)(2,1)}, u32[]{:S(2)}) copy-start(bf16[1,1,16,128,128]{4,3,2,1,0:T(8,128)(2,1)} %param.12) | copy-start | bytes 1572868
  2.2 41.5 %copy-start.1 = (bf16[2,1024,1024]{2,1,0:T(8,128)(2,1)S(1)}, bf16[2,1024,1024]{2,1,0:T(8,128)(2,1)}, u32[]{:S(2)}) copy-start(bf16[2,1024,1024]{2,1,0:T(8,128)(2,1)} %w_out.7) | copy-start | bytes 12582916
  2.6 41.1 %copy-start = (bf16[2,1024,1024]{2,1,0:T(8,128)(2,1)S(1)}, bf16[2,1024,1024]{2,1,0:T(8,128)(2,1)}, u32[]{:S(2)}) copy-start(bf16[2,1024,1024]{2,1,0:T(8,128)(2,1)} %w_in.7) | copy-start | bytes 12582916
  2.6 41.1 %copy-start.2 = (bf16[2,64,1024]{2,1,0:T(8,128)(2,1)S(1)}, bf16[2,64,1024]{2,1,0:T(8,128)(2,1)}, u32[]{:S(2)}) copy-start(bf16[2,64,1024]{2,1,0:T(8,128)(2,1)} %w_up.7) | copy-start | bytes 786436
  2.7 41.1 %copy-start.5 = (bf16[1,1,512,1024]{3,2,1,0:T(8,128)(2,1)S(1)}, bf16[1,1,512,1024]{3,2,1,0:T(8,128)(2,1)}, u32[]{:S(2)}) copy-start(bf16[1,1,512,1024]{3,2,1,0:T(8,128)(2,1)} %param.11) | copy-start | bytes 3145732
  2.7 41.1 %copy-start.7 = (bf16[2,1024,64]{1,2,0:T(8,128)(2,1)S(1)}, bf16[2,1024,64]{1,2,0:T(8,128)(2,1)}, u32[]{:S(2)}) copy-start(bf16[2,1024,64]{1,2,0:T(8,128)(2,1)} %param.17) | copy-start | bytes 786436
  2.7 41.1 %copy-start.8 = (f32[2,1024]{1,0:T(2,128)S(1)}, f32[2,1024]{1,0:T(2,128)}, u32[]{:S(2)}) copy-start(f32[2,1024]{1,0:T(2,128)} %gain.7) | copy-start | bytes 24580
  2.7 41.1 %copy-start.9 = (s32[1,1,512]{2,1,0:T(1,128)S(1)}, s32[1,1,512]{2,1,0:T(1,128)}, u32[]{:S(2)}) copy-start(s32[1,1,512]{2,1,0:T(1,128)} %param.16) | copy-start | bytes 6148
  2.7 6.5 %collective-permute-start.2 = (bf16[1,64,512]{2,1,0:T(8,128)(2,1)S(1)}, bf16[1,64,512]{2,1,0:T(8,128)(2,1)S(1)}, u32[]{:S(2)}, u32[]{:S(2)}) collective-permute-start(bf16[1,64,512]{2,1,0:T(8,128)(2,1)S(1)} %bitcast.18), channel_id=1, source_target_pairs={{0,16},{2,18},{4,20},{6,22},{8,24},{10,26},{12,28},{14,30},{16,0},... | collective-permute-start | bytes 196616 | tf_op jit(solution)/shard_map/ppermute | solution.py:32
  5.4 4.3 %collective-permute-start = (bf16[64,1024]{1,0:T(8,128)(2,1)S(1)}, bf16[64,1024]{1,0:T(8,128)(2,1)S(1)}, u32[]{:S(2)}, u32[]{:S(2)}) collective-permute-start(bf16[64,1024]{1,0:T(8,128)(2,1)S(1)} %get-tuple-element.37), channel_id=1, source_target_pairs={{0,2},{2,0},{4,6},{6,4},{8,10},{10,8},{12,14},{14,12},{16,18},{18,... | collective-permute-start | bytes 393224 | tf_op jit(solution)/shard_map/ppermute | solution.py:32
  5.4 9.6 %collective-permute-start.8 = (bf16[112,1024]{1,0:T(8,128)(2,1)S(1)}, bf16[112,1024]{1,0:T(8,128)(2,1)S(1)}, u32[]{:S(2)}, u32[]{:S(2)}) collective-permute-start(bf16[112,1024]{1,0:T(8,128)(2,1)S(1)} %get-tuple-element.47), channel_id=1, source_target_pairs={{0,2},{2,0},{4,6},{6,4},{8,10},{10,8},{12,14},{14,12},{16,18},{18,... | collective-permute-start | bytes 688136 | tf_op jit(solution)/shard_map/ppermute | solution.py:32
  5.9 9.9 %collective-permute-start.11 = (bf16[112,1024]{1,0:T(8,128)(2,1)S(1)}, bf16[112,1024]{1,0:T(8,128)(2,1)S(1)}, u32[]{:S(2)}, u32[]{:S(2)}) collective-permute-start(bf16[112,1024]{1,0:T(8,128)(2,1)S(1)} %get-tuple-element.49), channel_id=1, source_target_pairs={{0,2},{2,0},{4,6},{6,4},{8,10},{10,8},{12,14},{14,12},{16,18},{18,... | collective-permute-start | bytes 688136 | tf_op jit(solution)/shard_map/ppermute | solution.py:32
  9.2 7.3 %collective-permute-start.3 = (bf16[2,64,512]{2,1,0:T(8,128)(2,1)S(1)}, bf16[2,64,512]{2,1,0:T(8,128)(2,1)S(1)}, u32[]{:S(2)}, u32[]{:S(2)}) collective-permute-start(bf16[2,64,512]{2,1,0:T(8,128)(2,1)S(1)} %pad_maximum_fusion.7), channel_id=1, source_target_pairs={{0,8},{2,10},{4,12},{6,14},{8,0},{10,2},{12,4},{14,6},{16,24},{18,... | collective-permute-start | bytes 393224 | tf_op jit(solution)/shard_map/ppermute | solution.py:32
  9.7 12.9 %collective-permute-start.1 = (bf16[128,1024]{1,0:T(8,128)(2,1)S(1)}, bf16[128,1024]{1,0:T(8,128)(2,1)S(1)}, u32[]{:S(2)}, u32[]{:S(2)}) collective-permute-start(bf16[128,1024]{1,0:T(8,128)(2,1)S(1)} %pad_maximum_fusion.4), channel_id=1, source_target_pairs={{1,16},{5,20},{9,24},{13,28},{16,1},{20,5},{24,9},{28,13}} | collective-permute-start | bytes 786440 | tf_op jit(solution)/shard_map/ppermute | solution.py:305
  15.0 7.6 %collective-permute-start.9 = (bf16[224,1024]{1,0:T(8,128)(2,1)S(1)}, bf16[224,1024]{1,0:T(8,128)(2,1)S(1)}, u32[]{:S(2)}, u32[]{:S(2)}) collective-permute-start(bf16[224,1024]{1,0:T(8,128)(2,1)S(1)} %pad_maximum_fusion.2), channel_id=1, source_target_pairs={{0,0},{1,1},{3,2},{4,4},{5,5},{7,6},{8,8},{9,9},{11,10},{12,12},{1... | collective-permute-start | bytes 1376264 | tf_op jit(solution)/shard_map/ppermute | solution.py:282
  15.8 9.9 %collective-permute-start.12 = (bf16[224,1024]{1,0:T(8,128)(2,1)S(1)}, bf16[224,1024]{1,0:T(8,128)(2,1)S(1)}, u32[]{:S(2)}, u32[]{:S(2)}) collective-permute-start(bf16[224,1024]{1,0:T(8,128)(2,1)S(1)} %pad_maximum_fusion.3), channel_id=1, source_target_pairs={{0,0},{1,1},{3,2},{4,4},{5,5},{7,6},{8,8},{9,9},{11,10},{12,12},{1... | collective-permute-start | bytes 1376264 | tf_op jit(solution)/shard_map/ppermute | solution.py:282
  22.6 10.1 %collective-permute-start.6 = (bf16[16,128,128]{2,1,0:T(8,128)(2,1)S(1)}, bf16[16,128,128]{2,1,0:T(8,128)(2,1)S(1)}, u32[]{:S(2)}, u32[]{:S(2)}) collective-permute-start(bf16[16,128,128]{2,1,0:T(8,128)(2,1)S(1)} %bitcast.10), channel_id=1, source_target_pairs={{0,2},{2,0},{4,6},{6,4},{8,10},{10,8},{12,14},{14,12},{16,18},{18,... | collective-permute-start | bytes 1572872 | tf_op jit(solution)/shard_map/ppermute | solution.py:32
  22.6 21.0 %collective-permute-start.10 = (bf16[224,1024]{1,0:T(8,128)(2,1)S(1)}, bf16[224,1024]{1,0:T(8,128)(2,1)S(1)}, u32[]{:S(2)}, u32[]{:S(2)}) collective-permute-start(bf16[224,1024]{1,0:T(8,128)(2,1)S(1)} %collective-permute-done.9), channel_id=1, source_target_pairs={{1,16},{2,18},{5,20},{6,22},{9,24},{10,26},{13,28},{14,30},{16,1},... | collective-permute-start | bytes 1376264 | tf_op jit(solution)/shard_map/ppermute | solution.py:295
  25.1 7.5 %collective-permute-start.5 = (bf16[4,64,512]{2,1,0:T(8,128)(2,1)S(1)}, bf16[4,64,512]{2,1,0:T(8,128)(2,1)S(1)}, u32[]{:S(2)}, u32[]{:S(2)}) collective-permute-start(bf16[4,64,512]{2,1,0:T(8,128)(2,1)S(1)} %pad_maximum_fusion.5), channel_id=1, source_target_pairs={{0,4},{2,6},{4,0},{6,2},{8,12},{10,14},{12,8},{14,10},{16,20},{18,... | collective-permute-start | bytes 786440 | tf_op jit(solution)/shard_map/ppermute | solution.py:32
  25.7 22.8 %collective-permute-start.13 = (bf16[224,1024]{1,0:T(8,128)(2,1)S(1)}, bf16[224,1024]{1,0:T(8,128)(2,1)S(1)}, u32[]{:S(2)}, u32[]{:S(2)}) collective-permute-start(bf16[224,1024]{1,0:T(8,128)(2,1)S(1)} %collective-permute-done.12), channel_id=1, source_target_pairs={{1,16},{2,18},{5,20},{6,22},{9,24},{10,26},{13,28},{14,30},{16,1},... | collective-permute-start | bytes 1376264 | tf_op jit(solution)/shard_map/ppermute | solution.py:295
  30.8 1.9 %collective-permute-start.4 = (s32[33]{0:T(128)S(1)}, s32[33]{0:T(128)S(1)}, u32[]{:S(2)}, u32[]{:S(2)}) collective-permute-start(s32[33]{0:T(128)S(1)} %pad_add_fusion.own_index), channel_id=1, source_target_pairs={{0,2},{2,0},{4,6},{6,4},{8,10},{10,8},{12,14},{14,12},{16,18},{18,... | collective-permute-start | bytes 404 | tf_op jit(solution)/shard_map/ppermute | solution.py:32
  34.0 9.7 %collective-permute-start.7 = (bf16[64,512]{1,0:T(8,128)(2,1)S(1)}, bf16[64,512]{1,0:T(8,128)(2,1)S(1)}, u32[]{:S(2)}, u32[]{:S(2)}) collective-permute-start(bf16[64,512]{1,0:T(8,128)(2,1)S(1)} %get-tuple-element.43), channel_id=1, source_target_pairs={{0,2},{2,0},{4,6},{6,4},{8,10},{10,8},{12,14},{14,12},{16,18},{18,... | collective-permute-start | bytes 196616 | tf_op jit(solution)/shard_map/ppermute | solution.py:32
  43.6 4.9 %collective-permute-start.14 = (bf16[112,1024]{1,0:T(8,128)(2,1)S(1)}, bf16[112,1024]{1,0:T(8,128)(2,1)S(1)}, u32[]{:S(2)}, u32[]{:S(2)}) collective-permute-start(bf16[112,1024]{1,0:T(8,128)(2,1)S(1)} %slice.12), channel_id=1, source_target_pairs={{0,2},{2,0},{4,6},{6,4},{8,10},{10,8},{12,14},{14,12},{16,18},{18,... | collective-permute-start | bytes 688136 | tf_op jit(solution)/shard_map/ppermute | solution.py:32
  48.5 5.2 %collective-permute-start.15 = (bf16[64,512]{1,0:T(8,128)(2,1)S(1)}, bf16[64,512]{1,0:T(8,128)(2,1)S(1)}, u32[]{:S(2)}, u32[]{:S(2)}) collective-permute-start(bf16[64,512]{1,0:T(8,128)(2,1)S(1)} %get-tuple-element.52.v_t), channel_id=1, source_target_pairs={{0,16},{2,18},{4,20},{6,22},{8,24},{10,26},{12,28},{14,30},{16,0},... | collective-permute-start | bytes 196616 | tf_op jit(solution)/shard_map/ppermute | solution.py:32
  48.5 8.1 %collective-permute-start.16 = (bf16[64,512]{1,0:T(8,128)(2,1)S(1)}, bf16[64,512]{1,0:T(8,128)(2,1)S(1)}, u32[]{:S(2)}, u32[]{:S(2)}) collective-permute-start(bf16[64,512]{1,0:T(8,128)(2,1)S(1)} %get-tuple-element.53), channel_id=1, source_target_pairs={{1,16},{3,18},{5,20},{7,22},{9,24},{11,26},{13,28},{15,30},{16,1},... | collective-permute-start | bytes 196616 | tf_op jit(solution)/shard_map/ppermute | solution.py:48
  50.4 6.2 %collective-permute-start.17 = (bf16[64,512]{1,0:T(8,128)(2,1)S(1)}, bf16[64,512]{1,0:T(8,128)(2,1)S(1)}, u32[]{:S(2)}, u32[]{:S(2)}) collective-permute-start(bf16[64,512]{1,0:T(8,128)(2,1)S(1)} %get-tuple-element.53), channel_id=1, source_target_pairs={{1,0},{3,2},{5,4},{7,6},{9,8},{11,10},{13,12},{15,14},{16,17},{18,... | collective-permute-start | bytes 196616 | tf_op jit(solution)/shard_map/ppermute | solution.py:332
  56.6 5.6 %collective-permute-start.18 = (bf16[2,64,512]{2,1,0:T(8,128)(2,1)S(1)}, bf16[2,64,512]{2,1,0:T(8,128)(2,1)S(1)}, u32[]{:S(2)}, u32[]{:S(2)}) collective-permute-start(bf16[2,64,512]{2,1,0:T(8,128)(2,1)S(1)} %combine.1), channel_id=1, source_target_pairs={{0,8},{2,10},{4,12},{6,14},{8,0},{10,2},{12,4},{14,6},{16,24},{18,... | collective-permute-start | bytes 393224 | tf_op jit(solution)/shard_map/ppermute | solution.py:32
  56.8 10.0 %collective-permute-start.22 = (bf16[112,1024]{1,0:T(8,128)(2,1)S(1)}, bf16[112,1024]{1,0:T(8,128)(2,1)S(1)}, u32[]{:S(2)}, u32[]{:S(2)}) collective-permute-start(bf16[112,1024]{1,0:T(8,128)(2,1)S(1)} %slice.11), channel_id=1, source_target_pairs={{0,2},{2,0},{4,6},{6,4},{8,10},{10,8},{12,14},{14,12},{16,18},{18,... | collective-permute-start | bytes 688136 | tf_op jit(solution)/shard_map/ppermute | solution.py:32
  56.9 5.9 %collective-permute-start.21 = (bf16[64,1024]{1,0:T(8,128)(2,1)S(1)}, bf16[64,1024]{1,0:T(8,128)(2,1)S(1)}, u32[]{:S(2)}, u32[]{:S(2)}) collective-permute-start(bf16[64,1024]{1,0:T(8,128)(2,1)S(1)} %slice.10), channel_id=1, source_target_pairs={{0,2},{2,0},{4,6},{6,4},{8,10},{10,8},{12,14},{14,12},{16,18},{18,... | collective-permute-start | bytes 393224 | tf_op jit(solution)/shard_map/ppermute | solution.py:32
  57.5 9.3 %collective-permute-start.20 = (bf16[64,512]{1,0:T(8,128)(2,1)S(1)}, bf16[64,512]{1,0:T(8,128)(2,1)S(1)}, u32[]{:S(2)}, u32[]{:S(2)}) collective-permute-start(bf16[64,512]{1,0:T(8,128)(2,1)S(1)} %add_convert_fusion.1.agg_t), channel_id=1, source_target_pairs={{1,16},{3,18},{5,20},{7,22},{9,24},{11,26},{13,28},{15,30},{16,1},... | collective-permute-start | bytes 196616 | tf_op jit(solution)/shard_map/ppermute | solution.py:48
  62.3 9.1 %collective-permute-start.19 = (bf16[4,64,512]{2,1,0:T(8,128)(2,1)S(1)}, bf16[4,64,512]{2,1,0:T(8,128)(2,1)S(1)}, u32[]{:S(2)}, u32[]{:S(2)}) collective-permute-start(bf16[4,64,512]{2,1,0:T(8,128)(2,1)S(1)} %pad_maximum_fusion.6), channel_id=1, source_target_pairs={{0,4},{2,6},{4,0},{6,2},{8,12},{10,14},{12,8},{14,10},{16,20},{18,... | collective-permute-start | bytes 786440 | tf_op jit(solution)/shard_map/ppermute | solution.py:32
  72.8 1.3 %collective-permute-start.23 = (bf16[64,512]{1,0:T(8,128)(2,1)S(1)}, bf16[64,512]{1,0:T(8,128)(2,1)S(1)}, u32[]{:S(2)}, u32[]{:S(2)}) collective-permute-start(bf16[64,512]{1,0:T(8,128)(2,1)S(1)} %get-tuple-element.67), channel_id=1, source_target_pairs={{0,2},{2,0},{4,6},{6,4},{8,10},{10,8},{12,14},{14,12},{16,18},{18,... | collective-permute-start | bytes 196616 | tf_op jit(solution)/shard_map/ppermute | solution.py:32
  74.1 9.2 %collective-permute-start.24 = (bf16[64,512]{1,0:T(8,128)(2,1)S(1)}, bf16[64,512]{1,0:T(8,128)(2,1)S(1)}, u32[]{:S(2)}, u32[]{:S(2)}) collective-permute-start(bf16[64,512]{1,0:T(8,128)(2,1)S(1)} %add_convert_fusion.agg_t), channel_id=1, source_target_pairs={{1,16},{3,18},{5,20},{7,22},{9,24},{11,26},{13,28},{15,30},{16,1},... | collective-permute-start | bytes 196616 | tf_op jit(solution)/shard_map/ppermute | solution.py:48
